TPU v7x, 512 devices: a whole 4x4x16 slice. The times are simulated.
512 devices in a mesh: step: 64 (over x, z), tp: 8 (over y, core).
Axes of the slice: x: 4, y: 4, z: 16, core: 2. Of those that a mesh axis runs over, the one named last changes fastest.
Arguments:
- latents: float32 [64, 256, 3072], P('step', None, 'tp'), may hold values from -6 to 6
- timesteps: int32 [65], replicated, may hold values from 0 to 3072, as said below
- start_offset: int32 [1], replicated, may hold values from 1 to 63
- slide_count: int32 [1], replicated, may hold values from 1 to 32
- mod_weight: bfloat16 [3, 256, 3072], P(None, None, 'tp'), may hold values from -2 to 2
- qkv_weight: bfloat16 [3, 3072, 2048], P(None, 'step', 'tp'), may hold values from -0.109375 to 0.109375
- out_weight: bfloat16 [2048, 3072], P('step', 'tp'), may hold values from -0.375 to 0.375
- q_gain: float32 [128], replicated
- k_gain: float32 [128], replicated
Outputs:
- updated: float32 [64, 256, 3072], P('step', None, 'tp')
Inputs may be any that keep to these rules, and one draw needn't show every extreme that they name: Strictly falling from slot to slot; timesteps[0] = 3072 and timesteps[64] = 0.
All inputs are finite; a program needn't handle non-finite values.
Results may differ from a plain program's by a relative error of at most 0.008.
The roundings to bfloat16 on the way count: a program that leaves them out, or rounds other values in their place, can miss the bound.
Values may be sent and summed in bfloat16 or wider, within the bound.
No kernel may reach another device: no remote copies, remote signals or barrier semaphores. Data moves between devices by JAX's collectives and lax.ppermute only.
A program may use at most 128 MiB of HBM per device.

v0:
```python
import math

import jax
import jax.numpy as jnp
from jax import lax
from jax.sharding import PartitionSpec as P

HD = 128


def prefix(value, axis, join, neutral):
    count, mine = (lax.axis_size(axis), lax.axis_index(axis))
    pieces = jax.tree.map(lambda part: lax.all_gather(part, axis), value)
    total = jax.tree.map(
        lambda part, zero: jnp.full_like(part, 0) + jnp.asarray(zero, part.dtype), value, neutral
    )

    def turn(position, total):
        longer = join(total, jax.tree.map(lambda part: part[position], pieces))
        return jax.tree.map(lambda new, old: jnp.where(position < mine, new, old), longer, total)

    return lax.fori_loop(0, count - 1, turn, total)


def embed_time(tval, width):
    half = width // 2
    freqs = jnp.exp(-math.log(10000.0) * jnp.arange(half, dtype=jnp.float32) / half)
    angles = 1000.0 * tval * freqs
    return jax.nn.silu(jnp.concatenate([jnp.cos(angles), jnp.sin(angles)])).astype(jnp.bfloat16)


def head_norm(values, gain):
    return values * lax.rsqrt(jnp.mean(values * values, axis=-1, keepdims=True) + 1e-06) * gain


def per_device(
    latents,
    timesteps,
    start_offset,
    slide_count,
    mod_weight,
    qkv_weight,
    out_weight,
    q_gain,
    k_gain,
):
    slot = lax.axis_index("step")
    count = lax.axis_size("step")
    grid = jnp.float32(48 * count)
    pair = lax.dynamic_slice_in_dim(timesteps, slot, 2, 0)
    tval = pair[0].astype(jnp.float32) / grid
    step_dt = (pair[0] - pair[1]).astype(jnp.float32) / grid
    emb = embed_time(tval, mod_weight.shape[1])
    mods = jnp.einsum("f,cfd->cd", emb.astype(jnp.float32), mod_weight.astype(jnp.float32)).astype(
        jnp.bfloat16
    )
    local = latents[0]
    tokens = local.shape[0]
    full_x, full_mod = (
        lax.all_gather(local.astype(jnp.bfloat16), "tp", axis=1, tiled=True),
        lax.all_gather(mods[:2], "tp", axis=1, tiled=True),
    )
    xf = full_x.astype(jnp.float32)
    mean = jnp.mean(xf, axis=-1, keepdims=True)
    cent = xf - mean
    var = jnp.mean(cent * cent, axis=-1, keepdims=True)
    normed = cent * lax.rsqrt(var + 1e-06)
    hidden = (
        normed * (1.0 + full_mod[1].astype(jnp.float32)) + full_mod[0].astype(jnp.float32)
    ).astype(jnp.bfloat16)
    inner_local = qkv_weight.shape[2]
    columns = hidden
    qkv = jnp.einsum(
        "tr,crj->ctj",
        columns,
        lax.all_gather(qkv_weight, "step", axis=1, tiled=True),
        preferred_element_type=jnp.float32,
    )
    heads_local = inner_local // HD
    query = qkv[0].reshape(tokens, heads_local, HD)
    keys = qkv[1].reshape(tokens, heads_local, HD)
    qn = head_norm(query, q_gain).astype(jnp.bfloat16)
    kn = head_norm(keys, k_gain).astype(jnp.bfloat16)
    vb = qkv[2].reshape(tokens, heads_local, HD).astype(jnp.bfloat16)
    scores = jnp.einsum("qhd,khd->hqk", qn, kn, preferred_element_type=jnp.float32) * HD ** (-0.5)
    scores = scores - jnp.max(scores, axis=-1, keepdims=True)
    weights = jnp.exp(scores)
    probs = (weights / jnp.sum(weights, axis=-1, keepdims=True)).astype(jnp.bfloat16)
    attn = jnp.einsum("hqk,khd->qhd", probs, vb, preferred_element_type=jnp.float32)
    attn = attn.reshape(tokens, inner_local).astype(jnp.bfloat16)
    all_heads = lax.all_gather(attn, "tp", axis=1, tiled=True)
    columns = all_heads
    proj = jnp.dot(
        columns,
        lax.all_gather(out_weight, "step", axis=0, tiled=True),
        preferred_element_type=jnp.float32,
    )
    start = start_offset[0]
    slide = slide_count[0]
    position = jnp.mod(slot - start + count, count)
    drift = step_dt * (mods[2].astype(jnp.float32) * proj)
    term = drift + jnp.where(position == 0, local, jnp.zeros_like(local))

    def combine(earlier, later):
        flag_early, sum_early = earlier
        flag_late, sum_late = later
        return (
            jnp.maximum(flag_early, flag_late),
            jnp.where(flag_late[0] > 0.0, sum_late, sum_early + sum_late),
        )

    flag = jnp.where(position == 0, 1.0, 0.0).astype(jnp.float32).reshape(1)
    identity = (jnp.zeros((1,), jnp.float32), jnp.zeros_like(term))
    seen_flag, partial_value = prefix((flag, term), "step", combine, identity)
    tail_term = jnp.where(slot >= start, term, jnp.zeros_like(term))
    total, tail = lax.psum((term, tail_term), "step")
    before = jnp.where(slot < start, partial_value + tail, partial_value)
    updated = jnp.where(position < slide, total, before)
    return updated[None]


def solution(mesh):
    return jax.shard_map(
        per_device,
        mesh=mesh,
        in_specs=(
            P("step", None, "tp"),
            P(),
            P(),
            P(),
            P(None, None, "tp"),
            P(None, "step", "tp"),
            P("step", "tp"),
            P(),
            P(),
        ),
        out_specs=P("step", None, "tp"),
        check_vma=False,
    )
```

profile of v0, /device:TPU:6, one launch (start us, length us, event | category | flops | bytes accessed | tf_op | source)
XLA Modules:
  0.0 889.5 jit_solution(8992154244323970573)
XLA Ops:
  12.2 12.0 %all_gather.25 = bf16[2,3072]{1,0:T(2,128)(2,1)S(1)} all-gather(bf16[2,384]{1,0:T(2,128)(2,1)S(1)} %slice.39), channel_id=1, replica_groups=mesh['step'=64,'tp'=8] {'tp'}, dimensions={1}, use_global_device_ids=true | all-gather | bytes 13824 | tf_op jit(solution)/shard_map/all_gather | solution.py:61
  24.2 22.0 %all-gather.14.cloned.1.call-done = bf16[1,256,3072]{2,1,0:T(8,128)(2,1)} async-done(((bf16[1,256,384]{2,1,0:T(8,128)(2,1)}), bf16[1,256,3072]{2,1,0:T(8,128)(2,1)}) %all-gather.14.cloned.1.call-update) | async-done | bytes 1572880 | tf_op jit(solution)/shard_map/all_gather | solution.py:60
  46.3 1.8 convert_reduce_fusion
  48.1 2.0 fusion.5
  50.1 144.9 %all-gather.8.cloned.1.call-done = bf16[3,3072,256]{2,1,0:T(8,128)(2,1)} async-done(((bf16[3,48,256]{2,1,0:T(8,128)(2,1)}), bf16[3,3072,256]{2,1,0:T(8,128)(2,1)}) %all-gather.8.cloned.1.call-update) | async-done | bytes 4718608 | tf_op jit(solution)/shard_map/all_gather | solution.py:76
  195.0 4.6 fusion.16
  203.6 130.5 %all-gather.12.cloned.1.call-done = bf16[2048,384]{1,0:T(8,128)(2,1)} async-done(((bf16[32,384]{1,0:T(8,128)(2,1)}), bf16[2048,384]{1,0:T(8,128)(2,1)}) %all-gather.12.cloned.1.call-update) | async-done | bytes 1572880 | tf_op jit(solution)/shard_map/all_gather | solution.py:95
  334.0 30.1 %all-gather.10.cloned.1.call-done = bf16[256,2048]{0,1:T(8,128)(2,1)} async-done(((bf16[256,256]{0,1:T(8,128)(2,1)}), bf16[256,2048]{0,1:T(8,128)(2,1)}) %all-gather.10.cloned.1.call-update) | async-done | bytes 1048592 | tf_op jit(solution)/shard_map/all_gather | solution.py:91
  364.2 3.3 broadcast_select_fusion
  370.4 124.1 %all-reduce = f32[64]{0:T(128)S(1)} all-reduce(f32[64]{0:T(128)S(1)} %dynamic-update-slice), channel_id=1, replica_groups=mesh['step'=64,'tp'=8] {'step'}, use_global_device_ids=true, to_apply=%add | all-reduce | flops 64 | bytes 512
  494.5 116.6 %all-gather.16.cloned.1.call-done = f32[16384,384]{1,0:T(8,128)} async-done(((f32[256,384]{1,0:T(8,128)}), f32[16384,384]{1,0:T(8,128)}) %all-gather.16.cloned.1.call-update) | async-done | bytes 25165840 | tf_op jit(solution)/shard_map/all_gather | solution.py:13
  611.7 150.5 %while.14 = (s32[]{:T(128)}, f32[256,384]{1,0:T(8,128)S(1)}, s32[]{:T(128)}, f32[64,1]{0,1:T(1,128)S(1)}, f32[64,256,384]{2,1,0:T(8,128)}, /*index=5*/s32[]{:T(128)}, s32[]{:T(128)}) while((s32[]{:T(128)}, f32[256,384]{1,0:T(8,128)S(1)}, s32[]{:T(128)}, f32[64,1]{0,1:T(1,128)S(1)}, f32[64,256,384]{2,1,0:T(8,128)}, ...), condition=%wide.region_8.9_spmd.clone, body=%wide.region_7.8_spmd.clone.sunk | while | flops 393221 | bytes 1179759 | solution.py:22
  633.8 1.8 fusion.51
  636.2 1.8 fusion.51
  638.5 1.8 fusion.51
  640.9 1.8 fusion.51
  643.3 1.8 fusion.51
  645.7 1.8 fusion.51
  648.1 1.8 fusion.51
  650.5 1.8 fusion.51
  655.3 1.8 fusion.51
  657.7 1.8 fusion.51
  660.1 1.8 fusion.51
  662.4 1.8 fusion.51
  664.8 1.8 fusion.51
  667.2 1.8 fusion.51
  672.0 1.8 fusion.51
  674.4 1.8 fusion.51
  681.6 1.8 fusion.51
  684.0 1.8 fusion.51
  686.3 1.8 fusion.51
  688.7 1.8 fusion.51
  691.1 1.8 fusion.51
  693.5 1.8 fusion.51
  695.9 1.8 fusion.51
  698.3 1.8 fusion.51
  700.7 1.8 fusion.51
  705.5 1.8 fusion.51
  707.8 1.8 fusion.51
  710.2 1.8 fusion.51
  731.7 1.8 fusion.51
  734.1 1.8 fusion.51
  738.9 1.8 fusion.51
  741.3 1.8 fusion.51
  748.5 1.8 fusion.51
  750.9 1.8 fusion.51
  762.2 118.5 %all-reduce.4.cloned.1.call-done = (f32[256,384]{1,0:T(8,128)}, f32[256,384]{1,0:T(8,128)}) async-done(((f32[256,384]{1,0:T(8,128)}, f32[256,384]{1,0:T(8,128)}), (f32[256,384]{1,0:T(8,128)}, f32[256,384]{1,0:T(8,128)})) %all-reduce.4.cloned.1.call-update) | async-done | bytes 786448 | tf_op jit(solution)/shard_map/psum | solution.py:116
  880.7 1.9 fusion.24
  (143 shorter events, 98.6 us)
Async XLA Ops:
  6.5 5.5 copy-start
  6.5 39.7 %all-gather.14.cloned.1.call-start = ((), (), s32[]{:S(2)}) async-start(), calls=%async_computation.3 | async-start | bytes 1769472 | tf_op jit(solution)/shard_map/all_gather | solution.py:60
  8.3 186.6 %all-gather.8.cloned.1.call-start = ((), (), s32[]{:S(2)}) async-start(), calls=%async_computation | async-start | bytes 4792320 | tf_op jit(solution)/shard_map/all_gather | solution.py:76
  9.1 325.0 %all-gather.12.cloned.1.call-start = ((), (), s32[]{:S(2)}) async-start(), calls=%async_computation.2 | async-start | bytes 1597440 | tf_op jit(solution)/shard_map/all_gather | solution.py:95
  9.8 354.4 %all-gather.10.cloned.1.call-start = ((), (), s32[]{:S(2)}) async-start(), calls=%async_computation.1 | async-start | bytes 1179648 | tf_op jit(solution)/shard_map/all_gather | solution.py:91
  46.3 148.7 %copy-start.1 = (bf16[1,256,3072]{2,1,0:T(8,128)(2,1)S(1)}, bf16[1,256,3072]{2,1,0:T(8,128)(2,1)}, u32[]{:S(2)}) copy-start(bf16[1,256,3072]{2,1,0:T(8,128)(2,1)} %all-gather.14.cloned.1.call-done) | copy-start | bytes 4718596
  195.0 5.1 copy-start.3
  195.0 5.1 copy-start.4
  199.6 164.6 %copy-start.2 = (f32[1,256,384]{2,1,0:T(8,128)S(1)}, f32[1,256,384]{2,1,0:T(8,128)}, u32[]{:S(2)}) copy-start(f32[1,256,384]{2,1,0:T(8,128)} %param.11) | copy-start | bytes 1179652
  201.5 409.6 %all-gather.16.cloned.1.call-start = ((), (), s32[]{:S(2)}) async-start(), calls=%async_computation.4 | async-start | bytes 25559040 | tf_op jit(solution)/shard_map/all_gather | solution.py:13
  611.1 269.6 %all-reduce.4.cloned.1.call-start = ((), (), s32[]{:S(2)}) async-start(), calls=%async_computation.5 | async-start | bytes 1572864 | tf_op jit(solution)/shard_map/psum | solution.py:116
Sparse Core Ops, SparseCore 0:
  9.5 36.7 all-gather.13
  49.2 145.6 all-gather.7
  197.9 136.0 all-gather.11
  336.1 28.0 all-gather.9
  367.7 243.3 all-gather.15
  615.0 265.6 all-reduce.3
where the time goes:
time: 894 us; the launch traced here: 889 us
  waiting for transfers between devices  565 us (63%)
  other arithmetic  157 us (18%)
  blocking collectives  136 us (15%)
  between operations  16.9 us (2%)
  matrix products  9.42 us (1%)
    all_gather x1, waiting for transfers between devices, per_device(): lax.all_gather(qkv_weight, 'step', axis=1, tiled=True)  145 us
    all_gather x1, waiting for transfers between devices, per_device(): lax.all_gather(out_weight, 'step', axis=0, tiled=True)  130 us
    unnamed x1, blocking collectives  124 us
    psum x1, waiting for transfers between devices, per_device(): total, tail = lax.psum((term, tail_term), 'step')  119 us
    all_gather x1, waiting for transfers between devices, prefix(): pieces = jax.tree.map(lambda part: lax.all_gather(part, axis), value)  117 us
    select_n x63, other arithmetic, turn(): jnp.where(position < mine, new, old)  112 us
    gt x63, other arithmetic, combine(): flag_late[0] > 0.0  37.4 us
    all_gather x1, waiting for transfers between devices, per_device(): all_heads = lax.all_gather(attn, 'tp', axis=1, tiled=True)  30.1 us
  transfers between devices with their start and end apart: 6, of which 6 were waited for; matrix products, arithmetic and copies ran while one was open for 18% of the time, Pallas kernels for 0%

commit v1 on v0

v1 whole, which is shorter than its diff:
```python
import math

import jax
import jax.numpy as jnp
from jax import lax
from jax.experimental import pallas as pl
from jax.experimental.pallas import tpu as pltpu
from jax.sharding import Mesh
from jax.sharding import PartitionSpec as P

HD = 128
NX, NZ, NY, NC = 4, 16, 4, 2
STEP = ("x", "z")
TP = ("y", "c")
VMEM_LIMIT = 40 * 1024 * 1024


def shift(value, axis, size, by):
    return lax.ppermute(value, axis, [(i, (i + by) % size) for i in range(size)])


def swap_pair(value):
    return lax.ppermute(value, "x", [(i, i ^ 1) for i in range(NX)])


def swap_core(value):
    return lax.ppermute(value, "c", [(i, i ^ 1) for i in range(NC)])


def to_all(value, axis, size):
    return lax.all_to_all(jnp.broadcast_to(value[None], (size,) + value.shape), axis, 0, 0)


def embed_time(tvals, width):
    half = width // 2
    freqs = jnp.exp(-math.log(10000.0) * jnp.arange(half, dtype=jnp.float32) / half)
    angles = 1000.0 * tvals[:, None] * freqs
    both = jnp.concatenate([jnp.cos(angles), jnp.sin(angles)], axis=1)
    return jax.nn.silu(both).astype(jnp.bfloat16)


def pack_kernel(idx_ref, emb_ref, mod_ref, lat_ref, out_ref, gate_ref, mods_ref):
    tokens = lat_ref.shape[0]
    out_ref[0:tokens, :] = lat_ref[...].astype(jnp.bfloat16)
    emb = emb_ref[...]
    for i in range(3):
        mods = jnp.dot(emb, mod_ref[i], preferred_element_type=jnp.float32)
        mods = mods.astype(jnp.bfloat16).astype(jnp.float32)
        if i < 2:
            mods_ref[i] = mods
        else:
            gate_ref[...] = mods
    slot = idx_ref[5]
    tail = out_ref.shape[0] - tokens
    which = lax.broadcasted_iota(jnp.int32, (tail, lat_ref.shape[1]), 0)
    block = jnp.where(which == 0, mods_ref[0, pl.ds(slot, 1), :], 0.0)
    block = jnp.where(which == 1, mods_ref[1, pl.ds(slot, 1), :], block)
    out_ref[tokens:, :] = block.astype(jnp.bfloat16)


def sort_kernel(qkv_ref, out_ref, to_ref, sems):
    loads = []
    for dest in range(NX):
        at = pl.ds(dest % 2 * HD, HD)
        pairs = [(out_ref, to_ref.at[dest, 48:80])]
        for i in range(3):
            pairs.append((qkv_ref.at[i, :, at], to_ref.at[dest, 0:48, i * HD : (i + 1) * HD]))
        for i, (source, target) in enumerate(pairs):
            loads.append(pltpu.make_async_copy(source, target, sems.at[dest, i]))
    for load in loads:
        load.start()
    for load in loads:
        load.wait()


def norm_kernel(idx_ref, *refs):
    xs, h_ref = refs[:8], refs[8]
    y, c = idx_ref[2], idx_ref[3]
    tokens, width = h_ref.shape[1], xs[0].shape[2]
    features = 8 * width
    for slot in range(2):
        total = jnp.zeros((tokens, 1), jnp.float32)
        for part in xs:
            total += jnp.sum(part[slot, 0:tokens, :].astype(jnp.float32), axis=-1, keepdims=True)
        mean = total / features
        total = jnp.zeros((tokens, 1), jnp.float32)
        for part in xs:
            cent = part[slot, 0:tokens, :].astype(jnp.float32) - mean
            total += jnp.sum(cent * cent, axis=-1, keepdims=True)
        inv = lax.rsqrt(total / features + 1e-06)
        for j in range(NY):
            for i in range(NC):
                part = xs[NC * j + i]
                place = lax.rem(y + NY - j, NY) * NC + lax.rem(c + i, NC)
                mods = part[slot, tokens : tokens + 16, :].astype(jnp.float32)
                cent = part[slot, 0:tokens, :].astype(jnp.float32) - mean
                hidden = cent * inv * (1.0 + mods[1:2]) + mods[0:1]
                at = pl.ds(pl.multiple_of(place * width, 128), width)
                h_ref[slot, :, at] = hidden.astype(jnp.bfloat16)


def attention_kernel(idx_ref, qg_ref, kg_ref, h_ref, all_ref, o_ref, w_ref):
    odd = lax.rem(idx_ref[0], 2)
    for x in range(NX):
        for z in range(NZ):
            row = (x * NZ + z) * 48
            w_ref[row : row + 48, :] = all_ref[z, x, 0:48, :]
    for slot in range(2):
        qkv = jnp.dot(h_ref[slot], w_ref[...], preferred_element_type=jnp.float32)
        q = qkv[:, 0:HD]
        k = qkv[:, HD : 2 * HD]
        v = qkv[:, 2 * HD : 3 * HD].astype(jnp.bfloat16)
        qn = q * lax.rsqrt(jnp.mean(q * q, axis=-1, keepdims=True) + 1e-06) * qg_ref[...]
        kn = k * lax.rsqrt(jnp.mean(k * k, axis=-1, keepdims=True) + 1e-06) * kg_ref[...]
        scores = lax.dot_general(
            qn.astype(jnp.bfloat16),
            kn.astype(jnp.bfloat16),
            (((1,), (1,)), ((), ())),
            preferred_element_type=jnp.float32,
        ) * HD ** (-0.5)
        weights = jnp.exp(scores - jnp.max(scores, axis=-1, keepdims=True))
        probs = (weights / jnp.sum(weights, axis=-1, keepdims=True)).astype(jnp.bfloat16)
        out = jnp.dot(probs, v, preferred_element_type=jnp.float32)
        o_ref[lax.rem(odd + slot, 2)] = out.astype(jnp.bfloat16)


def project_kernel(idx_ref, win_ref, dt_ref, gate_ref, lat_ref, mine_ref, other_ref, all_ref, *refs):
    out_ref, a_ref, w_ref, term_ref, run_ref = refs
    c = idx_ref[3]
    start, slide = win_ref[0], win_ref[1]
    for j in range(NY):
        for i, part in enumerate((mine_ref, other_ref)):
            for n in range(2):
                head = (j * NC + lax.rem(c + i, NC)) * 2 + n
                at = pl.ds(pl.multiple_of(head * HD, HD), HD)
                for m in range(2):
                    row = (2 * m + n) * 128
                    a_ref[m * 128 : (m + 1) * 128, at] = part[j, row : row + 128, :]
    for x in range(NX):
        for z in range(NZ):
            row = (x * NZ + z) * 32
            w_ref[row : row + 32, :] = all_ref[z, x, 48:80, :]
    proj = jnp.dot(a_ref[...], w_ref[...], preferred_element_type=jnp.float32)
    for slot in range(NX * NZ):
        row = slot // (2 * NZ) * 128 + slot % NZ * 8 + slot // NZ % 2 * 4
        gate = gate_ref[slot : slot + 1, :]
        term_ref[slot] = dt_ref[slot] * (gate * proj[row : row + 4, :])
    term_ref[start] = term_ref[start] + lat_ref[lax.rem(start, NZ)]
    count = NX * NZ

    def step(i, run):
        slot = lax.rem(start + i, count)
        run_ref[slot] = run
        return run + term_ref[slot]

    total = lax.fori_loop(0, count, step, jnp.zeros(run_ref.shape[1:], jnp.float32))

    def move(i, _):
        run_ref[lax.rem(start + i, count)] = total
        return 0

    lax.fori_loop(0, slide, move, 0)
    runs = run_ref[...]
    largest = jnp.max(jnp.max(jnp.abs(runs), axis=0), keepdims=True)
    power = jnp.clip(jnp.ceil(jnp.log2(largest)), -100.0, 100.0) - 14.0
    width = runs.shape[2]
    out_ref[:, :, 0:width] = runs * jnp.exp2(-power)[None]
    rest = out_ref.shape[2] - width
    out_ref[:, :, width:] = jnp.broadcast_to(power[None], runs.shape[:2] + (rest,))


def unscale_kernel(in_ref, out_ref):
    count, rows = in_ref.shape[0], in_ref.shape[1]
    width = out_ref.shape[1]
    scale = jnp.exp2(in_ref[:, :, width : width + 128])
    for g in range(width // 128):
        values = in_ref[:, :, g * 128 : (g + 1) * 128] * scale
        for i in range(count):
            out_ref[i * rows : (i + 1) * rows, g * 128 : (g + 1) * 128] = values[i]


def vmem():
    return pl.BlockSpec(memory_space=pltpu.VMEM)


def smem():
    return pl.BlockSpec(memory_space=pltpu.SMEM)


def params():
    return pltpu.CompilerParams(vmem_limit_bytes=VMEM_LIMIT)


def per_device(
    latents,
    timesteps,
    start_offset,
    slide_count,
    mod_weight,
    qkv_weight,
    out_weight,
    q_gain,
    k_gain,
):
    x, z, y, c = (lax.axis_index(a) for a in ("x", "z", "y", "c"))
    slot = x * NZ + z
    count = NX * NZ
    start, slide = start_offset[0], slide_count[0]
    grid = jnp.float32(48 * count)
    times = timesteps.astype(jnp.float32)
    tvals = times[:-1] / grid
    step_dts = (timesteps[:-1] - timesteps[1:]).astype(jnp.float32) / grid
    local = latents[0]
    tokens, width = local.shape

    sorted_rows = pl.pallas_call(
        sort_kernel,
        out_shape=jax.ShapeDtypeStruct((NX, 80, 3 * HD), jnp.bfloat16),
        in_specs=[pl.BlockSpec(memory_space=pl.ANY)] * 2,
        out_specs=vmem(),
        scratch_shapes=[pltpu.SemaphoreType.DMA((NX, 4))],
        compiler_params=pltpu.CompilerParams(vmem_limit_bytes=61 * 1024 * 1024),
        name="sort",
    )(qkv_weight, out_weight)
    weights = lax.all_gather(lax.all_to_all(sorted_rows, "x", 0, 0, tiled=True), "z")

    idx = jnp.stack([x, z, y, c, start, slot]).astype(jnp.int32)
    emb = embed_time(tvals, mod_weight.shape[1])
    packed, gates = pl.pallas_call(
        pack_kernel,
        out_shape=(
            jax.ShapeDtypeStruct((tokens + 16, width), jnp.bfloat16),
            jax.ShapeDtypeStruct((count, width), jnp.float32),
        ),
        in_specs=[smem()] + [vmem()] * 3,
        out_specs=(vmem(), vmem()),
        scratch_shapes=[pltpu.VMEM((2, count, width), jnp.float32)],
        compiler_params=params(),
        name="pack",
    )(idx, emb, mod_weight, local)
    both = jnp.stack([packed, swap_pair(packed)])
    xs = [both] + [shift(both, "y", NY, j) for j in range(1, NY)]
    xs = [b for mine in xs for b in (mine, swap_core(mine))]
    hidden = pl.pallas_call(
        norm_kernel,
        out_shape=jax.ShapeDtypeStruct((2, tokens, 8 * width), jnp.bfloat16),
        in_specs=[smem()] + [vmem()] * 8,
        out_specs=vmem(),
        compiler_params=params(),
        name="norm",
    )(idx, *xs)

    rows = tokens // count
    first = lax.all_to_all(local.reshape(NX, tokens // NX, width), "x", 0, 0, tiled=True)
    first = lax.dynamic_index_in_dim(first, start // NZ, 0, keepdims=False)
    first = lax.all_to_all(first.reshape(NZ, rows, width), "z", 0, 0, tiled=True)
    first, hidden = lax.optimization_barrier((first, hidden))
    attn = pl.pallas_call(
        attention_kernel,
        out_shape=jax.ShapeDtypeStruct((2, tokens, HD), jnp.bfloat16),
        in_specs=[smem()] + [vmem()] * 4,
        out_specs=vmem(),
        scratch_shapes=[pltpu.VMEM((48 * count, 3 * HD), jnp.bfloat16)],
        compiler_params=params(),
        name="attention",
    )(idx, q_gain[None], k_gain[None], hidden, weights)
    attn = attn.reshape(2, count, rows, HD).transpose(1, 0, 2, 3).reshape(count, 2 * rows, HD)
    attn = lax.all_to_all(attn, STEP, 0, 0, tiled=True).reshape(count * 2 * rows, HD)
    mine = to_all(attn, "y", NY)
    sums = pl.pallas_call(
        project_kernel,
        out_shape=jax.ShapeDtypeStruct((count, rows, width + 128), jnp.float32),
        in_specs=[smem()] * 3 + [vmem()] * 5,
        out_specs=vmem(),
        scratch_shapes=[
            pltpu.VMEM((tokens, 2048), jnp.bfloat16),
            pltpu.VMEM((2048, width), jnp.bfloat16),
            pltpu.VMEM((count, rows, width), jnp.float32),
            pltpu.VMEM((count, rows, width), jnp.float32),
        ],
        compiler_params=params(),
        name="project",
    )(idx, jnp.stack([start, slide]), step_dts, gates, first, mine, swap_core(mine), weights)
    back = lax.all_to_all(sums.astype(jnp.float16), STEP, 0, 0, tiled=True).astype(jnp.float32)
    return pl.pallas_call(
        unscale_kernel,
        out_shape=jax.ShapeDtypeStruct((tokens, width), jnp.float32),
        in_specs=[vmem()],
        out_specs=vmem(),
        compiler_params=params(),
        name="unscale",
    )(back)[None]


def solution(mesh):
    fine = Mesh(mesh.devices.reshape(NX, NZ, NY, NC), ("x", "z", "y", "c"))
    return jax.shard_map(
        per_device,
        mesh=fine,
        in_specs=(
            P(STEP, None, TP),
            P(),
            P(),
            P(),
            P(None, None, TP),
            P(None, STEP, TP),
            P(STEP, TP),
            P(),
            P(),
        ),
        out_specs=P(STEP, None, TP),
        check_vma=False,
    )
```

time: 894 us -> 189 us (0.21)
  waiting for transfers between devices: 565 us -> 22.7 us
  other arithmetic: 157 us -> 1.28 us
  blocking collectives: 136 us -> 78.4 us
  starting transfers between devices: 0.16 us -> 38.7 us
  local copies, waits for them, and re-layouts: 3.88 us -> 18.6 us
  Pallas kernels: 0 us -> 12.8 us
  matrix products: 9.42 us -> 0 us
    all_gather x5 -> x1, waiting for transfers between devices: 444 us -> 14.3 us  [per_device(): lax.all_gather(lax.all_to_all(sorted_rows, 'x', 0, 0, tiled=True), 'z')]
    unnamed x1 -> x0, blocking collectives: 124 us -> none
    psum x1 -> x0, waiting for transfers between devices: 119 us -> none  [per_device(): total, tail = lax.psum((term, tail_term), 'step')]
    select_n x63 -> x0, other arithmetic: 112 us -> none  [turn(): jnp.where(position < mine, new, old)]
    all_to_all x0 -> x4, blocking collectives: none -> 78.4 us  [the longest x1 27.6 us: per_device(): lax.all_to_all(sums.astype(jnp.float16), STEP, 0, 0, tiled=True)]
    gt x63 -> x0, other arithmetic: 37.4 us -> none  [combine(): flag_late[0] > 0.0]
    ppermute x0 -> x9, starting transfers between devices: none -> 21.2 us  [the longest x5 10 us: swap_core(): return lax.ppermute(value, 'c', [(i, i ^ 1) for i in range(NC)])]
    all_to_all x0 -> x2, starting transfers between devices: none -> 17.6 us  [the longest x1 11.4 us: per_device(): lax.all_to_all(first.reshape(NZ, rows, width), 'z', 0, 0, tiled=True)]
  transfers between devices with their start and end apart: 6 -> 12, of which waited for: 6 -> 4; matrix products, arithmetic and copies ran while one was open for 18% -> 1% of each run, Pallas kernels for 0% -> 2%
where the time goes in v1:
time: 189 us; the launch traced here: 188 us
  blocking collectives  78.4 us (41%)
  starting transfers between devices  38.7 us (20%)
  waiting for transfers between devices  22.7 us (12%)
  local copies, waits for them, and re-layouts  18.6 us (10%)
  between operations  15 us (8%)
  Pallas kernels  12.8 us (7%)
    all_to_all x1, blocking collectives, per_device(): lax.all_to_all(sums.astype(jnp.float16), STEP, 0, 0, tiled=True)  27.6 us
    all_to_all x1, blocking collectives, per_device(): lax.all_to_all(attn, STEP, 0, 0, tiled=True).reshape(count * 2 * rows, HD)  23.8 us
    unnamed x46, local copies, waits for them, and re-layouts  16.8 us
    all_to_all x1, blocking collectives, per_device(): lax.all_to_all(sorted_rows, 'x', 0, 0, tiled=True)  14.5 us
    all_gather x1, waiting for transfers between devices, per_device(): lax.all_gather(lax.all_to_all(sorted_rows, 'x', 0, 0, tiled=True), 'z')  14.3 us
    all_to_all x1, blocking collectives, to_all(): lax.all_to_all(jnp.broadcast_to(value[None], (size,) + value.shape), axis...  12.5 us
    all_to_all x1, starting transfers between devices, per_device(): lax.all_to_all(first.reshape(NZ, rows, width), 'z', 0, 0, tiled=True)  11.4 us
    ppermute x5, starting transfers between devices, swap_core(): return lax.ppermute(value, 'c', [(i, i ^ 1) for i in range(NC)])  10 us
  transfers between devices with their start and end apart: 12, of which 4 were waited for; matrix products, arithmetic and copies ran while one was open for 1% of the time, Pallas kernels for 2%

profile of v1, /device:TPU:6, one launch (start us, length us, event | category | flops | bytes accessed | tf_op | source)
XLA Modules:
  0.0 187.6 jit_solution(14769605021951478168)
XLA Ops:
  6.5 1.8 sort.1
  8.3 14.5 %all_to_all.30 = bf16[4,80,384]{2,1,0:T(8,128)(2,1)} all-to-all(bf16[4,80,384]{2,1,0:T(8,128)(2,1)} %sort.1), channel_id=1, replica_groups=mesh['x'=4,'z'=16,'y'=4,'c'=2] {'x'}, dimensions={0} | all-to-all | bytes 491520 | tf_op jit(solution)/shard_map/all_to_all | solution.py:225
  23.5 0.7 convert_element_type.16
  24.3 0.2 multiply_cosine_fusion
  24.5 1.0 copy-done.4
  25.5 1.1 copy-done.5
  26.6 0.8 pack.1
  27.4 2.2 %collective-permute-start = (bf16[272,384]{1,0:T(8,128)(2,1)S(1)}, bf16[272,384]{1,0:T(8,128)(2,1)S(1)}, u32[]{:S(2)}, u32[]{:S(2)}) collective-permute-start(bf16[272,384]{1,0:T(8,128)(2,1)S(1)} %get-tuple-element.10), channel_id=1, source_target_pairs={{0,128},{128,0},{256,384},{384,256},{1,129},{129,1},{257,385},{385... | collective-permute-start | bytes 626696 | tf_op jit(solution)/shard_map/ppermute | solution.py:23
  29.5 5.5 %collective-permute-done = bf16[272,384]{1,0:T(8,128)(2,1)S(1)} collective-permute-done((bf16[272,384]{1,0:T(8,128)(2,1)S(1)}, bf16[272,384]{1,0:T(8,128)(2,1)S(1)}, u32[]{:S(2)}, u32[]{:S(2)}) %collective-permute-start) | collective-permute-done | bytes 208928 | tf_op jit(solution)/shard_map/ppermute | solution.py:23
  35.1 1.9 %collective-permute-start.2 = (bf16[2,272,384]{2,1,0:T(8,128)(2,1)S(1)}, bf16[2,272,384]{2,1,0:T(8,128)(2,1)S(1)}, u32[]{:S(2)}, u32[]{:S(2)}) collective-permute-start(bf16[2,272,384]{2,1,0:T(8,128)(2,1)S(1)} %pad_maximum_fusion.refs_0_), channel_id=1, source_target_pairs={{0,2},{2,4},{4,6},{6,0},{1,3},{3,5},{5,7},{7,1},{8,10},{10,12},{12... | collective-permute-start | bytes 1253384 | tf_op jit(solution)/shard_map/ppermute | solution.py:19
  37.1 1.9 %collective-permute-start.4 = (bf16[2,272,384]{2,1,0:T(8,128)(2,1)S(1)}, bf16[2,272,384]{2,1,0:T(8,128)(2,1)S(1)}, u32[]{:S(2)}, u32[]{:S(2)}) collective-permute-start(bf16[2,272,384]{2,1,0:T(8,128)(2,1)S(1)} %pad_maximum_fusion.refs_0_), channel_id=1, source_target_pairs={{0,4},{2,6},{4,0},{6,2},{1,5},{3,7},{5,1},{7,3},{8,12},{10,14},{12... | collective-permute-start | bytes 1253384 | tf_op jit(solution)/shard_map/ppermute | solution.py:19
  39.0 5.1 %collective-permute-start.6 = (bf16[2,272,384]{2,1,0:T(8,128)(2,1)S(1)}, bf16[2,272,384]{2,1,0:T(8,128)(2,1)S(1)}, u32[]{:S(2)}, u32[]{:S(2)}) collective-permute-start(bf16[2,272,384]{2,1,0:T(8,128)(2,1)S(1)} %pad_maximum_fusion.refs_0_), channel_id=1, source_target_pairs={{0,6},{2,0},{4,2},{6,4},{1,7},{3,1},{5,3},{7,5},{8,14},{10,8},{12,... | collective-permute-start | bytes 1253384 | tf_op jit(solution)/shard_map/ppermute | solution.py:19
  44.1 6.2 %all-to-all-start = ((f32[4,64,384]{2,1,0:T(8,128)}), f32[4,64,384]{2,1,0:T(8,128)}, u32[]{:S(2)}, u32[]{:S(2)}) async-start(f32[4,64,384]{2,1,0:T(8,128)} %bitcast.25), calls=%async_computation | async-start | bytes 786432 | tf_op jit(solution)/shard_map/all_to_all | solution.py:254
  50.3 1.9 %collective-permute-start.1 = (bf16[2,272,384]{2,1,0:T(8,128)(2,1)S(1)}, bf16[2,272,384]{2,1,0:T(8,128)(2,1)S(1)}, u32[]{:S(2)}, u32[]{:S(2)}) collective-permute-start(bf16[2,272,384]{2,1,0:T(8,128)(2,1)S(1)} %pad_maximum_fusion.refs_0_), channel_id=1, source_target_pairs={{0,1},{1,0},{2,3},{3,2},{4,5},{5,4},{6,7},{7,6},{8,9},{9,8},{10,11... | collective-permute-start | bytes 1253384 | tf_op jit(solution)/shard_map/ppermute | solution.py:27
  52.2 1.8 collective-permute-done.2.refs_2_
  54.0 1.9 %collective-permute-start.3 = (bf16[2,272,384]{2,1,0:T(8,128)(2,1)S(1)}, bf16[2,272,384]{2,1,0:T(8,128)(2,1)S(1)}, u32[]{:S(2)}, u32[]{:S(2)}) collective-permute-start(bf16[2,272,384]{2,1,0:T(8,128)(2,1)S(1)} %collective-permute-done.2.refs_2_), channel_id=1, source_target_pairs={{0,1},{1,0},{2,3},{3,2},{4,5},{5,4},{6,7},{7,6},{8,9},{9,8},{10,11... | collective-permute-start | bytes 1253384 | tf_op jit(solution)/shard_map/ppermute | solution.py:27
  56.0 2.4 %collective-permute-start.5 = (bf16[2,272,384]{2,1,0:T(8,128)(2,1)S(1)}, bf16[2,272,384]{2,1,0:T(8,128)(2,1)S(1)}, u32[]{:S(2)}, u32[]{:S(2)}) collective-permute-start(bf16[2,272,384]{2,1,0:T(8,128)(2,1)S(1)} %collective-permute-done.4.refs_4_), channel_id=1, source_target_pairs={{0,1},{1,0},{2,3},{3,2},{4,5},{5,4},{6,7},{7,6},{8,9},{9,8},{10,11... | collective-permute-start | bytes 1253384 | tf_op jit(solution)/shard_map/ppermute | solution.py:27
  58.4 0.8 copy-done.8
  59.2 1.9 %collective-permute-start.7 = (bf16[2,272,384]{2,1,0:T(8,128)(2,1)S(1)}, bf16[2,272,384]{2,1,0:T(8,128)(2,1)S(1)}, u32[]{:S(2)}, u32[]{:S(2)}) collective-permute-start(bf16[2,272,384]{2,1,0:T(8,128)(2,1)S(1)} %collective-permute-done.6.refs_6_), channel_id=1, source_target_pairs={{0,1},{1,0},{2,3},{3,2},{4,5},{5,4},{6,7},{7,6},{8,9},{9,8},{10,11... | collective-permute-start | bytes 1253384 | tf_op jit(solution)/shard_map/ppermute | solution.py:27
  61.1 0.8 copy-done.10
  61.8 0.9 constant_dynamic-slice_fusion
  62.7 0.7 reshape.18
  63.4 11.4 %all-to-all-start.1 = ((f32[16,4,384]{2,1,0:T(4,128)}), f32[16,4,384]{2,1,0:T(4,128)S(1)}, u32[]{:S(2)}, u32[]{:S(2)}) async-start(f32[16,4,384]{2,1,0:T(4,128)} %reshape.18), calls=%async_computation.1 | async-start | bytes 196608 | tf_op jit(solution)/shard_map/all_to_all | solution.py:256
  74.8 0.8 copy-done.12
  75.6 0.8 copy-done.14
  76.4 0.8 copy-done.16
  77.1 0.8 copy-done.18
  77.9 1.0 copy-done.3
  78.9 1.0 copy-done.7
  79.9 1.0 copy-done.9
  80.9 1.0 copy-done.11
  81.9 1.0 copy-done.13
  82.9 1.0 copy-done.15
  83.9 1.0 copy-done.17
  84.9 1.0 copy-done.19
  86.0 3.9 %norm.1.h_ref = bf16[2,256,3072]{2,1,0:T(8,128)(2,1)S(1)} custom-call(s32[6]{0:T(128)S(1)} %stack.35.idx_ref, bf16[2,272,384]{2,1,0:T(8,128)(2,1)S(1)} %copy-done.3, bf16[2,272,384]{2,1,0:T(8,128)(2,1)S(1)} %copy-done.13, bf16[2,272,384]{2,1,0:T(8,128)(2,1)S(1)} %copy-done.7, bf16[2,272,384]{2,1,0:T(8,128)(2,1)S(1)} %copy-done.15, ...), custom_call_target="tpu_custom_call" | custom-call | tf_op jit(solution)/shard_map/norm/pallas_call | solution.py:244
  89.8 14.3 %all-gather.3.cloned.1.call-done = bf16[64,80,384]{2,1,0:T(8,128)(2,1)} async-done(((bf16[4,80,384]{2,1,0:T(8,128)(2,1)}), bf16[64,80,384]{2,1,0:T(8,128)(2,1)}) %all-gather.3.cloned.1.call-update) | async-done | bytes 3932176 | tf_op jit(solution)/shard_map/all_gather | solution.py:225
  104.1 2.1 %copy-done = bf16[64,80,384]{2,1,0:T(8,128)(2,1)S(1)} copy-done((bf16[64,80,384]{2,1,0:T(8,128)(2,1)S(1)}, bf16[64,80,384]{2,1,0:T(8,128)(2,1)}, u32[]{:S(2)}) %copy-start) | copy-done | bytes 3932184
  106.2 3.2 %attention.1 = bf16[2,256,128]{2,1,0:T(8,128)(2,1)S(1)} custom-call(s32[6]{0:T(128)S(1)} %stack.35.idx_ref, f32[1,128]{1,0:T(1,128)S(1)} %bitcast.29, f32[1,128]{1,0:T(1,128)S(1)} %bitcast.30, bf16[2,256,3072]{2,1,0:T(8,128)(2,1)S(1)} %norm.1.h_ref, bf16[16,4,80,384]{3,2,1,0:T(8,128)(2,1)S(1)} %bitcast.23), custom_call_target="tpu_custom_call" | custom-call | tf_op jit(solution)/shard_map/attention/pallas_call | solution.py:258
  109.6 23.8 %all_to_all.31 = bf16[64,8,128]{2,1,0:T(8,128)(2,1)S(1)} all-to-all(bf16[64,8,128]{2,1,0:T(8,128)(2,1)S(1)} %copy.14), channel_id=1, replica_groups=mesh['x'=4,'z'=16,'y'=4,'c'=2] {'x','z'}, dimensions={0} | all-to-all | bytes 262144 | tf_op jit(solution)/shard_map/all_to_all | solution.py:268
  133.5 12.5 %all_to_all.32.mine_ref = bf16[4,512,128]{2,1,0:T(8,128)(2,1)S(1)} all-to-all(bf16[4,512,128]{2,1,0:T(8,128)(2,1)S(1)} %broadcast_in_dim.21), channel_id=1, replica_groups=mesh['x'=4,'z'=16,'y'=4,'c'=2] {'y'}, dimensions={0} | all-to-all | bytes 1048576 | tf_op jit(solution)/shard_map/all_to_all | solution.py:31
  146.0 1.9 %collective-permute-start.8 = (bf16[4,512,128]{2,1,0:T(8,128)(2,1)S(1)}, bf16[4,512,128]{2,1,0:T(8,128)(2,1)S(1)}, u32[]{:S(2)}, u32[]{:S(2)}) collective-permute-start(bf16[4,512,128]{2,1,0:T(8,128)(2,1)S(1)} %all_to_all.32.mine_ref), channel_id=1, source_target_pairs={{0,1},{1,0},{2,3},{3,2},{4,5},{5,4},{6,7},{7,6},{8,9},{9,8},{10,11... | collective-permute-start | bytes 1572872 | tf_op jit(solution)/shard_map/ppermute | solution.py:27
  148.7 1.1 collective-permute-done.8.other_ref
  149.8 2.3 %project.1 = f32[64,4,512]{2,1,0:T(4,128)S(1)} custom-call(s32[6]{0:T(128)S(1)} %stack.35.idx_ref, s32[2]{0:T(128)S(1)} %pad_add_fusion.win_ref, f32[64]{0:T(128)S(1)} %convert_multiply_fusion.dt_ref, f32[64,384]{1,0:T(8,128)S(1)} %get-tuple-element.9.gate_ref, f32[16,4,384]{2,1,0:T(4,128)S(1)} %all-to-all-done.1.lat_ref, ...), custom_call_target="tpu_custom_call" | custom-call | tf_op jit(solution)/shard_map/project/pallas_call | solution.py:270
  152.1 0.1 convert_element_type.18
  152.2 27.6 %all_to_all.33 = f16[64,4,512]{2,1,0:T(4,128)(2,1)S(1)} all-to-all(f16[64,4,512]{2,1,0:T(4,128)(2,1)S(1)} %convert_element_type.18), channel_id=1, replica_groups=mesh['x'=4,'z'=16,'y'=4,'c'=2] {'x','z'}, dimensions={0} | all-to-all | bytes 524288 | tf_op jit(solution)/shard_map/all_to_all | solution.py:284
  179.8 0.1 convert_element_type.19.in_ref
  179.9 0.8 unscale.1
  (49 shorter events, 0.6 us)
Async XLA Ops:
  6.5 97.6 %all-gather.3.cloned.1.call-start = ((), (), s32[]{:S(2)}) async-start(), calls=%async_computation.6 | async-start | bytes 4177920 | tf_op jit(solution)/shard_map/all_gather | solution.py:225
  24.5 1.0 copy-start.4
  25.5 1.1 copy-start.5
  27.4 7.7 %collective-permute-start = (bf16[272,384]{1,0:T(8,128)(2,1)S(1)}, bf16[272,384]{1,0:T(8,128)(2,1)S(1)}, u32[]{:S(2)}, u32[]{:S(2)}) collective-permute-start(bf16[272,384]{1,0:T(8,128)(2,1)S(1)} %get-tuple-element.10), channel_id=1, source_target_pairs={{0,128},{128,0},{256,384},{384,256},{1,129},{129,1},{257,385},{385... | collective-permute-start | bytes 626696 | tf_op jit(solution)/shard_map/ppermute | solution.py:23
  35.1 41.3 %copy-start.2 = (bf16[2,272,384]{2,1,0:T(8,128)(2,1)}, bf16[2,272,384]{2,1,0:T(8,128)(2,1)S(1)}, u32[]{:S(2)}) copy-start(bf16[2,272,384]{2,1,0:T(8,128)(2,1)S(1)} %pad_maximum_fusion.refs_0_) | copy-start | bytes 1253380
  35.1 18.9 %collective-permute-start.2 = (bf16[2,272,384]{2,1,0:T(8,128)(2,1)S(1)}, bf16[2,272,384]{2,1,0:T(8,128)(2,1)S(1)}, u32[]{:S(2)}, u32[]{:S(2)}) collective-permute-start(bf16[2,272,384]{2,1,0:T(8,128)(2,1)S(1)} %pad_maximum_fusion.refs_0_), channel_id=1, source_target_pairs={{0,2},{2,4},{4,6},{6,0},{1,3},{3,5},{5,7},{7,1},{8,10},{10,12},{12... | collective-permute-start | bytes 1253384 | tf_op jit(solution)/shard_map/ppermute | solution.py:19
  37.1 18.9 %collective-permute-start.4 = (bf16[2,272,384]{2,1,0:T(8,128)(2,1)S(1)}, bf16[2,272,384]{2,1,0:T(8,128)(2,1)S(1)}, u32[]{:S(2)}, u32[]{:S(2)}) collective-permute-start(bf16[2,272,384]{2,1,0:T(8,128)(2,1)S(1)} %pad_maximum_fusion.refs_0_), channel_id=1, source_target_pairs={{0,4},{2,6},{4,0},{6,2},{1,5},{3,7},{5,1},{7,3},{8,12},{10,14},{12... | collective-permute-start | bytes 1253384 | tf_op jit(solution)/shard_map/ppermute | solution.py:19
  39.0 20.2 %collective-permute-start.6 = (bf16[2,272,384]{2,1,0:T(8,128)(2,1)S(1)}, bf16[2,272,384]{2,1,0:T(8,128)(2,1)S(1)}, u32[]{:S(2)}, u32[]{:S(2)}) collective-permute-start(bf16[2,272,384]{2,1,0:T(8,128)(2,1)S(1)} %pad_maximum_fusion.refs_0_), channel_id=1, source_target_pairs={{0,6},{2,0},{4,2},{6,4},{1,7},{3,1},{5,3},{7,5},{8,14},{10,8},{12,... | collective-permute-start | bytes 1253384 | tf_op jit(solution)/shard_map/ppermute | solution.py:19
  44.1 60.0 %copy-start.20 = (f32[128]{0:T(128)S(1)}, f32[128]{0:T(128)}, u32[]{:S(2)}) copy-start(f32[128]{0:T(128)} %param.16) | copy-start | bytes 1540
  44.1 60.0 %copy-start.21 = (f32[128]{0:T(128)S(1)}, f32[128]{0:T(128)}, u32[]{:S(2)}) copy-start(f32[128]{0:T(128)} %param.17) | copy-start | bytes 1540
  44.1 17.7 %all-to-all-start = ((f32[4,64,384]{2,1,0:T(8,128)}), f32[4,64,384]{2,1,0:T(8,128)}, u32[]{:S(2)}, u32[]{:S(2)}) async-start(f32[4,64,384]{2,1,0:T(8,128)} %bitcast.25), calls=%async_computation | async-start | bytes 786432 | tf_op jit(solution)/shard_map/all_to_all | solution.py:254
  50.3 24.5 %collective-permute-start.1 = (bf16[2,272,384]{2,1,0:T(8,128)(2,1)S(1)}, bf16[2,272,384]{2,1,0:T(8,128)(2,1)S(1)}, u32[]{:S(2)}, u32[]{:S(2)}) collective-permute-start(bf16[2,272,384]{2,1,0:T(8,128)(2,1)S(1)} %pad_maximum_fusion.refs_0_), channel_id=1, source_target_pairs={{0,1},{1,0},{2,3},{3,2},{4,5},{5,4},{6,7},{7,6},{8,9},{9,8},{10,11... | collective-permute-start | bytes 1253384 | tf_op jit(solution)/shard_map/ppermute | solution.py:27
  54.0 22.3 %copy-start.6 = (bf16[2,272,384]{2,1,0:T(8,128)(2,1)}, bf16[2,272,384]{2,1,0:T(8,128)(2,1)S(1)}, u32[]{:S(2)}) copy-start(bf16[2,272,384]{2,1,0:T(8,128)(2,1)S(1)} %collective-permute-done.2.refs_2_) | copy-start | bytes 1253380
  54.0 21.6 %collective-permute-start.3 = (bf16[2,272,384]{2,1,0:T(8,128)(2,1)S(1)}, bf16[2,272,384]{2,1,0:T(8,128)(2,1)S(1)}, u32[]{:S(2)}, u32[]{:S(2)}) collective-permute-start(bf16[2,272,384]{2,1,0:T(8,128)(2,1)S(1)} %collective-permute-done.2.refs_2_), channel_id=1, source_target_pairs={{0,1},{1,0},{2,3},{3,2},{4,5},{5,4},{6,7},{7,6},{8,9},{9,8},{10,11... | collective-permute-start | bytes 1253384 | tf_op jit(solution)/shard_map/ppermute | solution.py:27
  56.0 20.4 %collective-permute-start.5 = (bf16[2,272,384]{2,1,0:T(8,128)(2,1)S(1)}, bf16[2,272,384]{2,1,0:T(8,128)(2,1)S(1)}, u32[]{:S(2)}, u32[]{:S(2)}) collective-permute-start(bf16[2,272,384]{2,1,0:T(8,128)(2,1)S(1)} %collective-permute-done.4.refs_4_), channel_id=1, source_target_pairs={{0,1},{1,0},{2,3},{3,2},{4,5},{5,4},{6,7},{7,6},{8,9},{9,8},{10,11... | collective-permute-start | bytes 1253384 | tf_op jit(solution)/shard_map/ppermute | solution.py:27
  58.4 0.8 copy-start.8
  59.2 18.0 %collective-permute-start.7 = (bf16[2,272,384]{2,1,0:T(8,128)(2,1)S(1)}, bf16[2,272,384]{2,1,0:T(8,128)(2,1)S(1)}, u32[]{:S(2)}, u32[]{:S(2)}) collective-permute-start(bf16[2,272,384]{2,1,0:T(8,128)(2,1)S(1)} %collective-permute-done.6.refs_6_), channel_id=1, source_target_pairs={{0,1},{1,0},{2,3},{3,2},{4,5},{5,4},{6,7},{7,6},{8,9},{9,8},{10,11... | collective-permute-start | bytes 1253384 | tf_op jit(solution)/shard_map/ppermute | solution.py:27
  61.1 0.8 copy-start.10
  63.4 26.4 %all-to-all-start.1 = ((f32[16,4,384]{2,1,0:T(4,128)}), f32[16,4,384]{2,1,0:T(4,128)S(1)}, u32[]{:S(2)}, u32[]{:S(2)}) async-start(f32[16,4,384]{2,1,0:T(4,128)} %reshape.18), calls=%async_computation.1 | async-start | bytes 196608 | tf_op jit(solution)/shard_map/all_to_all | solution.py:256
  74.8 0.8 copy-start.12
  75.6 0.8 copy-start.14
  76.4 0.8 copy-start.16
  77.1 0.8 copy-start.18
  77.9 1.0 copy-start.3
  78.9 1.0 copy-start.7
  79.9 1.0 copy-start.9
  80.9 1.0 copy-start.11
  81.9 1.0 copy-start.13
  82.9 1.0 copy-start.15
  83.9 1.0 copy-start.17
  84.9 1.0 copy-start.19
  104.1 2.1 %copy-start = (bf16[64,80,384]{2,1,0:T(8,128)(2,1)S(1)}, bf16[64,80,384]{2,1,0:T(8,128)(2,1)}, u32[]{:S(2)}) copy-start(bf16[64,80,384]{2,1,0:T(8,128)(2,1)} %all-gather.3.cloned.1.call-done) | copy-start | bytes 11796484
  106.2 42.4 %copy-start.22 = (s32[65]{0:T(128)S(1)}, s32[65]{0:T(128)}, u32[]{:S(2)}) copy-start(s32[65]{0:T(128)} %param.10) | copy-start | bytes 784
  106.2 43.6 %copy-start.1 = (bf16[64,80,384]{2,1,0:T(8,128)(2,1)S(1)}, bf16[64,80,384]{2,1,0:T(8,128)(2,1)}, u32[]{:S(2)}) copy-start(bf16[64,80,384]{2,1,0:T(8,128)(2,1)} %all-gather.3.cloned.1.call-done) | copy-start | bytes 11796484
  146.0 3.8 %collective-permute-start.8 = (bf16[4,512,128]{2,1,0:T(8,128)(2,1)S(1)}, bf16[4,512,128]{2,1,0:T(8,128)(2,1)S(1)}, u32[]{:S(2)}, u32[]{:S(2)}) collective-permute-start(bf16[4,512,128]{2,1,0:T(8,128)(2,1)S(1)} %all_to_all.32.mine_ref), channel_id=1, source_target_pairs={{0,1},{1,0},{2,3},{3,2},{4,5},{5,4},{6,7},{7,6},{8,9},{9,8},{10,11... | collective-permute-start | bytes 1572872 | tf_op jit(solution)/shard_map/ppermute | solution.py:27
Sparse Core Ops, SparseCore 0:
  23.0 81.1 all-gather.2

commit v2 on v1

--- a/solution.py
+++ b/solution.py
@@ -58,25 +58,33 @@
     out_ref[tokens:, :] = block.astype(jnp.bfloat16)
 
 
-def sort_kernel(qkv_ref, out_ref, to_ref, sems):
-    loads = []
-    for dest in range(NX):
-        at = pl.ds(dest % 2 * HD, HD)
-        pairs = [(out_ref, to_ref.at[dest, 48:80])]
-        for i in range(3):
-            pairs.append((qkv_ref.at[i, :, at], to_ref.at[dest, 0:48, i * HD : (i + 1) * HD]))
-        for i, (source, target) in enumerate(pairs):
-            loads.append(pltpu.make_async_copy(source, target, sems.at[dest, i]))
+def sort_kernel(qkv_hbm, out_hbm, to_ref, qkv_ref, out_ref, sems):
+    loads = [
+        pltpu.make_async_copy(qkv_hbm, qkv_ref, sems.at[0]),
+        pltpu.make_async_copy(out_hbm, out_ref, sems.at[1]),
+    ]
     for load in loads:
         load.start()
     for load in loads:
         load.wait()
-
-
-def norm_kernel(idx_ref, *refs):
-    xs, h_ref = refs[:8], refs[8]
-    y, c = idx_ref[2], idx_ref[3]
-    tokens, width = h_ref.shape[1], xs[0].shape[2]
+    for dest in range(NX):
+        head = dest % 2
+        for i in range(3):
+            to_ref[dest, 0:48, i * HD : (i + 1) * HD] = qkv_ref[i, :, head * HD : (head + 1) * HD]
+        to_ref[dest, 48:80, :] = out_ref[...]
+
+
+def order_kernel(all_ref, to_ref):
+    for x in range(NX):
+        for z in range(NZ):
+            row = (x * NZ + z) * 32
+            to_ref[row : row + 32, :] = all_ref[z, x, 48:80, :]
+
+
+def norm_kernel(idx_ref, mine_ref, other_ref, h_ref):
+    c = idx_ref[3]
+    xs = [ref.at[j] for j in range(NY) for ref in (mine_ref, other_ref)]
+    tokens, width = h_ref.shape[1], mine_ref.shape[3]
     features = 8 * width
     for slot in range(2):
         total = jnp.zeros((tokens, 1), jnp.float32)
@@ -91,7 +99,7 @@
         for j in range(NY):
             for i in range(NC):
                 part = xs[NC * j + i]
-                place = lax.rem(y + NY - j, NY) * NC + lax.rem(c + i, NC)
+                place = j * NC + lax.rem(c + i, NC)
                 mods = part[slot, tokens : tokens + 16, :].astype(jnp.float32)
                 cent = part[slot, 0:tokens, :].astype(jnp.float32) - mean
                 hidden = cent * inv * (1.0 + mods[1:2]) + mods[0:1]
@@ -124,8 +132,8 @@
         o_ref[lax.rem(odd + slot, 2)] = out.astype(jnp.bfloat16)
 
 
-def project_kernel(idx_ref, win_ref, dt_ref, gate_ref, lat_ref, mine_ref, other_ref, all_ref, *refs):
-    out_ref, a_ref, w_ref, term_ref, run_ref = refs
+def project_kernel(idx_ref, win_ref, dt_ref, gate_ref, lat_ref, mine_ref, other_ref, w_ref, *refs):
+    out_ref, a_ref, term_ref, run_ref = refs
     c = idx_ref[3]
     start, slide = win_ref[0], win_ref[1]
     for j in range(NY):
@@ -136,10 +144,6 @@
                 for m in range(2):
                     row = (2 * m + n) * 128
                     a_ref[m * 128 : (m + 1) * 128, at] = part[j, row : row + 128, :]
-    for x in range(NX):
-        for z in range(NZ):
-            row = (x * NZ + z) * 32
-            w_ref[row : row + 32, :] = all_ref[z, x, 48:80, :]
     proj = jnp.dot(a_ref[...], w_ref[...], preferred_element_type=jnp.float32)
     for slot in range(NX * NZ):
         row = slot // (2 * NZ) * 128 + slot % NZ * 8 + slot // NZ % 2 * 4
@@ -153,7 +157,9 @@
         run_ref[slot] = run
         return run + term_ref[slot]
 
-    total = lax.fori_loop(0, count, step, jnp.zeros(run_ref.shape[1:], jnp.float32))
+    total = lax.fori_loop(
+        0, count, step, jnp.zeros(run_ref.shape[1:], jnp.float32), unroll=8
+    )
 
     def move(i, _):
         run_ref[lax.rem(start + i, count)] = total
@@ -218,7 +224,11 @@
         out_shape=jax.ShapeDtypeStruct((NX, 80, 3 * HD), jnp.bfloat16),
         in_specs=[pl.BlockSpec(memory_space=pl.ANY)] * 2,
         out_specs=vmem(),
-        scratch_shapes=[pltpu.SemaphoreType.DMA((NX, 4))],
+        scratch_shapes=[
+            pltpu.VMEM(qkv_weight.shape, jnp.bfloat16),
+            pltpu.VMEM(out_weight.shape, jnp.bfloat16),
+            pltpu.SemaphoreType.DMA((2,)),
+        ],
         compiler_params=pltpu.CompilerParams(vmem_limit_bytes=61 * 1024 * 1024),
         name="sort",
     )(qkv_weight, out_weight)
@@ -238,22 +248,22 @@
         compiler_params=params(),
         name="pack",
     )(idx, emb, mod_weight, local)
-    both = jnp.stack([packed, swap_pair(packed)])
-    xs = [both] + [shift(both, "y", NY, j) for j in range(1, NY)]
-    xs = [b for mine in xs for b in (mine, swap_core(mine))]
+    everywhere = to_all(jnp.stack([packed, swap_pair(packed)]), "y", NY)
     hidden = pl.pallas_call(
         norm_kernel,
         out_shape=jax.ShapeDtypeStruct((2, tokens, 8 * width), jnp.bfloat16),
-        in_specs=[smem()] + [vmem()] * 8,
+        in_specs=[smem()] + [vmem()] * 2,
         out_specs=vmem(),
         compiler_params=params(),
         name="norm",
-    )(idx, *xs)
+    )(idx, everywhere, swap_core(everywhere))
 
     rows = tokens // count
-    first = lax.all_to_all(local.reshape(NX, tokens // NX, width), "x", 0, 0, tiled=True)
+    first = local.astype(jnp.float16).reshape(NX, tokens // NX, width)
+    first = lax.all_to_all(first, "x", 0, 0, tiled=True)
     first = lax.dynamic_index_in_dim(first, start // NZ, 0, keepdims=False)
     first = lax.all_to_all(first.reshape(NZ, rows, width), "z", 0, 0, tiled=True)
+    first = first.astype(jnp.float32)
     first, hidden = lax.optimization_barrier((first, hidden))
     attn = pl.pallas_call(
         attention_kernel,
@@ -267,6 +277,14 @@
     attn = attn.reshape(2, count, rows, HD).transpose(1, 0, 2, 3).reshape(count, 2 * rows, HD)
     attn = lax.all_to_all(attn, STEP, 0, 0, tiled=True).reshape(count * 2 * rows, HD)
     mine = to_all(attn, "y", NY)
+    out_rows = pl.pallas_call(
+        order_kernel,
+        out_shape=jax.ShapeDtypeStruct((2048, width), jnp.bfloat16),
+        in_specs=[vmem()],
+        out_specs=vmem(),
+        compiler_params=params(),
+        name="order",
+    )(weights)
     sums = pl.pallas_call(
         project_kernel,
         out_shape=jax.ShapeDtypeStruct((count, rows, width + 128), jnp.float32),
@@ -274,13 +292,12 @@
         out_specs=vmem(),
         scratch_shapes=[
             pltpu.VMEM((tokens, 2048), jnp.bfloat16),
-            pltpu.VMEM((2048, width), jnp.bfloat16),
             pltpu.VMEM((count, rows, width), jnp.float32),
             pltpu.VMEM((count, rows, width), jnp.float32),
         ],
         compiler_params=params(),
         name="project",
-    )(idx, jnp.stack([start, slide]), step_dts, gates, first, mine, swap_core(mine), weights)
+    )(idx, jnp.stack([start, slide]), step_dts, gates, first, mine, swap_core(mine), out_rows)
     back = lax.all_to_all(sums.astype(jnp.float16), STEP, 0, 0, tiled=True).astype(jnp.float32)
     return pl.pallas_call(
         unscale_kernel,

time: 189 us -> 186 us (0.984)
  blocking collectives: 78.4 us -> 123 us
  starting transfers between devices: 38.7 us -> 12 us
  waiting for transfers between devices: 22.7 us -> 11.4 us
  local copies, waits for them, and re-layouts: 18.6 us -> 9.64 us
    all_to_all x0 -> x1, blocking collectives: none -> 28 us  [per_device(): lax.all_to_all(first.reshape(NZ, rows, width), 'z', 0, 0, tiled=True)]
    all_to_all x1 -> x2, blocking collectives: 12.5 us -> 31.2 us  [to_all(): lax.all_to_all(jnp.broadcast_to(value[None], (size,) + value.shape), axis...]
    all_gather x1, waiting for transfers between devices: 14.3 us -> 0.02 us  [per_device(): lax.all_gather(lax.all_to_all(sorted_rows, 'x', 0, 0, tiled=True), 'z')]
    all_to_all x2 -> x1, starting transfers between devices: 17.6 us -> 6.04 us  [per_device(): first = lax.all_to_all(first, 'x', 0, 0, tiled=True)]
    ppermute x3 -> x0, starting transfers between devices: 8.97 us -> none  [shift(): lax.ppermute(value, axis, [(i, (i + by) % size) for i in range(size)])]
    unnamed x46 -> x22, local copies, waits for them, and re-layouts: 16.8 us -> 8.39 us
    ppermute x5 -> x2, starting transfers between devices: 10 us -> 3.82 us  [swap_core(): return lax.ppermute(value, 'c', [(i, i ^ 1) for i in range(NC)])]
    all_to_all x2 -> x1, waiting for transfers between devices: 0.01 us -> 4.94 us  [per_device(): first = lax.all_to_all(first, 'x', 0, 0, tiled=True)]
  transfers between devices with their start and end apart: 12 -> 5, of which waited for: 4 -> 3; matrix products, arithmetic and copies ran while one was open for 1% -> 2% of each run, Pallas kernels for 2% -> 2%
where the time goes in v2:
time: 186 us; the launch traced here: 185 us
  blocking collectives  123 us (66%)
  between operations  14.9 us (8%)
  Pallas kernels  12.3 us (7%)
  starting transfers between devices  12 us (6%)
  waiting for transfers between devices  11.4 us (6%)
  local copies, waits for them, and re-layouts  9.64 us (5%)
  other arithmetic  2 us (1%)
    all_to_all x2, blocking collectives, to_all(): lax.all_to_all(jnp.broadcast_to(value[None], (size,) + value.shape), axis...  31.2 us
    all_to_all x1, blocking collectives, per_device(): lax.all_to_all(first.reshape(NZ, rows, width), 'z', 0, 0, tiled=True)  28 us
    all_to_all x1, blocking collectives, per_device(): lax.all_to_all(sums.astype(jnp.float16), STEP, 0, 0, tiled=True)  27.3 us
    all_to_all x1, blocking collectives, per_device(): lax.all_to_all(attn, STEP, 0, 0, tiled=True).reshape(count * 2 * rows, HD)  21.9 us
    all_to_all x1, blocking collectives, per_device(): lax.all_to_all(sorted_rows, 'x', 0, 0, tiled=True)  14.5 us
    unnamed x22, local copies, waits for them, and re-layouts  8.39 us
    all_to_all x1, starting transfers between devices, per_device(): first = lax.all_to_all(first, 'x', 0, 0, tiled=True)  6.04 us
    ppermute x1, waiting for transfers between devices, swap_pair(): return lax.ppermute(value, 'x', [(i, i ^ 1) for i in range(NX)])  5.52 us
  transfers between devices with their start and end apart: 5, of which 3 were waited for; matrix products, arithmetic and copies ran while one was open for 2% of the time, Pallas kernels for 2%

profile of v2, /device:TPU:6, one launch (start us, length us, event | category | flops | bytes accessed | tf_op | source)
XLA Modules:
  0.0 185.1 jit_solution(2811926150601839760)
XLA Ops:
  6.5 0.0 all-gather.3.cloned.1.call-start
  6.5 1.7 sort.1
  8.2 14.5 %all_to_all.35 = bf16[4,80,384]{2,1,0:T(8,128)(2,1)} all-to-all(bf16[4,80,384]{2,1,0:T(8,128)(2,1)} %sort.1), channel_id=1, replica_groups=mesh['x'=4,'z'=16,'y'=4,'c'=2] {'x'}, dimensions={0} | all-to-all | bytes 491520 | tf_op jit(solution)/shard_map/all_to_all | solution.py:235
  22.7 0.0 all-gather.3.cloned.1.call-update
  23.4 0.7 convert_element_type.26
  24.0 0.1 stack.35.idx_ref
  24.1 0.2 multiply_cosine_fusion
  24.4 0.0 copy-start.6
  24.4 1.0 copy-done.6
  25.4 0.8 pack.1
  26.2 2.2 %collective-permute-start = (bf16[272,384]{1,0:T(8,128)(2,1)S(1)}, bf16[272,384]{1,0:T(8,128)(2,1)S(1)}, u32[]{:S(2)}, u32[]{:S(2)}) collective-permute-start(bf16[272,384]{1,0:T(8,128)(2,1)S(1)} %get-tuple-element.10), channel_id=1, source_target_pairs={{0,128},{128,0},{256,384},{384,256},{1,129},{129,1},{257,385},{385... | collective-permute-start | bytes 626696 | tf_op jit(solution)/shard_map/ppermute | solution.py:23
  28.4 5.5 %collective-permute-done = bf16[272,384]{1,0:T(8,128)(2,1)S(1)} collective-permute-done((bf16[272,384]{1,0:T(8,128)(2,1)S(1)}, bf16[272,384]{1,0:T(8,128)(2,1)S(1)}, u32[]{:S(2)}, u32[]{:S(2)}) %collective-permute-start) | collective-permute-done | bytes 208928 | tf_op jit(solution)/shard_map/ppermute | solution.py:23
  33.9 0.1 broadcast_in_dim.24
  34.1 18.4 %all_to_all.36.mine_ref = bf16[4,2,272,384]{3,2,1,0:T(8,128)(2,1)S(1)} all-to-all(bf16[4,2,272,384]{3,2,1,0:T(8,128)(2,1)S(1)} %broadcast_in_dim.24), channel_id=1, replica_groups=mesh['x'=4,'z'=16,'y'=4,'c'=2] {'y'}, dimensions={0} | all-to-all | bytes 3342336 | tf_op jit(solution)/shard_map/all_to_all | solution.py:31
  52.5 1.9 %collective-permute-start.1 = (bf16[4,2,272,384]{3,2,1,0:T(8,128)(2,1)S(1)}, bf16[4,2,272,384]{3,2,1,0:T(8,128)(2,1)S(1)}, u32[]{:S(2)}, u32[]{:S(2)}) collective-permute-start(bf16[4,2,272,384]{3,2,1,0:T(8,128)(2,1)S(1)} %all_to_all.36.mine_ref), channel_id=1, source_target_pairs={{0,1},{1,0},{2,3},{3,2},{4,5},{5,4},{6,7},{7,6},{8,9},{9,8},{10,11... | collective-permute-start | bytes 5013512 | tf_op jit(solution)/shard_map/ppermute | solution.py:27
  54.4 0.0 copy-start.2
  54.4 1.2 copy-done.2
  55.6 0.7 convert_element_type.28
  56.3 6.0 %all-to-all-start = ((f16[4,64,384]{2,1,0:T(8,128)(2,1)}), f16[4,64,384]{2,1,0:T(8,128)(2,1)}, u32[]{:S(2)}, u32[]{:S(2)}) async-start(f16[4,64,384]{2,1,0:T(8,128)(2,1)} %bitcast.30), calls=%async_computation | async-start | bytes 393216 | tf_op jit(solution)/shard_map/all_to_all | solution.py:263
  62.3 4.9 %all-to-all-done = f16[4,64,384]{2,1,0:T(8,128)(2,1)} async-done(((f16[4,64,384]{2,1,0:T(8,128)(2,1)}), f16[4,64,384]{2,1,0:T(8,128)(2,1)}, u32[]{:S(2)}, u32[]{:S(2)}) %all-to-all-start) | async-done | bytes 196640 | tf_op jit(solution)/shard_map/all_to_all | solution.py:263
  67.3 0.8 constant_dynamic-slice_fusion
  68.1 28.0 %all_to_all.37 = f16[16,4,384]{2,1,0:T(4,128)(2,1)S(1)} all-to-all(f16[16,4,384]{2,1,0:T(4,128)(2,1)S(1)} %reshape.22), channel_id=1, replica_groups=mesh['x'=4,'z'=16,'y'=4,'c'=2] {'z'}, dimensions={0} | all-to-all | bytes 98304 | tf_op jit(solution)/shard_map/all_to_all | solution.py:265
  96.1 0.0 collective-permute-done.1.other_ref
  96.2 1.2 copy-done.4
  97.4 1.4 copy-done.3
  98.8 1.4 copy-done.5
  100.3 3.6 %norm.1.h_ref = bf16[2,256,3072]{2,1,0:T(8,128)(2,1)S(1)} custom-call(s32[6]{0:T(128)S(1)} %stack.35.idx_ref, bf16[4,2,272,384]{3,2,1,0:T(8,128)(2,1)S(1)} %copy-done.3, bf16[4,2,272,384]{3,2,1,0:T(8,128)(2,1)S(1)} %copy-done.5), custom_call_target="tpu_custom_call" | custom-call | tf_op jit(solution)/shard_map/norm/pallas_call | solution.py:252
  103.9 0.0 all-gather.3.cloned.1.call-done
  103.9 0.0 copy-done.8
  103.9 0.0 copy-done.9
  103.9 0.0 copy-start
  103.9 2.1 %copy-done = bf16[64,80,384]{2,1,0:T(8,128)(2,1)S(1)} copy-done((bf16[64,80,384]{2,1,0:T(8,128)(2,1)S(1)}, bf16[64,80,384]{2,1,0:T(8,128)(2,1)}, u32[]{:S(2)}) %copy-start) | copy-done | bytes 3932184
  106.0 3.3 %attention.1 = bf16[2,256,128]{2,1,0:T(8,128)(2,1)S(1)} custom-call(s32[6]{0:T(128)S(1)} %stack.35.idx_ref, f32[1,128]{1,0:T(1,128)S(1)} %bitcast.28, f32[1,128]{1,0:T(1,128)S(1)} %bitcast.29, bf16[2,256,3072]{2,1,0:T(8,128)(2,1)S(1)} %norm.1.h_ref, bf16[16,4,80,384]{3,2,1,0:T(8,128)(2,1)S(1)} %bitcast.23), custom_call_target="tpu_custom_call" | custom-call | tf_op jit(solution)/shard_map/attention/pallas_call | solution.py:268
  109.3 0.1 copy.14
  109.4 21.9 %all_to_all.38 = bf16[64,8,128]{2,1,0:T(8,128)(2,1)S(1)} all-to-all(bf16[64,8,128]{2,1,0:T(8,128)(2,1)S(1)} %copy.14), channel_id=1, replica_groups=mesh['x'=4,'z'=16,'y'=4,'c'=2] {'x','z'}, dimensions={0} | all-to-all | bytes 262144 | tf_op jit(solution)/shard_map/all_to_all | solution.py:278
  131.3 0.1 broadcast_in_dim.28
  131.4 12.8 %all_to_all.39.mine_ref = bf16[4,512,128]{2,1,0:T(8,128)(2,1)S(1)} all-to-all(bf16[4,512,128]{2,1,0:T(8,128)(2,1)S(1)} %broadcast_in_dim.28), channel_id=1, replica_groups=mesh['x'=4,'z'=16,'y'=4,'c'=2] {'y'}, dimensions={0} | all-to-all | bytes 1048576 | tf_op jit(solution)/shard_map/all_to_all | solution.py:31
  144.2 1.9 %collective-permute-start.2 = (bf16[4,512,128]{2,1,0:T(8,128)(2,1)S(1)}, bf16[4,512,128]{2,1,0:T(8,128)(2,1)S(1)}, u32[]{:S(2)}, u32[]{:S(2)}) collective-permute-start(bf16[4,512,128]{2,1,0:T(8,128)(2,1)S(1)} %all_to_all.39.mine_ref), channel_id=1, source_target_pairs={{0,1},{1,0},{2,3},{3,2},{4,5},{5,4},{6,7},{7,6},{8,9},{9,8},{10,11... | collective-permute-start | bytes 1572872 | tf_op jit(solution)/shard_map/ppermute | solution.py:27
  146.8 0.1 pad_add_fusion.win_ref
  146.8 0.1 convert_multiply_fusion.dt_ref
  146.9 0.0 copy-done.1
  146.9 0.1 order.1.w_ref
  147.0 0.9 collective-permute-done.2.other_ref
  148.0 2.0 %project.1 = f32[64,4,512]{2,1,0:T(4,128)S(1)} custom-call(s32[6]{0:T(128)S(1)} %stack.35.idx_ref, s32[2]{0:T(128)S(1)} %pad_add_fusion.win_ref, f32[64]{0:T(128)S(1)} %convert_multiply_fusion.dt_ref, f32[64,384]{1,0:T(8,128)S(1)} %get-tuple-element.9.gate_ref, f32[16,4,384]{2,1,0:T(4,128)S(1)} %convert_element_type.30.lat_ref, ...), custom_call_target="tpu_custom_call" | custom-call | tf_op jit(solution)/shard_map/project/pallas_call | solution.py:288
  150.0 0.1 convert_element_type.31
  150.1 27.3 %all_to_all.40 = f16[64,4,512]{2,1,0:T(4,128)(2,1)S(1)} all-to-all(f16[64,4,512]{2,1,0:T(4,128)(2,1)S(1)} %convert_element_type.31), channel_id=1, replica_groups=mesh['x'=4,'z'=16,'y'=4,'c'=2] {'x','z'}, dimensions={0} | all-to-all | bytes 524288 | tf_op jit(solution)/shard_map/all_to_all | solution.py:301
  177.4 0.1 convert_element_type.32.in_ref
  177.5 0.8 unscale.1
  (17 shorter events, 0.2 us)
Async XLA Ops:
  6.5 17.8 %copy-start.7 = (bf16[3,256,384]{2,1,0:T(8,128)(2,1)S(1)}, bf16[3,256,384]{2,1,0:T(8,128)(2,1)}, u32[]{:S(2)}) copy-start(bf16[3,256,384]{2,1,0:T(8,128)(2,1)} %mod_ref.1) | copy-start | bytes 1769476
  6.5 97.4 %all-gather.3.cloned.1.call-start = ((), (), s32[]{:S(2)}) async-start(), calls=%async_computation.7 | async-start | bytes 4177920 | tf_op jit(solution)/shard_map/all_gather | solution.py:235
  24.4 1.0 copy-start.6
  26.2 7.7 %collective-permute-start = (bf16[272,384]{1,0:T(8,128)(2,1)S(1)}, bf16[272,384]{1,0:T(8,128)(2,1)S(1)}, u32[]{:S(2)}, u32[]{:S(2)}) collective-permute-start(bf16[272,384]{1,0:T(8,128)(2,1)S(1)} %get-tuple-element.10), channel_id=1, source_target_pairs={{0,128},{128,0},{256,384},{384,256},{1,129},{129,1},{257,385},{385... | collective-permute-start | bytes 626696 | tf_op jit(solution)/shard_map/ppermute | solution.py:23
  52.5 43.7 %collective-permute-start.1 = (bf16[4,2,272,384]{3,2,1,0:T(8,128)(2,1)S(1)}, bf16[4,2,272,384]{3,2,1,0:T(8,128)(2,1)S(1)}, u32[]{:S(2)}, u32[]{:S(2)}) collective-permute-start(bf16[4,2,272,384]{3,2,1,0:T(8,128)(2,1)S(1)} %all_to_all.36.mine_ref), channel_id=1, source_target_pairs={{0,1},{1,0},{2,3},{3,2},{4,5},{5,4},{6,7},{7,6},{8,9},{9,8},{10,11... | collective-permute-start | bytes 5013512 | tf_op jit(solution)/shard_map/ppermute | solution.py:27
  54.4 1.2 copy-start.2
  56.3 11.0 %all-to-all-start = ((f16[4,64,384]{2,1,0:T(8,128)(2,1)}), f16[4,64,384]{2,1,0:T(8,128)(2,1)}, u32[]{:S(2)}, u32[]{:S(2)}) async-start(f16[4,64,384]{2,1,0:T(8,128)(2,1)} %bitcast.30), calls=%async_computation | async-start | bytes 393216 | tf_op jit(solution)/shard_map/all_to_all | solution.py:263
  96.2 1.2 copy-start.4
  97.4 1.5 copy-start.3
  98.8 1.4 copy-start.5
  100.2 3.7 %copy-start.8 = (f32[128]{0:T(128)S(1)}, f32[128]{0:T(128)}, u32[]{:S(2)}) copy-start(f32[128]{0:T(128)} %param.16) | copy-start | bytes 1540
  100.2 3.7 %copy-start.9 = (f32[128]{0:T(128)S(1)}, f32[128]{0:T(128)}, u32[]{:S(2)}) copy-start(f32[128]{0:T(128)} %param.17) | copy-start | bytes 1540
  103.9 2.1 %copy-start = (bf16[64,80,384]{2,1,0:T(8,128)(2,1)S(1)}, bf16[64,80,384]{2,1,0:T(8,128)(2,1)}, u32[]{:S(2)}) copy-start(bf16[64,80,384]{2,1,0:T(8,128)(2,1)} %all-gather.3.cloned.1.call-done) | copy-start | bytes 11796484
  106.0 40.9 %copy-start.1 = (bf16[64,80,384]{2,1,0:T(8,128)(2,1)S(1)}, bf16[64,80,384]{2,1,0:T(8,128)(2,1)}, u32[]{:S(2)}) copy-start(bf16[64,80,384]{2,1,0:T(8,128)(2,1)} %all-gather.3.cloned.1.call-done) | copy-start | bytes 11796484
  109.3 37.5 %copy-start.10 = (s32[65]{0:T(128)S(1)}, s32[65]{0:T(128)}, u32[]{:S(2)}) copy-start(s32[65]{0:T(128)} %param.10) | copy-start | bytes 784
  144.2 3.8 %collective-permute-start.2 = (bf16[4,512,128]{2,1,0:T(8,128)(2,1)S(1)}, bf16[4,512,128]{2,1,0:T(8,128)(2,1)S(1)}, u32[]{:S(2)}, u32[]{:S(2)}) collective-permute-start(bf16[4,512,128]{2,1,0:T(8,128)(2,1)S(1)} %all_to_all.39.mine_ref), channel_id=1, source_target_pairs={{0,1},{1,0},{2,3},{3,2},{4,5},{5,4},{6,7},{7,6},{8,9},{9,8},{10,11... | collective-permute-start | bytes 1572872 | tf_op jit(solution)/shard_map/ppermute | solution.py:27
Sparse Core Ops, SparseCore 0:
  22.8 77.8 all-gather.2

commit v3 on v2

--- a/solution.py
+++ b/solution.py
@@ -81,10 +81,10 @@
             to_ref[row : row + 32, :] = all_ref[z, x, 48:80, :]
 
 
-def norm_kernel(idx_ref, mine_ref, other_ref, h_ref):
-    c = idx_ref[3]
-    xs = [ref.at[j] for j in range(NY) for ref in (mine_ref, other_ref)]
-    tokens, width = h_ref.shape[1], mine_ref.shape[3]
+def norm_kernel(idx_ref, *refs):
+    xs, h_ref = refs[:8], refs[8]
+    y, c = idx_ref[2], idx_ref[3]
+    tokens, width = h_ref.shape[1], xs[0].shape[2]
     features = 8 * width
     for slot in range(2):
         total = jnp.zeros((tokens, 1), jnp.float32)
@@ -99,7 +99,7 @@
         for j in range(NY):
             for i in range(NC):
                 part = xs[NC * j + i]
-                place = j * NC + lax.rem(c + i, NC)
+                place = lax.rem(y + NY - j, NY) * NC + lax.rem(c + i, NC)
                 mods = part[slot, tokens : tokens + 16, :].astype(jnp.float32)
                 cent = part[slot, 0:tokens, :].astype(jnp.float32) - mean
                 hidden = cent * inv * (1.0 + mods[1:2]) + mods[0:1]
@@ -248,15 +248,17 @@
         compiler_params=params(),
         name="pack",
     )(idx, emb, mod_weight, local)
-    everywhere = to_all(jnp.stack([packed, swap_pair(packed)]), "y", NY)
+    both = jnp.stack([packed, swap_pair(packed)])
+    xs = [both] + [shift(both, "y", NY, j) for j in range(1, NY)]
+    xs = [b for mine in xs for b in (mine, swap_core(mine))]
     hidden = pl.pallas_call(
         norm_kernel,
         out_shape=jax.ShapeDtypeStruct((2, tokens, 8 * width), jnp.bfloat16),
-        in_specs=[smem()] + [vmem()] * 2,
+        in_specs=[smem()] + [vmem()] * 8,
         out_specs=vmem(),
         compiler_params=params(),
         name="norm",
-    )(idx, everywhere, swap_core(everywhere))
+    )(idx, *xs)
 
     rows = tokens // count
     first = local.astype(jnp.float16).reshape(NX, tokens // NX, width)

time: 186 us -> 187 us (level)
  blocking collectives: 123 us -> 103 us
  starting transfers between devices: 12 us -> 27.2 us
  local copies, waits for them, and re-layouts: 9.64 us -> 17.9 us
  waiting for transfers between devices: 11.4 us -> 7.78 us
    all_to_all x2 -> x1, blocking collectives: 31.2 us -> 13.1 us  [to_all(): lax.all_to_all(jnp.broadcast_to(value[None], (size,) + value.shape), axis...]
    ppermute x0 -> x3, starting transfers between devices: none -> 8.97 us  [shift(): lax.ppermute(value, axis, [(i, (i + by) % size) for i in range(size)])]
    unnamed x22 -> x46, local copies, waits for them, and re-layouts: 8.39 us -> 16.8 us
    ppermute x2 -> x5, starting transfers between devices: 3.82 us -> 10 us  [swap_core(): return lax.ppermute(value, 'c', [(i, i ^ 1) for i in range(NC)])]
    all_to_all x1, waiting for transfers between devices: 4.94 us -> 0.01 us  [per_device(): first = lax.all_to_all(first, 'x', 0, 0, tiled=True)]
    all_to_all x1, blocking collectives: 28 us -> 24.6 us  [per_device(): lax.all_to_all(first.reshape(NZ, rows, width), 'z', 0, 0, tiled=True)]
  transfers between devices with their start and end apart: 5 -> 11, of which waited for: 3 -> 3; matrix products, arithmetic and copies ran while one was open for 2% -> 1% of each run, Pallas kernels for 2% -> 3%
where the time goes in v3:
time: 187 us; the launch traced here: 186 us
  blocking collectives  103 us (55%)
  starting transfers between devices  27.2 us (15%)
  local copies, waits for them, and re-layouts  17.9 us (10%)
  between operations  15 us (8%)
  Pallas kernels  12.4 us (7%)
  waiting for transfers between devices  7.78 us (4%)
  other arithmetic  2 us (1%)
    all_to_all x1, blocking collectives, per_device(): lax.all_to_all(sums.astype(jnp.float16), STEP, 0, 0, tiled=True)  27.6 us
    all_to_all x1, blocking collectives, per_device(): lax.all_to_all(first.reshape(NZ, rows, width), 'z', 0, 0, tiled=True)  24.6 us
    all_to_all x1, blocking collectives, per_device(): lax.all_to_all(attn, STEP, 0, 0, tiled=True).reshape(count * 2 * rows, HD)  23.5 us
    unnamed x46, local copies, waits for them, and re-layouts  16.8 us
    all_to_all x1, blocking collectives, per_device(): lax.all_to_all(sorted_rows, 'x', 0, 0, tiled=True)  14.5 us
    all_to_all x1, blocking collectives, to_all(): lax.all_to_all(jnp.broadcast_to(value[None], (size,) + value.shape), axis...  13.1 us
    ppermute x5, starting transfers between devices, swap_core(): return lax.ppermute(value, 'c', [(i, i ^ 1) for i in range(NC)])  10 us
    ppermute x3, starting transfers between devices, shift(): lax.ppermute(value, axis, [(i, (i + by) % size) for i in range(size)])  8.97 us
  transfers between devices with their start and end apart: 11, of which 3 were waited for; matrix products, arithmetic and copies ran while one was open for 1% of the time, Pallas kernels for 3%

profile of v3, /device:TPU:6, one launch (start us, length us, event | category | flops | bytes accessed | tf_op | source)
XLA Modules:
  0.0 185.6 jit_solution(17905698278374769210)
XLA Ops:
  6.5 1.6 sort.1
  8.2 14.5 %all_to_all.30 = bf16[4,80,384]{2,1,0:T(8,128)(2,1)} all-to-all(bf16[4,80,384]{2,1,0:T(8,128)(2,1)} %sort.1), channel_id=1, replica_groups=mesh['x'=4,'z'=16,'y'=4,'c'=2] {'x'}, dimensions={0} | all-to-all | bytes 491520 | tf_op jit(solution)/shard_map/all_to_all | solution.py:235
  23.3 0.7 convert_element_type.26
  24.1 0.2 multiply_cosine_fusion
  24.3 1.0 copy-done.4
  25.3 1.1 copy-done.5
  26.4 0.8 pack.1
  27.2 2.2 %collective-permute-start = (bf16[272,384]{1,0:T(8,128)(2,1)S(1)}, bf16[272,384]{1,0:T(8,128)(2,1)S(1)}, u32[]{:S(2)}, u32[]{:S(2)}) collective-permute-start(bf16[272,384]{1,0:T(8,128)(2,1)S(1)} %get-tuple-element.10), channel_id=1, source_target_pairs={{0,128},{128,0},{256,384},{384,256},{1,129},{129,1},{257,385},{385... | collective-permute-start | bytes 626696 | tf_op jit(solution)/shard_map/ppermute | solution.py:23
  29.4 5.5 %collective-permute-done = bf16[272,384]{1,0:T(8,128)(2,1)S(1)} collective-permute-done((bf16[272,384]{1,0:T(8,128)(2,1)S(1)}, bf16[272,384]{1,0:T(8,128)(2,1)S(1)}, u32[]{:S(2)}, u32[]{:S(2)}) %collective-permute-start) | collective-permute-done | bytes 208928 | tf_op jit(solution)/shard_map/ppermute | solution.py:23
  34.9 1.9 %collective-permute-start.2 = (bf16[2,272,384]{2,1,0:T(8,128)(2,1)S(1)}, bf16[2,272,384]{2,1,0:T(8,128)(2,1)S(1)}, u32[]{:S(2)}, u32[]{:S(2)}) collective-permute-start(bf16[2,272,384]{2,1,0:T(8,128)(2,1)S(1)} %pad_maximum_fusion.refs_0_), channel_id=1, source_target_pairs={{0,2},{2,4},{4,6},{6,0},{1,3},{3,5},{5,7},{7,1},{8,10},{10,12},{12... | collective-permute-start | bytes 1253384 | tf_op jit(solution)/shard_map/ppermute | solution.py:19
  36.9 1.9 %collective-permute-start.4 = (bf16[2,272,384]{2,1,0:T(8,128)(2,1)S(1)}, bf16[2,272,384]{2,1,0:T(8,128)(2,1)S(1)}, u32[]{:S(2)}, u32[]{:S(2)}) collective-permute-start(bf16[2,272,384]{2,1,0:T(8,128)(2,1)S(1)} %pad_maximum_fusion.refs_0_), channel_id=1, source_target_pairs={{0,4},{2,6},{4,0},{6,2},{1,5},{3,7},{5,1},{7,3},{8,12},{10,14},{12... | collective-permute-start | bytes 1253384 | tf_op jit(solution)/shard_map/ppermute | solution.py:19
  38.8 5.1 %collective-permute-start.6 = (bf16[2,272,384]{2,1,0:T(8,128)(2,1)S(1)}, bf16[2,272,384]{2,1,0:T(8,128)(2,1)S(1)}, u32[]{:S(2)}, u32[]{:S(2)}) collective-permute-start(bf16[2,272,384]{2,1,0:T(8,128)(2,1)S(1)} %pad_maximum_fusion.refs_0_), channel_id=1, source_target_pairs={{0,6},{2,0},{4,2},{6,4},{1,7},{3,1},{5,3},{7,5},{8,14},{10,8},{12,... | collective-permute-start | bytes 1253384 | tf_op jit(solution)/shard_map/ppermute | solution.py:19
  43.9 0.7 convert_element_type.28
  44.6 6.0 %all-to-all-start = ((f16[4,64,384]{2,1,0:T(8,128)(2,1)}), f16[4,64,384]{2,1,0:T(8,128)(2,1)}, u32[]{:S(2)}, u32[]{:S(2)}) async-start(f16[4,64,384]{2,1,0:T(8,128)(2,1)} %bitcast.6), calls=%async_computation | async-start | bytes 393216 | tf_op jit(solution)/shard_map/all_to_all | solution.py:265
  50.7 1.9 %collective-permute-start.1 = (bf16[2,272,384]{2,1,0:T(8,128)(2,1)S(1)}, bf16[2,272,384]{2,1,0:T(8,128)(2,1)S(1)}, u32[]{:S(2)}, u32[]{:S(2)}) collective-permute-start(bf16[2,272,384]{2,1,0:T(8,128)(2,1)S(1)} %pad_maximum_fusion.refs_0_), channel_id=1, source_target_pairs={{0,1},{1,0},{2,3},{3,2},{4,5},{5,4},{6,7},{7,6},{8,9},{9,8},{10,11... | collective-permute-start | bytes 1253384 | tf_op jit(solution)/shard_map/ppermute | solution.py:27
  52.6 1.3 collective-permute-done.2.refs_2_
  53.9 1.9 %collective-permute-start.3 = (bf16[2,272,384]{2,1,0:T(8,128)(2,1)S(1)}, bf16[2,272,384]{2,1,0:T(8,128)(2,1)S(1)}, u32[]{:S(2)}, u32[]{:S(2)}) collective-permute-start(bf16[2,272,384]{2,1,0:T(8,128)(2,1)S(1)} %collective-permute-done.2.refs_2_), channel_id=1, source_target_pairs={{0,1},{1,0},{2,3},{3,2},{4,5},{5,4},{6,7},{7,6},{8,9},{9,8},{10,11... | collective-permute-start | bytes 1253384 | tf_op jit(solution)/shard_map/ppermute | solution.py:27
  55.8 2.4 %collective-permute-start.5 = (bf16[2,272,384]{2,1,0:T(8,128)(2,1)S(1)}, bf16[2,272,384]{2,1,0:T(8,128)(2,1)S(1)}, u32[]{:S(2)}, u32[]{:S(2)}) collective-permute-start(bf16[2,272,384]{2,1,0:T(8,128)(2,1)S(1)} %collective-permute-done.4.refs_4_), channel_id=1, source_target_pairs={{0,1},{1,0},{2,3},{3,2},{4,5},{5,4},{6,7},{7,6},{8,9},{9,8},{10,11... | collective-permute-start | bytes 1253384 | tf_op jit(solution)/shard_map/ppermute | solution.py:27
  58.2 0.8 copy-done.8
  59.0 1.9 %collective-permute-start.7 = (bf16[2,272,384]{2,1,0:T(8,128)(2,1)S(1)}, bf16[2,272,384]{2,1,0:T(8,128)(2,1)S(1)}, u32[]{:S(2)}, u32[]{:S(2)}) collective-permute-start(bf16[2,272,384]{2,1,0:T(8,128)(2,1)S(1)} %collective-permute-done.6.refs_6_), channel_id=1, source_target_pairs={{0,1},{1,0},{2,3},{3,2},{4,5},{5,4},{6,7},{7,6},{8,9},{9,8},{10,11... | collective-permute-start | bytes 1253384 | tf_op jit(solution)/shard_map/ppermute | solution.py:27
  60.9 0.8 copy-done.10
  61.7 0.8 constant_dynamic-slice_fusion
  62.5 24.6 %all_to_all.31 = f16[16,4,384]{2,1,0:T(4,128)(2,1)S(1)} all-to-all(f16[16,4,384]{2,1,0:T(4,128)(2,1)S(1)} %reshape.21), channel_id=1, replica_groups=mesh['x'=4,'z'=16,'y'=4,'c'=2] {'z'}, dimensions={0} | all-to-all | bytes 98304 | tf_op jit(solution)/shard_map/all_to_all | solution.py:267
  87.2 0.8 copy-done.12
  88.0 0.8 copy-done.14
  88.8 0.7 copy-done.16
  89.5 0.7 copy-done.18
  90.3 1.0 copy-done.3
  91.3 1.0 copy-done.7
  92.3 1.0 copy-done.9
  93.3 1.0 copy-done.11
  94.3 1.0 copy-done.13
  95.3 1.0 copy-done.15
  96.3 1.0 copy-done.17
  97.3 1.0 copy-done.19
  98.3 3.9 %norm.1.h_ref = bf16[2,256,3072]{2,1,0:T(8,128)(2,1)S(1)} custom-call(s32[6]{0:T(128)S(1)} %stack.35.idx_ref, bf16[2,272,384]{2,1,0:T(8,128)(2,1)S(1)} %copy-done.3, bf16[2,272,384]{2,1,0:T(8,128)(2,1)S(1)} %copy-done.13, bf16[2,272,384]{2,1,0:T(8,128)(2,1)S(1)} %copy-done.7, bf16[2,272,384]{2,1,0:T(8,128)(2,1)S(1)} %copy-done.15, ...), custom_call_target="tpu_custom_call" | custom-call | tf_op jit(solution)/shard_map/norm/pallas_call | solution.py:254
  102.2 2.1 %copy-done = bf16[64,80,384]{2,1,0:T(8,128)(2,1)S(1)} copy-done((bf16[64,80,384]{2,1,0:T(8,128)(2,1)S(1)}, bf16[64,80,384]{2,1,0:T(8,128)(2,1)}, u32[]{:S(2)}) %copy-start) | copy-done | bytes 3932184
  104.4 3.3 %attention.1 = bf16[2,256,128]{2,1,0:T(8,128)(2,1)S(1)} custom-call(s32[6]{0:T(128)S(1)} %stack.35.idx_ref, f32[1,128]{1,0:T(1,128)S(1)} %bitcast.28, f32[1,128]{1,0:T(1,128)S(1)} %bitcast.29, bf16[2,256,3072]{2,1,0:T(8,128)(2,1)S(1)} %norm.1.h_ref, bf16[16,4,80,384]{3,2,1,0:T(8,128)(2,1)S(1)} %bitcast.23), custom_call_target="tpu_custom_call" | custom-call | tf_op jit(solution)/shard_map/attention/pallas_call | solution.py:270
  107.8 23.5 %all_to_all.32 = bf16[64,8,128]{2,1,0:T(8,128)(2,1)S(1)} all-to-all(bf16[64,8,128]{2,1,0:T(8,128)(2,1)S(1)} %copy.14), channel_id=1, replica_groups=mesh['x'=4,'z'=16,'y'=4,'c'=2] {'x','z'}, dimensions={0} | all-to-all | bytes 262144 | tf_op jit(solution)/shard_map/all_to_all | solution.py:280
  131.3 13.1 %all_to_all.33.mine_ref = bf16[4,512,128]{2,1,0:T(8,128)(2,1)S(1)} all-to-all(bf16[4,512,128]{2,1,0:T(8,128)(2,1)S(1)} %broadcast_in_dim.21), channel_id=1, replica_groups=mesh['x'=4,'z'=16,'y'=4,'c'=2] {'y'}, dimensions={0} | all-to-all | bytes 1048576 | tf_op jit(solution)/shard_map/all_to_all | solution.py:31
  144.5 1.9 %collective-permute-start.8 = (bf16[4,512,128]{2,1,0:T(8,128)(2,1)S(1)}, bf16[4,512,128]{2,1,0:T(8,128)(2,1)S(1)}, u32[]{:S(2)}, u32[]{:S(2)}) collective-permute-start(bf16[4,512,128]{2,1,0:T(8,128)(2,1)S(1)} %all_to_all.33.mine_ref), channel_id=1, source_target_pairs={{0,1},{1,0},{2,3},{3,2},{4,5},{5,4},{6,7},{7,6},{8,9},{9,8},{10,11... | collective-permute-start | bytes 1572872 | tf_op jit(solution)/shard_map/ppermute | solution.py:27
  147.2 0.1 order.1.w_ref
  147.3 0.9 collective-permute-done.8.other_ref
  148.3 1.9 %project.1 = f32[64,4,512]{2,1,0:T(4,128)S(1)} custom-call(s32[6]{0:T(128)S(1)} %stack.35.idx_ref, s32[2]{0:T(128)S(1)} %pad_add_fusion.win_ref, f32[64]{0:T(128)S(1)} %convert_multiply_fusion.dt_ref, f32[64,384]{1,0:T(8,128)S(1)} %get-tuple-element.9.gate_ref, f32[16,4,384]{2,1,0:T(4,128)S(1)} %convert_element_type.30.lat_ref, ...), custom_call_target="tpu_custom_call" | custom-call | tf_op jit(solution)/shard_map/project/pallas_call | solution.py:290
  150.2 0.1 convert_element_type.31
  150.3 27.6 %all_to_all.34 = f16[64,4,512]{2,1,0:T(4,128)(2,1)S(1)} all-to-all(f16[64,4,512]{2,1,0:T(4,128)(2,1)S(1)} %convert_element_type.31), channel_id=1, replica_groups=mesh['x'=4,'z'=16,'y'=4,'c'=2] {'x','z'}, dimensions={0} | all-to-all | bytes 524288 | tf_op jit(solution)/shard_map/all_to_all | solution.py:303
  177.9 0.1 convert_element_type.32.in_ref
  178.0 0.8 unscale.1
  (51 shorter events, 0.7 us)
Async XLA Ops:
  6.5 95.7 %all-gather.3.cloned.1.call-start = ((), (), s32[]{:S(2)}) async-start(), calls=%async_computation.6 | async-start | bytes 4177920 | tf_op jit(solution)/shard_map/all_gather | solution.py:235
  24.3 1.0 copy-start.4
  25.3 1.1 copy-start.5
  27.2 7.7 %collective-permute-start = (bf16[272,384]{1,0:T(8,128)(2,1)S(1)}, bf16[272,384]{1,0:T(8,128)(2,1)S(1)}, u32[]{:S(2)}, u32[]{:S(2)}) collective-permute-start(bf16[272,384]{1,0:T(8,128)(2,1)S(1)} %get-tuple-element.10), channel_id=1, source_target_pairs={{0,128},{128,0},{256,384},{384,256},{1,129},{129,1},{257,385},{385... | collective-permute-start | bytes 626696 | tf_op jit(solution)/shard_map/ppermute | solution.py:23
  34.9 53.8 %copy-start.2 = (bf16[2,272,384]{2,1,0:T(8,128)(2,1)}, bf16[2,272,384]{2,1,0:T(8,128)(2,1)S(1)}, u32[]{:S(2)}) copy-start(bf16[2,272,384]{2,1,0:T(8,128)(2,1)S(1)} %pad_maximum_fusion.refs_0_) | copy-start | bytes 1253380
  34.9 18.9 %collective-permute-start.2 = (bf16[2,272,384]{2,1,0:T(8,128)(2,1)S(1)}, bf16[2,272,384]{2,1,0:T(8,128)(2,1)S(1)}, u32[]{:S(2)}, u32[]{:S(2)}) collective-permute-start(bf16[2,272,384]{2,1,0:T(8,128)(2,1)S(1)} %pad_maximum_fusion.refs_0_), channel_id=1, source_target_pairs={{0,2},{2,4},{4,6},{6,0},{1,3},{3,5},{5,7},{7,1},{8,10},{10,12},{12... | collective-permute-start | bytes 1253384 | tf_op jit(solution)/shard_map/ppermute | solution.py:19
  36.9 18.9 %collective-permute-start.4 = (bf16[2,272,384]{2,1,0:T(8,128)(2,1)S(1)}, bf16[2,272,384]{2,1,0:T(8,128)(2,1)S(1)}, u32[]{:S(2)}, u32[]{:S(2)}) collective-permute-start(bf16[2,272,384]{2,1,0:T(8,128)(2,1)S(1)} %pad_maximum_fusion.refs_0_), channel_id=1, source_target_pairs={{0,4},{2,6},{4,0},{6,2},{1,5},{3,7},{5,1},{7,3},{8,12},{10,14},{12... | collective-permute-start | bytes 1253384 | tf_op jit(solution)/shard_map/ppermute | solution.py:19
  38.8 20.2 %collective-permute-start.6 = (bf16[2,272,384]{2,1,0:T(8,128)(2,1)S(1)}, bf16[2,272,384]{2,1,0:T(8,128)(2,1)S(1)}, u32[]{:S(2)}, u32[]{:S(2)}) collective-permute-start(bf16[2,272,384]{2,1,0:T(8,128)(2,1)S(1)} %pad_maximum_fusion.refs_0_), channel_id=1, source_target_pairs={{0,6},{2,0},{4,2},{6,4},{1,7},{3,1},{5,3},{7,5},{8,14},{10,8},{12,... | collective-permute-start | bytes 1253384 | tf_op jit(solution)/shard_map/ppermute | solution.py:19
  44.6 17.0 %all-to-all-start = ((f16[4,64,384]{2,1,0:T(8,128)(2,1)}), f16[4,64,384]{2,1,0:T(8,128)(2,1)}, u32[]{:S(2)}, u32[]{:S(2)}) async-start(f16[4,64,384]{2,1,0:T(8,128)(2,1)} %bitcast.6), calls=%async_computation | async-start | bytes 393216 | tf_op jit(solution)/shard_map/all_to_all | solution.py:265
  50.7 36.5 %collective-permute-start.1 = (bf16[2,272,384]{2,1,0:T(8,128)(2,1)S(1)}, bf16[2,272,384]{2,1,0:T(8,128)(2,1)S(1)}, u32[]{:S(2)}, u32[]{:S(2)}) collective-permute-start(bf16[2,272,384]{2,1,0:T(8,128)(2,1)S(1)} %pad_maximum_fusion.refs_0_), channel_id=1, source_target_pairs={{0,1},{1,0},{2,3},{3,2},{4,5},{5,4},{6,7},{7,6},{8,9},{9,8},{10,11... | collective-permute-start | bytes 1253384 | tf_op jit(solution)/shard_map/ppermute | solution.py:27
  53.9 34.9 %copy-start.6 = (bf16[2,272,384]{2,1,0:T(8,128)(2,1)}, bf16[2,272,384]{2,1,0:T(8,128)(2,1)S(1)}, u32[]{:S(2)}) copy-start(bf16[2,272,384]{2,1,0:T(8,128)(2,1)S(1)} %collective-permute-done.2.refs_2_) | copy-start | bytes 1253380
  53.9 34.1 %collective-permute-start.3 = (bf16[2,272,384]{2,1,0:T(8,128)(2,1)S(1)}, bf16[2,272,384]{2,1,0:T(8,128)(2,1)S(1)}, u32[]{:S(2)}, u32[]{:S(2)}) collective-permute-start(bf16[2,272,384]{2,1,0:T(8,128)(2,1)S(1)} %collective-permute-done.2.refs_2_), channel_id=1, source_target_pairs={{0,1},{1,0},{2,3},{3,2},{4,5},{5,4},{6,7},{7,6},{8,9},{9,8},{10,11... | collective-permute-start | bytes 1253384 | tf_op jit(solution)/shard_map/ppermute | solution.py:27
  55.8 33.0 %collective-permute-start.5 = (bf16[2,272,384]{2,1,0:T(8,128)(2,1)S(1)}, bf16[2,272,384]{2,1,0:T(8,128)(2,1)S(1)}, u32[]{:S(2)}, u32[]{:S(2)}) collective-permute-start(bf16[2,272,384]{2,1,0:T(8,128)(2,1)S(1)} %collective-permute-done.4.refs_4_), channel_id=1, source_target_pairs={{0,1},{1,0},{2,3},{3,2},{4,5},{5,4},{6,7},{7,6},{8,9},{9,8},{10,11... | collective-permute-start | bytes 1253384 | tf_op jit(solution)/shard_map/ppermute | solution.py:27
  58.2 0.8 copy-start.8
  59.0 30.5 %collective-permute-start.7 = (bf16[2,272,384]{2,1,0:T(8,128)(2,1)S(1)}, bf16[2,272,384]{2,1,0:T(8,128)(2,1)S(1)}, u32[]{:S(2)}, u32[]{:S(2)}) collective-permute-start(bf16[2,272,384]{2,1,0:T(8,128)(2,1)S(1)} %collective-permute-done.6.refs_6_), channel_id=1, source_target_pairs={{0,1},{1,0},{2,3},{3,2},{4,5},{5,4},{6,7},{7,6},{8,9},{9,8},{10,11... | collective-permute-start | bytes 1253384 | tf_op jit(solution)/shard_map/ppermute | solution.py:27
  60.9 0.8 copy-start.10
  87.2 15.1 %copy-start.20 = (f32[128]{0:T(128)S(1)}, f32[128]{0:T(128)}, u32[]{:S(2)}) copy-start(f32[128]{0:T(128)} %param.16) | copy-start | bytes 1540
  87.2 15.1 %copy-start.21 = (f32[128]{0:T(128)S(1)}, f32[128]{0:T(128)}, u32[]{:S(2)}) copy-start(f32[128]{0:T(128)} %param.17) | copy-start | bytes 1540
  87.2 0.8 copy-start.12
  88.0 0.8 copy-start.14
  88.8 0.8 copy-start.16
  89.5 0.7 copy-start.18
  90.3 1.0 copy-start.3
  91.3 1.0 copy-start.7
  92.3 1.0 copy-start.9
  93.3 1.0 copy-start.11
  94.3 1.0 copy-start.13
  95.3 1.0 copy-start.15
  96.3 1.0 copy-start.17
  97.3 1.0 copy-start.19
  102.2 2.1 %copy-start = (bf16[64,80,384]{2,1,0:T(8,128)(2,1)S(1)}, bf16[64,80,384]{2,1,0:T(8,128)(2,1)}, u32[]{:S(2)}) copy-start(bf16[64,80,384]{2,1,0:T(8,128)(2,1)} %all-gather.3.cloned.1.call-done) | copy-start | bytes 11796484
  104.3 42.8 %copy-start.22 = (s32[65]{0:T(128)S(1)}, s32[65]{0:T(128)}, u32[]{:S(2)}) copy-start(s32[65]{0:T(128)} %param.10) | copy-start | bytes 784
  104.3 42.8 %copy-start.1 = (bf16[64,80,384]{2,1,0:T(8,128)(2,1)S(1)}, bf16[64,80,384]{2,1,0:T(8,128)(2,1)}, u32[]{:S(2)}) copy-start(bf16[64,80,384]{2,1,0:T(8,128)(2,1)} %all-gather.3.cloned.1.call-done) | copy-start | bytes 11796484
  144.5 3.8 %collective-permute-start.8 = (bf16[4,512,128]{2,1,0:T(8,128)(2,1)S(1)}, bf16[4,512,128]{2,1,0:T(8,128)(2,1)S(1)}, u32[]{:S(2)}, u32[]{:S(2)}) collective-permute-start(bf16[4,512,128]{2,1,0:T(8,128)(2,1)S(1)} %all_to_all.33.mine_ref), channel_id=1, source_target_pairs={{0,1},{1,0},{2,3},{3,2},{4,5},{5,4},{6,7},{7,6},{8,9},{9,8},{10,11... | collective-permute-start | bytes 1572872 | tf_op jit(solution)/shard_map/ppermute | solution.py:27
Sparse Core Ops, SparseCore 0:
  22.8 78.7 all-gather.2

commit v4 on v3

--- a/solution.py
+++ b/solution.py
@@ -67,18 +67,22 @@
         load.start()
     for load in loads:
         load.wait()
+    out_rows = out_ref[...].astype(jnp.float32)
+    quarter = out_rows.shape[0] // NX
     for dest in range(NX):
-        head = dest % 2
-        for i in range(3):
-            to_ref[dest, 0:48, i * HD : (i + 1) * HD] = qkv_ref[i, :, head * HD : (head + 1) * HD]
-        to_ref[dest, 48:80, :] = out_ref[...]
+        at = slice(dest % 2 * HD, (dest % 2 + 1) * HD)
+        rows = [qkv_ref[i, :, at].astype(jnp.float32) for i in range(3)]
+        rows = jnp.concatenate(rows, axis=1)
+        some = out_rows[dest * quarter : (dest + 1) * quarter]
+        to_ref[dest] = jnp.concatenate([rows, some], axis=0).astype(jnp.bfloat16)
 
 
 def order_kernel(all_ref, to_ref):
     for x in range(NX):
         for z in range(NZ):
             row = (x * NZ + z) * 32
-            to_ref[row : row + 32, :] = all_ref[z, x, 48:80, :]
+            rows = [all_ref[part, z, x].astype(jnp.float32) for part in range(NX)]
+            to_ref[row : row + 32, :] = jnp.concatenate(rows, axis=0).astype(jnp.bfloat16)
 
 
 def norm_kernel(idx_ref, *refs):
@@ -107,12 +111,14 @@
                 h_ref[slot, :, at] = hidden.astype(jnp.bfloat16)
 
 
-def attention_kernel(idx_ref, qg_ref, kg_ref, h_ref, all_ref, o_ref, w_ref):
+def attention_kernel(idx_ref, qg_ref, kg_ref, h_ref, all_ref, o_ref, rest_ref, w_ref):
     odd = lax.rem(idx_ref[0], 2)
     for x in range(NX):
         for z in range(NZ):
             row = (x * NZ + z) * 48
-            w_ref[row : row + 48, :] = all_ref[z, x, 0:48, :]
+            rows = all_ref[z, x]
+            w_ref[row : row + 48, :] = rows[0:48]
+            rest_ref[z, x] = rows[48:56]
     for slot in range(2):
         qkv = jnp.dot(h_ref[slot], w_ref[...], preferred_element_type=jnp.float32)
         q = qkv[:, 0:HD]
@@ -221,7 +227,7 @@
 
     sorted_rows = pl.pallas_call(
         sort_kernel,
-        out_shape=jax.ShapeDtypeStruct((NX, 80, 3 * HD), jnp.bfloat16),
+        out_shape=jax.ShapeDtypeStruct((NX, 56, 3 * HD), jnp.bfloat16),
         in_specs=[pl.BlockSpec(memory_space=pl.ANY)] * 2,
         out_specs=vmem(),
         scratch_shapes=[
@@ -265,17 +271,20 @@
     first = lax.all_to_all(first, "x", 0, 0, tiled=True)
     first = lax.dynamic_index_in_dim(first, start // NZ, 0, keepdims=False)
     first = lax.all_to_all(first.reshape(NZ, rows, width), "z", 0, 0, tiled=True)
-    first = first.astype(jnp.float32)
-    first, hidden = lax.optimization_barrier((first, hidden))
-    attn = pl.pallas_call(
+    weights, first, hidden = lax.optimization_barrier((weights, first, hidden))
+    attn, out_rows = pl.pallas_call(
         attention_kernel,
-        out_shape=jax.ShapeDtypeStruct((2, tokens, HD), jnp.bfloat16),
+        out_shape=(
+            jax.ShapeDtypeStruct((2, tokens, HD), jnp.bfloat16),
+            jax.ShapeDtypeStruct((NZ, NX, 8, width), jnp.bfloat16),
+        ),
         in_specs=[smem()] + [vmem()] * 4,
-        out_specs=vmem(),
+        out_specs=(vmem(), vmem()),
         scratch_shapes=[pltpu.VMEM((48 * count, 3 * HD), jnp.bfloat16)],
         compiler_params=params(),
         name="attention",
     )(idx, q_gain[None], k_gain[None], hidden, weights)
+    out_parts = lax.all_gather(out_rows, "x")
     attn = attn.reshape(2, count, rows, HD).transpose(1, 0, 2, 3).reshape(count, 2 * rows, HD)
     attn = lax.all_to_all(attn, STEP, 0, 0, tiled=True).reshape(count * 2 * rows, HD)
     mine = to_all(attn, "y", NY)
@@ -286,7 +295,7 @@
         out_specs=vmem(),
         compiler_params=params(),
         name="order",
-    )(weights)
+    )(out_parts)
     sums = pl.pallas_call(
         project_kernel,
         out_shape=jax.ShapeDtypeStruct((count, rows, width + 128), jnp.float32),
@@ -299,7 +308,7 @@
         ],
         compiler_params=params(),
         name="project",
-    )(idx, jnp.stack([start, slide]), step_dts, gates, first, mine, swap_core(mine), out_rows)
+    )(idx, jnp.stack([start, slide]), step_dts, gates, first.astype(jnp.float32), mine, swap_core(mine), out_rows)
     back = lax.all_to_all(sums.astype(jnp.float16), STEP, 0, 0, tiled=True).astype(jnp.float32)
     return pl.pallas_call(
         unscale_kernel,

time: 187 us -> 185 us (0.989)
  blocking collectives: 103 us -> 79.5 us
  starting transfers between devices: 27.2 us -> 39.5 us
  waiting for transfers between devices: 7.78 us -> 13.7 us
  local copies, waits for them, and re-layouts: 17.9 us -> 20.3 us
    all_to_all x1 -> x0, blocking collectives: 24.6 us -> none  [per_device(): lax.all_to_all(first.reshape(NZ, rows, width), 'z', 0, 0, tiled=True)]
    all_to_all x0 -> x1, starting transfers between devices: none -> 12.1 us  [per_device(): lax.all_to_all(first.reshape(NZ, rows, width), 'z', 0, 0, tiled=True)]
    all_gather x1, waiting for transfers between devices: 0.02 us -> 6.99 us  [per_device(): lax.all_gather(lax.all_to_all(sorted_rows, 'x', 0, 0, tiled=True), 'z')]
  transfers between devices with their start and end apart: 11 -> 13, of which waited for: 3 -> 3; matrix products, arithmetic and copies ran while one was open for 1% -> 2% of each run, Pallas kernels for 3% -> 3%
where the time goes in v4:
time: 185 us; the launch traced here: 183 us
  blocking collectives  79.5 us (43%)
  starting transfers between devices  39.5 us (21%)
  local copies, waits for them, and re-layouts  20.3 us (11%)
  between operations  15 us (8%)
  waiting for transfers between devices  13.7 us (7%)
  Pallas kernels  13.2 us (7%)
  other arithmetic  2 us (1%)
    all_to_all x1, blocking collectives, per_device(): lax.all_to_all(sums.astype(jnp.float16), STEP, 0, 0, tiled=True)  28 us
    all_to_all x1, blocking collectives, per_device(): lax.all_to_all(attn, STEP, 0, 0, tiled=True).reshape(count * 2 * rows, HD)  25.2 us
    unnamed x46, local copies, waits for them, and re-layouts  18.6 us
    all_to_all x1, blocking collectives, per_device(): lax.all_to_all(sorted_rows, 'x', 0, 0, tiled=True)  14 us
    all_to_all x1, blocking collectives, to_all(): lax.all_to_all(jnp.broadcast_to(value[None], (size,) + value.shape), axis...  12.2 us
    all_to_all x1, starting transfers between devices, per_device(): lax.all_to_all(first.reshape(NZ, rows, width), 'z', 0, 0, tiled=True)  12.1 us
    ppermute x5, starting transfers between devices, swap_core(): return lax.ppermute(value, 'c', [(i, i ^ 1) for i in range(NC)])  10 us
    ppermute x3, starting transfers between devices, shift(): lax.ppermute(value, axis, [(i, (i + by) % size) for i in range(size)])  8.97 us
  transfers between devices with their start and end apart: 13, of which 3 were waited for; matrix products, arithmetic and copies ran while one was open for 2% of the time, Pallas kernels for 3%

profile of v4, /device:TPU:6, one launch (start us, length us, event | category | flops | bytes accessed | tf_op | source)
XLA Modules:
  0.0 183.3 jit_solution(17549187483321983211)
XLA Ops:
  6.5 1.6 sort.1
  8.1 14.0 %all_to_all.30 = bf16[4,56,384]{2,1,0:T(8,128)(2,1)} all-to-all(bf16[4,56,384]{2,1,0:T(8,128)(2,1)} %sort.1), channel_id=1, replica_groups=mesh['x'=4,'z'=16,'y'=4,'c'=2] {'x'}, dimensions={0} | all-to-all | bytes 344064 | tf_op jit(solution)/shard_map/all_to_all | solution.py:241
  22.8 0.7 convert_element_type.26
  23.6 0.2 multiply_cosine_fusion
  23.9 1.0 copy-done.4
  24.8 1.1 copy-done.5
  25.9 0.8 pack.1
  26.7 2.4 %collective-permute-start = (bf16[272,384]{1,0:T(8,128)(2,1)S(1)}, bf16[272,384]{1,0:T(8,128)(2,1)S(1)}, u32[]{:S(2)}, u32[]{:S(2)}) collective-permute-start(bf16[272,384]{1,0:T(8,128)(2,1)S(1)} %get-tuple-element.13), channel_id=1, source_target_pairs={{0,128},{128,0},{256,384},{384,256},{1,129},{129,1},{257,385},{385... | collective-permute-start | bytes 626696 | tf_op jit(solution)/shard_map/ppermute | solution.py:23
  29.1 5.3 %collective-permute-done = bf16[272,384]{1,0:T(8,128)(2,1)S(1)} collective-permute-done((bf16[272,384]{1,0:T(8,128)(2,1)S(1)}, bf16[272,384]{1,0:T(8,128)(2,1)S(1)}, u32[]{:S(2)}, u32[]{:S(2)}) %collective-permute-start) | collective-permute-done | bytes 208928 | tf_op jit(solution)/shard_map/ppermute | solution.py:23
  34.5 1.9 %collective-permute-start.2 = (bf16[2,272,384]{2,1,0:T(8,128)(2,1)S(1)}, bf16[2,272,384]{2,1,0:T(8,128)(2,1)S(1)}, u32[]{:S(2)}, u32[]{:S(2)}) collective-permute-start(bf16[2,272,384]{2,1,0:T(8,128)(2,1)S(1)} %pad_maximum_fusion.refs_0_), channel_id=1, source_target_pairs={{0,2},{2,4},{4,6},{6,0},{1,3},{3,5},{5,7},{7,1},{8,10},{10,12},{12... | collective-permute-start | bytes 1253384 | tf_op jit(solution)/shard_map/ppermute | solution.py:19
  36.4 1.9 %collective-permute-start.4 = (bf16[2,272,384]{2,1,0:T(8,128)(2,1)S(1)}, bf16[2,272,384]{2,1,0:T(8,128)(2,1)S(1)}, u32[]{:S(2)}, u32[]{:S(2)}) collective-permute-start(bf16[2,272,384]{2,1,0:T(8,128)(2,1)S(1)} %pad_maximum_fusion.refs_0_), channel_id=1, source_target_pairs={{0,4},{2,6},{4,0},{6,2},{1,5},{3,7},{5,1},{7,3},{8,12},{10,14},{12... | collective-permute-start | bytes 1253384 | tf_op jit(solution)/shard_map/ppermute | solution.py:19
  38.3 5.1 %collective-permute-start.6 = (bf16[2,272,384]{2,1,0:T(8,128)(2,1)S(1)}, bf16[2,272,384]{2,1,0:T(8,128)(2,1)S(1)}, u32[]{:S(2)}, u32[]{:S(2)}) collective-permute-start(bf16[2,272,384]{2,1,0:T(8,128)(2,1)S(1)} %pad_maximum_fusion.refs_0_), channel_id=1, source_target_pairs={{0,6},{2,0},{4,2},{6,4},{1,7},{3,1},{5,3},{7,5},{8,14},{10,8},{12,... | collective-permute-start | bytes 1253384 | tf_op jit(solution)/shard_map/ppermute | solution.py:19
  43.4 0.7 convert_element_type.28
  44.2 6.0 %all-to-all-start.1 = ((f16[4,64,384]{2,1,0:T(8,128)(2,1)}), f16[4,64,384]{2,1,0:T(8,128)(2,1)}, u32[]{:S(2)}, u32[]{:S(2)}) async-start(f16[4,64,384]{2,1,0:T(8,128)(2,1)} %bitcast.7), calls=%async_computation.1 | async-start | bytes 393216 | tf_op jit(solution)/shard_map/all_to_all | solution.py:271
  50.2 1.9 %collective-permute-start.1 = (bf16[2,272,384]{2,1,0:T(8,128)(2,1)S(1)}, bf16[2,272,384]{2,1,0:T(8,128)(2,1)S(1)}, u32[]{:S(2)}, u32[]{:S(2)}) collective-permute-start(bf16[2,272,384]{2,1,0:T(8,128)(2,1)S(1)} %pad_maximum_fusion.refs_0_), channel_id=1, source_target_pairs={{0,1},{1,0},{2,3},{3,2},{4,5},{5,4},{6,7},{7,6},{8,9},{9,8},{10,11... | collective-permute-start | bytes 1253384 | tf_op jit(solution)/shard_map/ppermute | solution.py:27
  52.1 1.3 collective-permute-done.2.refs_2_
  53.4 1.9 %collective-permute-start.3 = (bf16[2,272,384]{2,1,0:T(8,128)(2,1)S(1)}, bf16[2,272,384]{2,1,0:T(8,128)(2,1)S(1)}, u32[]{:S(2)}, u32[]{:S(2)}) collective-permute-start(bf16[2,272,384]{2,1,0:T(8,128)(2,1)S(1)} %collective-permute-done.2.refs_2_), channel_id=1, source_target_pairs={{0,1},{1,0},{2,3},{3,2},{4,5},{5,4},{6,7},{7,6},{8,9},{9,8},{10,11... | collective-permute-start | bytes 1253384 | tf_op jit(solution)/shard_map/ppermute | solution.py:27
  55.3 0.7 copy-done.6
  56.1 2.4 %collective-permute-start.5 = (bf16[2,272,384]{2,1,0:T(8,128)(2,1)S(1)}, bf16[2,272,384]{2,1,0:T(8,128)(2,1)S(1)}, u32[]{:S(2)}, u32[]{:S(2)}) collective-permute-start(bf16[2,272,384]{2,1,0:T(8,128)(2,1)S(1)} %collective-permute-done.4.refs_4_), channel_id=1, source_target_pairs={{0,1},{1,0},{2,3},{3,2},{4,5},{5,4},{6,7},{7,6},{8,9},{9,8},{10,11... | collective-permute-start | bytes 1253384 | tf_op jit(solution)/shard_map/ppermute | solution.py:27
  58.5 0.7 copy-done.8
  59.2 1.9 %collective-permute-start.7 = (bf16[2,272,384]{2,1,0:T(8,128)(2,1)S(1)}, bf16[2,272,384]{2,1,0:T(8,128)(2,1)S(1)}, u32[]{:S(2)}, u32[]{:S(2)}) collective-permute-start(bf16[2,272,384]{2,1,0:T(8,128)(2,1)S(1)} %collective-permute-done.6.refs_6_), channel_id=1, source_target_pairs={{0,1},{1,0},{2,3},{3,2},{4,5},{5,4},{6,7},{7,6},{8,9},{9,8},{10,11... | collective-permute-start | bytes 1253384 | tf_op jit(solution)/shard_map/ppermute | solution.py:27
  61.2 0.8 copy-done.10
  61.9 0.8 constant_dynamic-slice_fusion
  62.7 0.6 reshape.21
  63.4 12.1 %all-to-all-start.2 = ((f16[16,4,384]{2,1,0:T(4,128)(2,1)}), f16[16,4,384]{2,1,0:T(4,128)(2,1)S(1)}, u32[]{:S(2)}, u32[]{:S(2)}) async-start(f16[16,4,384]{2,1,0:T(4,128)(2,1)} %reshape.21), calls=%async_computation.2 | async-start | bytes 98304 | tf_op jit(solution)/shard_map/all_to_all | solution.py:273
  75.6 0.7 copy-done.12
  76.3 0.8 copy-done.14
  77.1 0.8 copy-done.16
  77.9 0.8 copy-done.18
  78.6 1.0 copy-done.2
  79.7 1.0 copy-done.7
  80.7 1.0 copy-done.9
  81.7 1.0 copy-done.11
  82.7 1.0 copy-done.13
  83.7 1.0 copy-done.15
  84.7 1.0 copy-done.17
  85.7 1.0 copy-done.19
  86.7 3.9 %norm.1.h_ref = bf16[2,256,3072]{2,1,0:T(8,128)(2,1)S(1)} custom-call(s32[6]{0:T(128)S(1)} %stack.35.idx_ref, bf16[2,272,384]{2,1,0:T(8,128)(2,1)S(1)} %copy-done.2, bf16[2,272,384]{2,1,0:T(8,128)(2,1)S(1)} %copy-done.13, bf16[2,272,384]{2,1,0:T(8,128)(2,1)S(1)} %copy-done.7, bf16[2,272,384]{2,1,0:T(8,128)(2,1)S(1)} %copy-done.15, ...), custom_call_target="tpu_custom_call" | custom-call | tf_op jit(solution)/shard_map/norm/pallas_call | solution.py:260
  90.6 7.0 %all-gather.5.cloned.1.call-done = bf16[64,56,384]{2,1,0:T(8,128)(2,1)} async-done(((bf16[4,56,384]{2,1,0:T(8,128)(2,1)}), bf16[64,56,384]{2,1,0:T(8,128)(2,1)}) %all-gather.5.cloned.1.call-update) | async-done | bytes 2752528 | tf_op jit(solution)/shard_map/all_gather | solution.py:241
  97.6 1.8 copy-done
  99.3 4.0 %attention.1 = (bf16[2,256,128]{2,1,0:T(8,128)(2,1)S(1)}, bf16[16,4,8,384]{3,2,1,0:T(8,128)(2,1)}) custom-call(s32[6]{0:T(128)S(1)} %stack.35.idx_ref, f32[1,128]{1,0:T(1,128)S(1)} %bitcast.29, f32[1,128]{1,0:T(1,128)S(1)} %bitcast.30, bf16[2,256,3072]{2,1,0:T(8,128)(2,1)S(1)} %norm.1.h_ref, bf16[16,4,56,384]{3,2,1,0:T(8,128)(2,1)S(1)} %bitcast.24), custom_call_target="tpu_custom_call" | custom-call | tf_op jit(solution)/shard_map/attention/pallas_call | solution.py:275
  103.5 25.2 %all_to_all.31 = bf16[64,8,128]{2,1,0:T(8,128)(2,1)S(1)} all-to-all(bf16[64,8,128]{2,1,0:T(8,128)(2,1)S(1)} %copy.14), channel_id=1, replica_groups=mesh['x'=4,'z'=16,'y'=4,'c'=2] {'x','z'}, dimensions={0} | all-to-all | bytes 262144 | tf_op jit(solution)/shard_map/all_to_all | solution.py:289
  128.8 12.2 %all_to_all.32.mine_ref = bf16[4,512,128]{2,1,0:T(8,128)(2,1)S(1)} all-to-all(bf16[4,512,128]{2,1,0:T(8,128)(2,1)S(1)} %broadcast_in_dim.21), channel_id=1, replica_groups=mesh['x'=4,'z'=16,'y'=4,'c'=2] {'y'}, dimensions={0} | all-to-all | bytes 1048576 | tf_op jit(solution)/shard_map/all_to_all | solution.py:31
  141.0 1.9 %collective-permute-start.8 = (bf16[4,512,128]{2,1,0:T(8,128)(2,1)S(1)}, bf16[4,512,128]{2,1,0:T(8,128)(2,1)S(1)}, u32[]{:S(2)}, u32[]{:S(2)}) collective-permute-start(bf16[4,512,128]{2,1,0:T(8,128)(2,1)S(1)} %all_to_all.32.mine_ref), channel_id=1, source_target_pairs={{0,1},{1,0},{2,3},{3,2},{4,5},{5,4},{6,7},{7,6},{8,9},{9,8},{10,11... | collective-permute-start | bytes 1572872 | tf_op jit(solution)/shard_map/ppermute | solution.py:27
  143.8 1.4 copy-done.3
  145.3 2.1 %project.1 = f32[64,4,512]{2,1,0:T(4,128)S(1)} custom-call(s32[6]{0:T(128)S(1)} %stack.35.idx_ref, s32[2]{0:T(128)S(1)} %pad_add_fusion.win_ref, f32[64]{0:T(128)S(1)} %convert_multiply_fusion.dt_ref, f32[64,384]{1,0:T(8,128)S(1)} %get-tuple-element.12.gate_ref, f32[16,4,384]{2,1,0:T(4,128)S(1)} %convert_element_type.30.lat_ref, ...), custom_call_target="tpu_custom_call" | custom-call | tf_op jit(solution)/shard_map/project/pallas_call | solution.py:299
  147.5 28.0 %all_to_all.33 = f16[64,4,512]{2,1,0:T(4,128)(2,1)S(1)} all-to-all(f16[64,4,512]{2,1,0:T(4,128)(2,1)S(1)} %convert_element_type.31), channel_id=1, replica_groups=mesh['x'=4,'z'=16,'y'=4,'c'=2] {'x','z'}, dimensions={0} | all-to-all | bytes 524288 | tf_op jit(solution)/shard_map/all_to_all | solution.py:312
  175.6 0.8 unscale.1
  (55 shorter events, 1.0 us)
Async XLA Ops:
  6.5 91.0 %all-gather.5.cloned.1.call-start = ((), (), s32[]{:S(2)}) async-start(), calls=%async_computation.6 | async-start | bytes 2924544 | tf_op jit(solution)/shard_map/all_gather | solution.py:241
  23.8 1.0 copy-start.4
  24.8 1.1 copy-start.5
  26.7 7.7 %collective-permute-start = (bf16[272,384]{1,0:T(8,128)(2,1)S(1)}, bf16[272,384]{1,0:T(8,128)(2,1)S(1)}, u32[]{:S(2)}, u32[]{:S(2)}) collective-permute-start(bf16[272,384]{1,0:T(8,128)(2,1)S(1)} %get-tuple-element.13), channel_id=1, source_target_pairs={{0,128},{128,0},{256,384},{384,256},{1,129},{129,1},{257,385},{385... | collective-permute-start | bytes 626696 | tf_op jit(solution)/shard_map/ppermute | solution.py:23
  34.4 42.7 %copy-start.1 = (bf16[2,272,384]{2,1,0:T(8,128)(2,1)}, bf16[2,272,384]{2,1,0:T(8,128)(2,1)S(1)}, u32[]{:S(2)}) copy-start(bf16[2,272,384]{2,1,0:T(8,128)(2,1)S(1)} %pad_maximum_fusion.refs_0_) | copy-start | bytes 1253380
  34.5 18.9 %collective-permute-start.2 = (bf16[2,272,384]{2,1,0:T(8,128)(2,1)S(1)}, bf16[2,272,384]{2,1,0:T(8,128)(2,1)S(1)}, u32[]{:S(2)}, u32[]{:S(2)}) collective-permute-start(bf16[2,272,384]{2,1,0:T(8,128)(2,1)S(1)} %pad_maximum_fusion.refs_0_), channel_id=1, source_target_pairs={{0,2},{2,4},{4,6},{6,0},{1,3},{3,5},{5,7},{7,1},{8,10},{10,12},{12... | collective-permute-start | bytes 1253384 | tf_op jit(solution)/shard_map/ppermute | solution.py:19
  36.4 19.7 %collective-permute-start.4 = (bf16[2,272,384]{2,1,0:T(8,128)(2,1)S(1)}, bf16[2,272,384]{2,1,0:T(8,128)(2,1)S(1)}, u32[]{:S(2)}, u32[]{:S(2)}) collective-permute-start(bf16[2,272,384]{2,1,0:T(8,128)(2,1)S(1)} %pad_maximum_fusion.refs_0_), channel_id=1, source_target_pairs={{0,4},{2,6},{4,0},{6,2},{1,5},{3,7},{5,1},{7,3},{8,12},{10,14},{12... | collective-permute-start | bytes 1253384 | tf_op jit(solution)/shard_map/ppermute | solution.py:19
  38.3 20.9 %collective-permute-start.6 = (bf16[2,272,384]{2,1,0:T(8,128)(2,1)S(1)}, bf16[2,272,384]{2,1,0:T(8,128)(2,1)S(1)}, u32[]{:S(2)}, u32[]{:S(2)}) collective-permute-start(bf16[2,272,384]{2,1,0:T(8,128)(2,1)S(1)} %pad_maximum_fusion.refs_0_), channel_id=1, source_target_pairs={{0,6},{2,0},{4,2},{6,4},{1,7},{3,1},{5,3},{7,5},{8,14},{10,8},{12,... | collective-permute-start | bytes 1253384 | tf_op jit(solution)/shard_map/ppermute | solution.py:19
  44.2 17.8 %all-to-all-start.1 = ((f16[4,64,384]{2,1,0:T(8,128)(2,1)}), f16[4,64,384]{2,1,0:T(8,128)(2,1)}, u32[]{:S(2)}, u32[]{:S(2)}) async-start(f16[4,64,384]{2,1,0:T(8,128)(2,1)} %bitcast.7), calls=%async_computation.1 | async-start | bytes 393216 | tf_op jit(solution)/shard_map/all_to_all | solution.py:271
  50.2 25.4 %collective-permute-start.1 = (bf16[2,272,384]{2,1,0:T(8,128)(2,1)S(1)}, bf16[2,272,384]{2,1,0:T(8,128)(2,1)S(1)}, u32[]{:S(2)}, u32[]{:S(2)}) collective-permute-start(bf16[2,272,384]{2,1,0:T(8,128)(2,1)S(1)} %pad_maximum_fusion.refs_0_), channel_id=1, source_target_pairs={{0,1},{1,0},{2,3},{3,2},{4,5},{5,4},{6,7},{7,6},{8,9},{9,8},{10,11... | collective-permute-start | bytes 1253384 | tf_op jit(solution)/shard_map/ppermute | solution.py:27
  53.4 22.9 %collective-permute-start.3 = (bf16[2,272,384]{2,1,0:T(8,128)(2,1)S(1)}, bf16[2,272,384]{2,1,0:T(8,128)(2,1)S(1)}, u32[]{:S(2)}, u32[]{:S(2)}) collective-permute-start(bf16[2,272,384]{2,1,0:T(8,128)(2,1)S(1)} %collective-permute-done.2.refs_2_), channel_id=1, source_target_pairs={{0,1},{1,0},{2,3},{3,2},{4,5},{5,4},{6,7},{7,6},{8,9},{9,8},{10,11... | collective-permute-start | bytes 1253384 | tf_op jit(solution)/shard_map/ppermute | solution.py:27
  55.3 0.8 copy-start.6
  56.1 21.0 %collective-permute-start.5 = (bf16[2,272,384]{2,1,0:T(8,128)(2,1)S(1)}, bf16[2,272,384]{2,1,0:T(8,128)(2,1)S(1)}, u32[]{:S(2)}, u32[]{:S(2)}) collective-permute-start(bf16[2,272,384]{2,1,0:T(8,128)(2,1)S(1)} %collective-permute-done.4.refs_4_), channel_id=1, source_target_pairs={{0,1},{1,0},{2,3},{3,2},{4,5},{5,4},{6,7},{7,6},{8,9},{9,8},{10,11... | collective-permute-start | bytes 1253384 | tf_op jit(solution)/shard_map/ppermute | solution.py:27
  58.5 0.8 copy-start.8
  59.2 18.6 %collective-permute-start.7 = (bf16[2,272,384]{2,1,0:T(8,128)(2,1)S(1)}, bf16[2,272,384]{2,1,0:T(8,128)(2,1)S(1)}, u32[]{:S(2)}, u32[]{:S(2)}) collective-permute-start(bf16[2,272,384]{2,1,0:T(8,128)(2,1)S(1)} %collective-permute-done.6.refs_6_), channel_id=1, source_target_pairs={{0,1},{1,0},{2,3},{3,2},{4,5},{5,4},{6,7},{7,6},{8,9},{9,8},{10,11... | collective-permute-start | bytes 1253384 | tf_op jit(solution)/shard_map/ppermute | solution.py:27
  61.1 0.8 copy-start.10
  63.4 34.2 %copy-start.20 = (f32[128]{0:T(128)S(1)}, f32[128]{0:T(128)}, u32[]{:S(2)}) copy-start(f32[128]{0:T(128)} %param.16) | copy-start | bytes 1540
  63.4 34.2 %copy-start.21 = (f32[128]{0:T(128)S(1)}, f32[128]{0:T(128)}, u32[]{:S(2)}) copy-start(f32[128]{0:T(128)} %param.17) | copy-start | bytes 1540
  63.4 27.2 %all-to-all-start.2 = ((f16[16,4,384]{2,1,0:T(4,128)(2,1)}), f16[16,4,384]{2,1,0:T(4,128)(2,1)S(1)}, u32[]{:S(2)}, u32[]{:S(2)}) async-start(f16[16,4,384]{2,1,0:T(4,128)(2,1)} %reshape.21), calls=%async_computation.2 | async-start | bytes 98304 | tf_op jit(solution)/shard_map/all_to_all | solution.py:273
  75.5 68.2 %all-gather.7.cloned.1.call-start = ((), (), s32[]{:S(2)}) async-start(), calls=%async_computation.7 | async-start | bytes 1966080 | tf_op jit(solution)/shard_map/all_gather | solution.py:287
  75.6 0.8 copy-start.12
  76.3 0.8 copy-start.14
  77.1 0.8 copy-start.16
  77.9 0.8 copy-start.18
  78.6 1.0 copy-start.2
  79.6 1.0 copy-start.7
  80.7 1.0 copy-start.9
  81.7 1.0 copy-start.11
  82.7 1.0 copy-start.13
  83.7 1.0 copy-start.15
  84.7 1.0 copy-start.17
  85.7 1.0 copy-start.19
  97.6 1.8 copy-start
  103.3 40.3 %copy-start.22 = (s32[65]{0:T(128)S(1)}, s32[65]{0:T(128)}, u32[]{:S(2)}) copy-start(s32[65]{0:T(128)} %param.10) | copy-start | bytes 784
  141.0 4.3 %collective-permute-start.8 = (bf16[4,512,128]{2,1,0:T(8,128)(2,1)S(1)}, bf16[4,512,128]{2,1,0:T(8,128)(2,1)S(1)}, u32[]{:S(2)}, u32[]{:S(2)}) collective-permute-start(bf16[4,512,128]{2,1,0:T(8,128)(2,1)S(1)} %all_to_all.32.mine_ref), channel_id=1, source_target_pairs={{0,1},{1,0},{2,3},{3,2},{4,5},{5,4},{6,7},{7,6},{8,9},{9,8},{10,11... | collective-permute-start | bytes 1572872 | tf_op jit(solution)/shard_map/ppermute | solution.py:27
  143.8 1.4 copy-start.3
Sparse Core Ops, SparseCore 0:
  22.3 75.1 all-gather.4
  103.5 30.8 all-gather.6

commit v5 on v4

--- a/solution.py
+++ b/solution.py
@@ -296,6 +296,7 @@
         compiler_params=params(),
         name="order",
     )(out_parts)
+    mine, out_rows = lax.optimization_barrier((mine, out_rows))
     sums = pl.pallas_call(
         project_kernel,
         out_shape=jax.ShapeDtypeStruct((count, rows, width + 128), jnp.float32),

time: 185 us -> 187 us (1.011)
  blocking collectives: 79.5 us -> 69.2 us
  waiting for transfers between devices: 13.7 us -> 21.3 us
  starting transfers between devices: 39.5 us -> 43.6 us
    all_to_all x1 -> x0, blocking collectives: 12.2 us -> none  [to_all(): lax.all_to_all(jnp.broadcast_to(value[None], (size,) + value.shape), axis...]
    all_to_all x0 -> x1, waiting for transfers between devices: none -> 6.17 us  [to_all(): lax.all_to_all(jnp.broadcast_to(value[None], (size,) + value.shape), axis...]
    all_to_all x0 -> x1, starting transfers between devices: none -> 4.08 us  [to_all(): lax.all_to_all(jnp.broadcast_to(value[None], (size,) + value.shape), axis...]
    all_to_all x1, blocking collectives: 28 us -> 29.9 us  [per_device(): lax.all_to_all(sums.astype(jnp.float16), STEP, 0, 0, tiled=True)]
  transfers between devices with their start and end apart: 13 -> 14, of which waited for: 3 -> 6; matrix products, arithmetic and copies ran while one was open for 2% -> 2% of each run, Pallas kernels for 3% -> 3%
where the time goes in v5:
time: 187 us; the launch traced here: 185 us
  blocking collectives  69.2 us (37%)
  starting transfers between devices  43.6 us (23%)
  waiting for transfers between devices  21.3 us (11%)
  local copies, waits for them, and re-layouts  21.2 us (11%)
  between operations  15 us (8%)
  Pallas kernels  13.1 us (7%)
  other arithmetic  2 us (1%)
    all_to_all x1, blocking collectives, per_device(): lax.all_to_all(sums.astype(jnp.float16), STEP, 0, 0, tiled=True)  29.9 us
    all_to_all x1, blocking collectives, per_device(): lax.all_to_all(attn, STEP, 0, 0, tiled=True).reshape(count * 2 * rows, HD)  25.3 us
    unnamed x46, local copies, waits for them, and re-layouts  18.7 us
    all_to_all x1, blocking collectives, per_device(): lax.all_to_all(sorted_rows, 'x', 0, 0, tiled=True)  14 us
    all_to_all x1, starting transfers between devices, per_device(): lax.all_to_all(first.reshape(NZ, rows, width), 'z', 0, 0, tiled=True)  12.1 us
    ppermute x5, starting transfers between devices, swap_core(): return lax.ppermute(value, 'c', [(i, i ^ 1) for i in range(NC)])  10 us
    ppermute x3, starting transfers between devices, shift(): lax.ppermute(value, axis, [(i, (i + by) % size) for i in range(size)])  8.97 us
    all_gather x1, waiting for transfers between devices, per_device(): lax.all_gather(lax.all_to_all(sorted_rows, 'x', 0, 0, tiled=True), 'z')  7.07 us
  transfers between devices with their start and end apart: 14, of which 6 were waited for; matrix products, arithmetic and copies ran while one was open for 2% of the time, Pallas kernels for 3%

profile of v5, /device:TPU:6, one launch (start us, length us, event | category | flops | bytes accessed | tf_op | source)
XLA Modules:
  0.0 185.4 jit_solution(11542582854174526896)
XLA Ops:
  6.5 1.6 sort.1
  8.1 14.0 %all_to_all.30 = bf16[4,56,384]{2,1,0:T(8,128)(2,1)} all-to-all(bf16[4,56,384]{2,1,0:T(8,128)(2,1)} %sort.1), channel_id=1, replica_groups=mesh['x'=4,'z'=16,'y'=4,'c'=2] {'x'}, dimensions={0} | all-to-all | bytes 344064 | tf_op jit(solution)/shard_map/all_to_all | solution.py:241
  23.8 1.0 copy-done.4
  24.8 1.1 copy-done.5
  25.9 0.8 pack.1
  26.7 2.4 %collective-permute-start = (bf16[272,384]{1,0:T(8,128)(2,1)S(1)}, bf16[272,384]{1,0:T(8,128)(2,1)S(1)}, u32[]{:S(2)}, u32[]{:S(2)}) collective-permute-start(bf16[272,384]{1,0:T(8,128)(2,1)S(1)} %get-tuple-element.15), channel_id=1, source_target_pairs={{0,128},{128,0},{256,384},{384,256},{1,129},{129,1},{257,385},{385... | collective-permute-start | bytes 626696 | tf_op jit(solution)/shard_map/ppermute | solution.py:23
  29.1 5.3 %collective-permute-done = bf16[272,384]{1,0:T(8,128)(2,1)S(1)} collective-permute-done((bf16[272,384]{1,0:T(8,128)(2,1)S(1)}, bf16[272,384]{1,0:T(8,128)(2,1)S(1)}, u32[]{:S(2)}, u32[]{:S(2)}) %collective-permute-start) | collective-permute-done | bytes 208928 | tf_op jit(solution)/shard_map/ppermute | solution.py:23
  34.4 1.9 %collective-permute-start.2 = (bf16[2,272,384]{2,1,0:T(8,128)(2,1)S(1)}, bf16[2,272,384]{2,1,0:T(8,128)(2,1)S(1)}, u32[]{:S(2)}, u32[]{:S(2)}) collective-permute-start(bf16[2,272,384]{2,1,0:T(8,128)(2,1)S(1)} %pad_maximum_fusion.refs_0_), channel_id=1, source_target_pairs={{0,2},{2,4},{4,6},{6,0},{1,3},{3,5},{5,7},{7,1},{8,10},{10,12},{12... | collective-permute-start | bytes 1253384 | tf_op jit(solution)/shard_map/ppermute | solution.py:19
  36.4 1.9 %collective-permute-start.4 = (bf16[2,272,384]{2,1,0:T(8,128)(2,1)S(1)}, bf16[2,272,384]{2,1,0:T(8,128)(2,1)S(1)}, u32[]{:S(2)}, u32[]{:S(2)}) collective-permute-start(bf16[2,272,384]{2,1,0:T(8,128)(2,1)S(1)} %pad_maximum_fusion.refs_0_), channel_id=1, source_target_pairs={{0,4},{2,6},{4,0},{6,2},{1,5},{3,7},{5,1},{7,3},{8,12},{10,14},{12... | collective-permute-start | bytes 1253384 | tf_op jit(solution)/shard_map/ppermute | solution.py:19
  38.3 5.1 %collective-permute-start.6 = (bf16[2,272,384]{2,1,0:T(8,128)(2,1)S(1)}, bf16[2,272,384]{2,1,0:T(8,128)(2,1)S(1)}, u32[]{:S(2)}, u32[]{:S(2)}) collective-permute-start(bf16[2,272,384]{2,1,0:T(8,128)(2,1)S(1)} %pad_maximum_fusion.refs_0_), channel_id=1, source_target_pairs={{0,6},{2,0},{4,2},{6,4},{1,7},{3,1},{5,3},{7,5},{8,14},{10,8},{12,... | collective-permute-start | bytes 1253384 | tf_op jit(solution)/shard_map/ppermute | solution.py:19
  43.4 0.7 convert_element_type.28
  44.1 6.0 %all-to-all-start.1 = ((f16[4,64,384]{2,1,0:T(8,128)(2,1)}), f16[4,64,384]{2,1,0:T(8,128)(2,1)}, u32[]{:S(2)}, u32[]{:S(2)}) async-start(f16[4,64,384]{2,1,0:T(8,128)(2,1)} %bitcast.7), calls=%async_computation.1 | async-start | bytes 393216 | tf_op jit(solution)/shard_map/all_to_all | solution.py:271
  50.2 1.9 %collective-permute-start.1 = (bf16[2,272,384]{2,1,0:T(8,128)(2,1)S(1)}, bf16[2,272,384]{2,1,0:T(8,128)(2,1)S(1)}, u32[]{:S(2)}, u32[]{:S(2)}) collective-permute-start(bf16[2,272,384]{2,1,0:T(8,128)(2,1)S(1)} %pad_maximum_fusion.refs_0_), channel_id=1, source_target_pairs={{0,1},{1,0},{2,3},{3,2},{4,5},{5,4},{6,7},{7,6},{8,9},{9,8},{10,11... | collective-permute-start | bytes 1253384 | tf_op jit(solution)/shard_map/ppermute | solution.py:27
  52.1 1.3 collective-permute-done.2.refs_2_
  53.4 1.9 %collective-permute-start.3 = (bf16[2,272,384]{2,1,0:T(8,128)(2,1)S(1)}, bf16[2,272,384]{2,1,0:T(8,128)(2,1)S(1)}, u32[]{:S(2)}, u32[]{:S(2)}) collective-permute-start(bf16[2,272,384]{2,1,0:T(8,128)(2,1)S(1)} %collective-permute-done.2.refs_2_), channel_id=1, source_target_pairs={{0,1},{1,0},{2,3},{3,2},{4,5},{5,4},{6,7},{7,6},{8,9},{9,8},{10,11... | collective-permute-start | bytes 1253384 | tf_op jit(solution)/shard_map/ppermute | solution.py:27
  55.3 0.7 copy-done.6
  56.1 2.4 %collective-permute-start.5 = (bf16[2,272,384]{2,1,0:T(8,128)(2,1)S(1)}, bf16[2,272,384]{2,1,0:T(8,128)(2,1)S(1)}, u32[]{:S(2)}, u32[]{:S(2)}) collective-permute-start(bf16[2,272,384]{2,1,0:T(8,128)(2,1)S(1)} %collective-permute-done.4.refs_4_), channel_id=1, source_target_pairs={{0,1},{1,0},{2,3},{3,2},{4,5},{5,4},{6,7},{7,6},{8,9},{9,8},{10,11... | collective-permute-start | bytes 1253384 | tf_op jit(solution)/shard_map/ppermute | solution.py:27
  58.5 0.8 copy-done.8
  59.3 1.9 %collective-permute-start.7 = (bf16[2,272,384]{2,1,0:T(8,128)(2,1)S(1)}, bf16[2,272,384]{2,1,0:T(8,128)(2,1)S(1)}, u32[]{:S(2)}, u32[]{:S(2)}) collective-permute-start(bf16[2,272,384]{2,1,0:T(8,128)(2,1)S(1)} %collective-permute-done.6.refs_6_), channel_id=1, source_target_pairs={{0,1},{1,0},{2,3},{3,2},{4,5},{5,4},{6,7},{7,6},{8,9},{9,8},{10,11... | collective-permute-start | bytes 1253384 | tf_op jit(solution)/shard_map/ppermute | solution.py:27
  61.2 0.8 copy-done.10
  62.0 0.8 constant_dynamic-slice_fusion
  63.4 12.1 %all-to-all-start.2 = ((f16[16,4,384]{2,1,0:T(4,128)(2,1)}), f16[16,4,384]{2,1,0:T(4,128)(2,1)S(1)}, u32[]{:S(2)}, u32[]{:S(2)}) async-start(f16[16,4,384]{2,1,0:T(4,128)(2,1)} %reshape.21), calls=%async_computation.2 | async-start | bytes 98304 | tf_op jit(solution)/shard_map/all_to_all | solution.py:273
  75.6 0.8 copy-done.12
  76.4 0.8 copy-done.14
  77.2 0.8 copy-done.16
  77.9 0.8 copy-done.18
  78.7 1.0 copy-done.2
  79.7 1.0 copy-done.7
  80.7 1.0 copy-done.9
  81.7 1.0 copy-done.11
  82.7 1.0 copy-done.13
  83.7 1.0 copy-done.15
  84.7 1.0 copy-done.17
  85.8 1.0 copy-done.19
  86.8 3.9 %norm.1.h_ref = bf16[2,256,3072]{2,1,0:T(8,128)(2,1)S(1)} custom-call(s32[6]{0:T(128)S(1)} %stack.35.idx_ref, bf16[2,272,384]{2,1,0:T(8,128)(2,1)S(1)} %copy-done.2, bf16[2,272,384]{2,1,0:T(8,128)(2,1)S(1)} %copy-done.13, bf16[2,272,384]{2,1,0:T(8,128)(2,1)S(1)} %copy-done.7, bf16[2,272,384]{2,1,0:T(8,128)(2,1)S(1)} %copy-done.15, ...), custom_call_target="tpu_custom_call" | custom-call | tf_op jit(solution)/shard_map/norm/pallas_call | solution.py:260
  90.6 7.1 %all-gather.5.cloned.1.call-done = bf16[64,56,384]{2,1,0:T(8,128)(2,1)} async-done(((bf16[4,56,384]{2,1,0:T(8,128)(2,1)}), bf16[64,56,384]{2,1,0:T(8,128)(2,1)}) %all-gather.5.cloned.1.call-update) | async-done | bytes 2752528 | tf_op jit(solution)/shard_map/all_gather | solution.py:241
  97.7 1.8 copy-done
  99.5 4.0 %attention.1 = (bf16[2,256,128]{2,1,0:T(8,128)(2,1)S(1)}, bf16[16,4,8,384]{3,2,1,0:T(8,128)(2,1)}) custom-call(s32[6]{0:T(128)S(1)} %stack.35.idx_ref, f32[1,128]{1,0:T(1,128)S(1)} %bitcast.29, f32[1,128]{1,0:T(1,128)S(1)} %bitcast.30, bf16[2,256,3072]{2,1,0:T(8,128)(2,1)S(1)} %norm.1.h_ref, bf16[16,4,56,384]{3,2,1,0:T(8,128)(2,1)S(1)} %bitcast.24), custom_call_target="tpu_custom_call" | custom-call | tf_op jit(solution)/shard_map/attention/pallas_call | solution.py:275
  103.6 25.3 %all_to_all.31 = bf16[64,8,128]{2,1,0:T(8,128)(2,1)S(1)} all-to-all(bf16[64,8,128]{2,1,0:T(8,128)(2,1)S(1)} %copy.14), channel_id=1, replica_groups=mesh['x'=4,'z'=16,'y'=4,'c'=2] {'x','z'}, dimensions={0} | all-to-all | bytes 262144 | tf_op jit(solution)/shard_map/all_to_all | solution.py:289
  129.0 0.9 broadcast_in_dim.21
  129.8 4.1 %all-to-all-start.4 = ((bf16[4,512,128]{2,1,0:T(8,128)(2,1)}), bf16[4,512,128]{2,1,0:T(8,128)(2,1)S(1)}, u32[]{:S(2)}, u32[]{:S(2)}) async-start(bf16[4,512,128]{2,1,0:T(8,128)(2,1)} %broadcast_in_dim.21), calls=%async_computation.4 | async-start | bytes 1048576 | tf_op jit(solution)/shard_map/all_to_all | solution.py:31
  134.3 1.4 copy-done.3
  135.8 6.2 %all-to-all-done.4.mine_ref = bf16[4,512,128]{2,1,0:T(8,128)(2,1)S(1)} async-done(((bf16[4,512,128]{2,1,0:T(8,128)(2,1)}), bf16[4,512,128]{2,1,0:T(8,128)(2,1)S(1)}, u32[]{:S(2)}, u32[]{:S(2)}) %all-to-all-start.4) | async-done | bytes 524320 | tf_op jit(solution)/shard_map/all_to_all | solution.py:31
  142.0 1.9 %collective-permute-start.8 = (bf16[4,512,128]{2,1,0:T(8,128)(2,1)S(1)}, bf16[4,512,128]{2,1,0:T(8,128)(2,1)S(1)}, u32[]{:S(2)}, u32[]{:S(2)}) collective-permute-start(bf16[4,512,128]{2,1,0:T(8,128)(2,1)S(1)} %all-to-all-done.4.mine_ref), channel_id=1, source_target_pairs={{0,1},{1,0},{2,3},{3,2},{4,5},{5,4},{6,7},{7,6},{8,9},{9,8},{10,11... | collective-permute-start | bytes 1572872 | tf_op jit(solution)/shard_map/ppermute | solution.py:27
  144.7 1.1 collective-permute-done.8.other_ref
  145.8 1.9 %project.1 = f32[64,4,512]{2,1,0:T(4,128)S(1)} custom-call(s32[6]{0:T(128)S(1)} %stack.35.idx_ref, s32[2]{0:T(128)S(1)} %pad_add_fusion.win_ref, f32[64]{0:T(128)S(1)} %convert_multiply_fusion.dt_ref, f32[64,384]{1,0:T(8,128)S(1)} %get-tuple-element.14.gate_ref, f32[16,4,384]{2,1,0:T(4,128)S(1)} %convert_element_type.30.lat_ref, ...), custom_call_target="tpu_custom_call" | custom-call | tf_op jit(solution)/shard_map/project/pallas_call | solution.py:300
  147.8 29.9 %all_to_all.32 = f16[64,4,512]{2,1,0:T(4,128)(2,1)S(1)} all-to-all(f16[64,4,512]{2,1,0:T(4,128)(2,1)S(1)} %convert_element_type.31), channel_id=1, replica_groups=mesh['x'=4,'z'=16,'y'=4,'c'=2] {'x','z'}, dimensions={0} | all-to-all | bytes 524288 | tf_op jit(solution)/shard_map/all_to_all | solution.py:313
  177.8 0.8 unscale.1
  (56 shorter events, 2.8 us)
Async XLA Ops:
  6.5 91.2 %all-gather.5.cloned.1.call-start = ((), (), s32[]{:S(2)}) async-start(), calls=%async_computation.6 | async-start | bytes 2924544 | tf_op jit(solution)/shard_map/all_gather | solution.py:241
  23.8 1.0 copy-start.4
  24.8 1.1 copy-start.5
  26.7 7.7 %collective-permute-start = (bf16[272,384]{1,0:T(8,128)(2,1)S(1)}, bf16[272,384]{1,0:T(8,128)(2,1)S(1)}, u32[]{:S(2)}, u32[]{:S(2)}) collective-permute-start(bf16[272,384]{1,0:T(8,128)(2,1)S(1)} %get-tuple-element.15), channel_id=1, source_target_pairs={{0,128},{128,0},{256,384},{384,256},{1,129},{129,1},{257,385},{385... | collective-permute-start | bytes 626696 | tf_op jit(solution)/shard_map/ppermute | solution.py:23
  34.4 42.7 %copy-start.1 = (bf16[2,272,384]{2,1,0:T(8,128)(2,1)}, bf16[2,272,384]{2,1,0:T(8,128)(2,1)S(1)}, u32[]{:S(2)}) copy-start(bf16[2,272,384]{2,1,0:T(8,128)(2,1)S(1)} %pad_maximum_fusion.refs_0_) | copy-start | bytes 1253380
  34.4 18.9 %collective-permute-start.2 = (bf16[2,272,384]{2,1,0:T(8,128)(2,1)S(1)}, bf16[2,272,384]{2,1,0:T(8,128)(2,1)S(1)}, u32[]{:S(2)}, u32[]{:S(2)}) collective-permute-start(bf16[2,272,384]{2,1,0:T(8,128)(2,1)S(1)} %pad_maximum_fusion.refs_0_), channel_id=1, source_target_pairs={{0,2},{2,4},{4,6},{6,0},{1,3},{3,5},{5,7},{7,1},{8,10},{10,12},{12... | collective-permute-start | bytes 1253384 | tf_op jit(solution)/shard_map/ppermute | solution.py:19
  36.4 19.7 %collective-permute-start.4 = (bf16[2,272,384]{2,1,0:T(8,128)(2,1)S(1)}, bf16[2,272,384]{2,1,0:T(8,128)(2,1)S(1)}, u32[]{:S(2)}, u32[]{:S(2)}) collective-permute-start(bf16[2,272,384]{2,1,0:T(8,128)(2,1)S(1)} %pad_maximum_fusion.refs_0_), channel_id=1, source_target_pairs={{0,4},{2,6},{4,0},{6,2},{1,5},{3,7},{5,1},{7,3},{8,12},{10,14},{12... | collective-permute-start | bytes 1253384 | tf_op jit(solution)/shard_map/ppermute | solution.py:19
  38.3 21.0 %collective-permute-start.6 = (bf16[2,272,384]{2,1,0:T(8,128)(2,1)S(1)}, bf16[2,272,384]{2,1,0:T(8,128)(2,1)S(1)}, u32[]{:S(2)}, u32[]{:S(2)}) collective-permute-start(bf16[2,272,384]{2,1,0:T(8,128)(2,1)S(1)} %pad_maximum_fusion.refs_0_), channel_id=1, source_target_pairs={{0,6},{2,0},{4,2},{6,4},{1,7},{3,1},{5,3},{7,5},{8,14},{10,8},{12,... | collective-permute-start | bytes 1253384 | tf_op jit(solution)/shard_map/ppermute | solution.py:19
  44.1 17.8 %all-to-all-start.1 = ((f16[4,64,384]{2,1,0:T(8,128)(2,1)}), f16[4,64,384]{2,1,0:T(8,128)(2,1)}, u32[]{:S(2)}, u32[]{:S(2)}) async-start(f16[4,64,384]{2,1,0:T(8,128)(2,1)} %bitcast.7), calls=%async_computation.1 | async-start | bytes 393216 | tf_op jit(solution)/shard_map/all_to_all | solution.py:271
  50.2 25.4 %collective-permute-start.1 = (bf16[2,272,384]{2,1,0:T(8,128)(2,1)S(1)}, bf16[2,272,384]{2,1,0:T(8,128)(2,1)S(1)}, u32[]{:S(2)}, u32[]{:S(2)}) collective-permute-start(bf16[2,272,384]{2,1,0:T(8,128)(2,1)S(1)} %pad_maximum_fusion.refs_0_), channel_id=1, source_target_pairs={{0,1},{1,0},{2,3},{3,2},{4,5},{5,4},{6,7},{7,6},{8,9},{9,8},{10,11... | collective-permute-start | bytes 1253384 | tf_op jit(solution)/shard_map/ppermute | solution.py:27
  53.4 23.0 %collective-permute-start.3 = (bf16[2,272,384]{2,1,0:T(8,128)(2,1)S(1)}, bf16[2,272,384]{2,1,0:T(8,128)(2,1)S(1)}, u32[]{:S(2)}, u32[]{:S(2)}) collective-permute-start(bf16[2,272,384]{2,1,0:T(8,128)(2,1)S(1)} %collective-permute-done.2.refs_2_), channel_id=1, source_target_pairs={{0,1},{1,0},{2,3},{3,2},{4,5},{5,4},{6,7},{7,6},{8,9},{9,8},{10,11... | collective-permute-start | bytes 1253384 | tf_op jit(solution)/shard_map/ppermute | solution.py:27
  55.3 0.8 copy-start.6
  56.1 21.1 %collective-permute-start.5 = (bf16[2,272,384]{2,1,0:T(8,128)(2,1)S(1)}, bf16[2,272,384]{2,1,0:T(8,128)(2,1)S(1)}, u32[]{:S(2)}, u32[]{:S(2)}) collective-permute-start(bf16[2,272,384]{2,1,0:T(8,128)(2,1)S(1)} %collective-permute-done.4.refs_4_), channel_id=1, source_target_pairs={{0,1},{1,0},{2,3},{3,2},{4,5},{5,4},{6,7},{7,6},{8,9},{9,8},{10,11... | collective-permute-start | bytes 1253384 | tf_op jit(solution)/shard_map/ppermute | solution.py:27
  58.5 0.8 copy-start.8
  59.3 18.7 %collective-permute-start.7 = (bf16[2,272,384]{2,1,0:T(8,128)(2,1)S(1)}, bf16[2,272,384]{2,1,0:T(8,128)(2,1)S(1)}, u32[]{:S(2)}, u32[]{:S(2)}) collective-permute-start(bf16[2,272,384]{2,1,0:T(8,128)(2,1)S(1)} %collective-permute-done.6.refs_6_), channel_id=1, source_target_pairs={{0,1},{1,0},{2,3},{3,2},{4,5},{5,4},{6,7},{7,6},{8,9},{9,8},{10,11... | collective-permute-start | bytes 1253384 | tf_op jit(solution)/shard_map/ppermute | solution.py:27
  61.2 0.8 copy-start.10
  63.4 34.3 %copy-start.20 = (f32[128]{0:T(128)S(1)}, f32[128]{0:T(128)}, u32[]{:S(2)}) copy-start(f32[128]{0:T(128)} %param.16) | copy-start | bytes 1540
  63.4 34.3 %copy-start.21 = (f32[128]{0:T(128)S(1)}, f32[128]{0:T(128)}, u32[]{:S(2)}) copy-start(f32[128]{0:T(128)} %param.17) | copy-start | bytes 1540
  63.4 27.2 %all-to-all-start.2 = ((f16[16,4,384]{2,1,0:T(4,128)(2,1)}), f16[16,4,384]{2,1,0:T(4,128)(2,1)S(1)}, u32[]{:S(2)}, u32[]{:S(2)}) async-start(f16[16,4,384]{2,1,0:T(4,128)(2,1)} %reshape.21), calls=%async_computation.2 | async-start | bytes 98304 | tf_op jit(solution)/shard_map/all_to_all | solution.py:273
  75.5 58.7 %all-gather.7.cloned.1.call-start = ((), (), s32[]{:S(2)}) async-start(), calls=%async_computation.7 | async-start | bytes 1966080 | tf_op jit(solution)/shard_map/all_gather | solution.py:287
  75.6 0.8 copy-start.12
  76.4 0.8 copy-start.14
  77.2 0.8 copy-start.16
  77.9 0.8 copy-start.18
  78.7 1.0 copy-start.2
  79.7 1.0 copy-start.7
  80.7 1.0 copy-start.9
  81.7 1.0 copy-start.11
  82.7 1.0 copy-start.13
  83.7 1.0 copy-start.15
  84.7 1.0 copy-start.17
  85.8 1.0 copy-start.19
  97.7 1.8 copy-start
  103.5 41.1 %copy-start.22 = (s32[65]{0:T(128)S(1)}, s32[65]{0:T(128)}, u32[]{:S(2)}) copy-start(s32[65]{0:T(128)} %param.10) | copy-start | bytes 784
  129.8 12.2 %all-to-all-start.4 = ((bf16[4,512,128]{2,1,0:T(8,128)(2,1)}), bf16[4,512,128]{2,1,0:T(8,128)(2,1)S(1)}, u32[]{:S(2)}, u32[]{:S(2)}) async-start(bf16[4,512,128]{2,1,0:T(8,128)(2,1)} %broadcast_in_dim.21), calls=%async_computation.4 | async-start | bytes 1048576 | tf_op jit(solution)/shard_map/all_to_all | solution.py:31
  134.3 1.4 copy-start.3
  142.0 3.8 %collective-permute-start.8 = (bf16[4,512,128]{2,1,0:T(8,128)(2,1)S(1)}, bf16[4,512,128]{2,1,0:T(8,128)(2,1)S(1)}, u32[]{:S(2)}, u32[]{:S(2)}) collective-permute-start(bf16[4,512,128]{2,1,0:T(8,128)(2,1)S(1)} %all-to-all-done.4.mine_ref), channel_id=1, source_target_pairs={{0,1},{1,0},{2,3},{3,2},{4,5},{5,4},{6,7},{7,6},{8,9},{9,8},{10,11... | collective-permute-start | bytes 1572872 | tf_op jit(solution)/shard_map/ppermute | solution.py:27
Sparse Core Ops, SparseCore 0:
  22.3 75.3 all-gather.4
  103.6 30.6 all-gather.6

commit v6 on v4

--- a/solution.py
+++ b/solution.py
@@ -176,19 +176,28 @@
     largest = jnp.max(jnp.max(jnp.abs(runs), axis=0), keepdims=True)
     power = jnp.clip(jnp.ceil(jnp.log2(largest)), -100.0, 100.0) - 14.0
     width = runs.shape[2]
-    out_ref[:, :, 0:width] = runs * jnp.exp2(-power)[None]
-    rest = out_ref.shape[2] - width
-    out_ref[:, :, width:] = jnp.broadcast_to(power[None], runs.shape[:2] + (rest,))
+    runs = runs * jnp.exp2(-power)[None]
+    half = runs.shape[1] // 2
+    for token in range(runs.shape[1]):
+        row, at = token // half, token % half * width
+        out_ref[:, row : row + 1, at : at + width] = runs[:, token : token + 1, :]
+    at = half * width
+    out_ref[:, :, at:] = jnp.broadcast_to(power[None], (out_ref.shape[0], 2, 128))
 
 
 def unscale_kernel(in_ref, out_ref):
-    count, rows = in_ref.shape[0], in_ref.shape[1]
-    width = out_ref.shape[1]
-    scale = jnp.exp2(in_ref[:, :, width : width + 128])
-    for g in range(width // 128):
-        values = in_ref[:, :, g * 128 : (g + 1) * 128] * scale
-        for i in range(count):
-            out_ref[i * rows : (i + 1) * rows, g * 128 : (g + 1) * 128] = values[i]
+    count, width = in_ref.shape[0], out_ref.shape[1]
+    rows = out_ref.shape[0] // count
+    half = rows // 2
+    scale = jnp.exp2(in_ref[:, :, half * width :])
+    for token in range(rows):
+        row, at = token // half, token % half * width
+        for g in range(width // 128):
+            part = in_ref[:, row : row + 1, at + g * 128 : at + (g + 1) * 128]
+            values = part * scale[:, row : row + 1, :]
+            for i in range(count):
+                to = i * rows + token
+                out_ref[to : to + 1, g * 128 : (g + 1) * 128] = values[i]
 
 
 def vmem():
@@ -298,7 +307,7 @@
     )(out_parts)
     sums = pl.pallas_call(
         project_kernel,
-        out_shape=jax.ShapeDtypeStruct((count, rows, width + 128), jnp.float32),
+        out_shape=jax.ShapeDtypeStruct((count, 2, rows // 2 * width + 128), jnp.float32),
         in_specs=[smem()] * 3 + [vmem()] * 5,
         out_specs=vmem(),
         scratch_shapes=[

time: 185 us -> 184 us (level)
  no operation moved by 1% of the time
where the time goes in v6:
time: 184 us; the launch traced here: 182 us
  blocking collectives  78.1 us (42%)
  starting transfers between devices  39.5 us (21%)
  local copies, waits for them, and re-layouts  20.3 us (11%)
  between operations  15 us (8%)
  waiting for transfers between devices  13.7 us (7%)
  Pallas kernels  13.4 us (7%)
  other arithmetic  2.14 us (1%)
    all_to_all x1, blocking collectives, per_device(): lax.all_to_all(sums.astype(jnp.float16), STEP, 0, 0, tiled=True)  26.6 us
    all_to_all x1, blocking collectives, per_device(): lax.all_to_all(attn, STEP, 0, 0, tiled=True).reshape(count * 2 * rows, HD)  25.2 us
    unnamed x46, local copies, waits for them, and re-layouts  18.6 us
    all_to_all x1, blocking collectives, per_device(): lax.all_to_all(sorted_rows, 'x', 0, 0, tiled=True)  14 us
    all_to_all x1, blocking collectives, to_all(): lax.all_to_all(jnp.broadcast_to(value[None], (size,) + value.shape), axis...  12.2 us
    all_to_all x1, starting transfers between devices, per_device(): lax.all_to_all(first.reshape(NZ, rows, width), 'z', 0, 0, tiled=True)  12.1 us
    ppermute x5, starting transfers between devices, swap_core(): return lax.ppermute(value, 'c', [(i, i ^ 1) for i in range(NC)])  10 us
    ppermute x3, starting transfers between devices, shift(): lax.ppermute(value, axis, [(i, (i + by) % size) for i in range(size)])  8.97 us
  transfers between devices with their start and end apart: 13, of which 3 were waited for; matrix products, arithmetic and copies ran while one was open for 2% of the time, Pallas kernels for 3%

profile of v6, /device:TPU:6, one launch (start us, length us, event | category | flops | bytes accessed | tf_op | source)
XLA Modules:
  0.0 182.2 jit_solution(9181485120457888944)
XLA Ops:
  6.5 1.6 sort.1
  8.1 14.0 %all_to_all.30 = bf16[4,56,384]{2,1,0:T(8,128)(2,1)} all-to-all(bf16[4,56,384]{2,1,0:T(8,128)(2,1)} %sort.1), channel_id=1, replica_groups=mesh['x'=4,'z'=16,'y'=4,'c'=2] {'x'}, dimensions={0} | all-to-all | bytes 344064 | tf_op jit(solution)/shard_map/all_to_all | solution.py:250
  22.8 0.7 convert_element_type.26
  23.6 0.2 multiply_cosine_fusion
  23.9 1.0 copy-done.4
  24.8 1.1 copy-done.5
  25.9 0.8 pack.1
  26.7 2.4 %collective-permute-start = (bf16[272,384]{1,0:T(8,128)(2,1)S(1)}, bf16[272,384]{1,0:T(8,128)(2,1)S(1)}, u32[]{:S(2)}, u32[]{:S(2)}) collective-permute-start(bf16[272,384]{1,0:T(8,128)(2,1)S(1)} %get-tuple-element.13), channel_id=1, source_target_pairs={{0,128},{128,0},{256,384},{384,256},{1,129},{129,1},{257,385},{385... | collective-permute-start | bytes 626696 | tf_op jit(solution)/shard_map/ppermute | solution.py:23
  29.1 5.3 %collective-permute-done = bf16[272,384]{1,0:T(8,128)(2,1)S(1)} collective-permute-done((bf16[272,384]{1,0:T(8,128)(2,1)S(1)}, bf16[272,384]{1,0:T(8,128)(2,1)S(1)}, u32[]{:S(2)}, u32[]{:S(2)}) %collective-permute-start) | collective-permute-done | bytes 208928 | tf_op jit(solution)/shard_map/ppermute | solution.py:23
  34.5 1.9 %collective-permute-start.2 = (bf16[2,272,384]{2,1,0:T(8,128)(2,1)S(1)}, bf16[2,272,384]{2,1,0:T(8,128)(2,1)S(1)}, u32[]{:S(2)}, u32[]{:S(2)}) collective-permute-start(bf16[2,272,384]{2,1,0:T(8,128)(2,1)S(1)} %pad_maximum_fusion.refs_0_), channel_id=1, source_target_pairs={{0,2},{2,4},{4,6},{6,0},{1,3},{3,5},{5,7},{7,1},{8,10},{10,12},{12... | collective-permute-start | bytes 1253384 | tf_op jit(solution)/shard_map/ppermute | solution.py:19
  36.4 1.9 %collective-permute-start.4 = (bf16[2,272,384]{2,1,0:T(8,128)(2,1)S(1)}, bf16[2,272,384]{2,1,0:T(8,128)(2,1)S(1)}, u32[]{:S(2)}, u32[]{:S(2)}) collective-permute-start(bf16[2,272,384]{2,1,0:T(8,128)(2,1)S(1)} %pad_maximum_fusion.refs_0_), channel_id=1, source_target_pairs={{0,4},{2,6},{4,0},{6,2},{1,5},{3,7},{5,1},{7,3},{8,12},{10,14},{12... | collective-permute-start | bytes 1253384 | tf_op jit(solution)/shard_map/ppermute | solution.py:19
  38.3 5.1 %collective-permute-start.6 = (bf16[2,272,384]{2,1,0:T(8,128)(2,1)S(1)}, bf16[2,272,384]{2,1,0:T(8,128)(2,1)S(1)}, u32[]{:S(2)}, u32[]{:S(2)}) collective-permute-start(bf16[2,272,384]{2,1,0:T(8,128)(2,1)S(1)} %pad_maximum_fusion.refs_0_), channel_id=1, source_target_pairs={{0,6},{2,0},{4,2},{6,4},{1,7},{3,1},{5,3},{7,5},{8,14},{10,8},{12,... | collective-permute-start | bytes 1253384 | tf_op jit(solution)/shard_map/ppermute | solution.py:19
  43.4 0.7 convert_element_type.28
  44.2 6.0 %all-to-all-start.1 = ((f16[4,64,384]{2,1,0:T(8,128)(2,1)}), f16[4,64,384]{2,1,0:T(8,128)(2,1)}, u32[]{:S(2)}, u32[]{:S(2)}) async-start(f16[4,64,384]{2,1,0:T(8,128)(2,1)} %bitcast.7), calls=%async_computation.1 | async-start | bytes 393216 | tf_op jit(solution)/shard_map/all_to_all | solution.py:280
  50.2 1.9 %collective-permute-start.1 = (bf16[2,272,384]{2,1,0:T(8,128)(2,1)S(1)}, bf16[2,272,384]{2,1,0:T(8,128)(2,1)S(1)}, u32[]{:S(2)}, u32[]{:S(2)}) collective-permute-start(bf16[2,272,384]{2,1,0:T(8,128)(2,1)S(1)} %pad_maximum_fusion.refs_0_), channel_id=1, source_target_pairs={{0,1},{1,0},{2,3},{3,2},{4,5},{5,4},{6,7},{7,6},{8,9},{9,8},{10,11... | collective-permute-start | bytes 1253384 | tf_op jit(solution)/shard_map/ppermute | solution.py:27
  52.1 1.3 collective-permute-done.2.refs_2_
  53.4 1.9 %collective-permute-start.3 = (bf16[2,272,384]{2,1,0:T(8,128)(2,1)S(1)}, bf16[2,272,384]{2,1,0:T(8,128)(2,1)S(1)}, u32[]{:S(2)}, u32[]{:S(2)}) collective-permute-start(bf16[2,272,384]{2,1,0:T(8,128)(2,1)S(1)} %collective-permute-done.2.refs_2_), channel_id=1, source_target_pairs={{0,1},{1,0},{2,3},{3,2},{4,5},{5,4},{6,7},{7,6},{8,9},{9,8},{10,11... | collective-permute-start | bytes 1253384 | tf_op jit(solution)/shard_map/ppermute | solution.py:27
  55.3 0.7 copy-done.6
  56.1 2.4 %collective-permute-start.5 = (bf16[2,272,384]{2,1,0:T(8,128)(2,1)S(1)}, bf16[2,272,384]{2,1,0:T(8,128)(2,1)S(1)}, u32[]{:S(2)}, u32[]{:S(2)}) collective-permute-start(bf16[2,272,384]{2,1,0:T(8,128)(2,1)S(1)} %collective-permute-done.4.refs_4_), channel_id=1, source_target_pairs={{0,1},{1,0},{2,3},{3,2},{4,5},{5,4},{6,7},{7,6},{8,9},{9,8},{10,11... | collective-permute-start | bytes 1253384 | tf_op jit(solution)/shard_map/ppermute | solution.py:27
  58.5 0.7 copy-done.8
  59.2 1.9 %collective-permute-start.7 = (bf16[2,272,384]{2,1,0:T(8,128)(2,1)S(1)}, bf16[2,272,384]{2,1,0:T(8,128)(2,1)S(1)}, u32[]{:S(2)}, u32[]{:S(2)}) collective-permute-start(bf16[2,272,384]{2,1,0:T(8,128)(2,1)S(1)} %collective-permute-done.6.refs_6_), channel_id=1, source_target_pairs={{0,1},{1,0},{2,3},{3,2},{4,5},{5,4},{6,7},{7,6},{8,9},{9,8},{10,11... | collective-permute-start | bytes 1253384 | tf_op jit(solution)/shard_map/ppermute | solution.py:27
  61.2 0.8 copy-done.10
  61.9 0.8 constant_dynamic-slice_fusion
  62.7 0.6 reshape.21
  63.4 12.1 %all-to-all-start.2 = ((f16[16,4,384]{2,1,0:T(4,128)(2,1)}), f16[16,4,384]{2,1,0:T(4,128)(2,1)S(1)}, u32[]{:S(2)}, u32[]{:S(2)}) async-start(f16[16,4,384]{2,1,0:T(4,128)(2,1)} %reshape.21), calls=%async_computation.2 | async-start | bytes 98304 | tf_op jit(solution)/shard_map/all_to_all | solution.py:282
  75.6 0.7 copy-done.12
  76.3 0.8 copy-done.14
  77.1 0.8 copy-done.16
  77.9 0.8 copy-done.18
  78.6 1.0 copy-done.2
  79.7 1.0 copy-done.7
  80.7 1.0 copy-done.9
  81.7 1.0 copy-done.11
  82.7 1.0 copy-done.13
  83.7 1.0 copy-done.15
  84.7 1.0 copy-done.17
  85.7 1.0 copy-done.19
  86.7 3.9 %norm.1.h_ref = bf16[2,256,3072]{2,1,0:T(8,128)(2,1)S(1)} custom-call(s32[6]{0:T(128)S(1)} %stack.35.idx_ref, bf16[2,272,384]{2,1,0:T(8,128)(2,1)S(1)} %copy-done.2, bf16[2,272,384]{2,1,0:T(8,128)(2,1)S(1)} %copy-done.13, bf16[2,272,384]{2,1,0:T(8,128)(2,1)S(1)} %copy-done.7, bf16[2,272,384]{2,1,0:T(8,128)(2,1)S(1)} %copy-done.15, ...), custom_call_target="tpu_custom_call" | custom-call | tf_op jit(solution)/shard_map/norm/pallas_call | solution.py:269
  90.6 7.0 %all-gather.5.cloned.1.call-done = bf16[64,56,384]{2,1,0:T(8,128)(2,1)} async-done(((bf16[4,56,384]{2,1,0:T(8,128)(2,1)}), bf16[64,56,384]{2,1,0:T(8,128)(2,1)}) %all-gather.5.cloned.1.call-update) | async-done | bytes 2752528 | tf_op jit(solution)/shard_map/all_gather | solution.py:250
  97.6 1.8 copy-done
  99.3 4.0 %attention.1 = (bf16[2,256,128]{2,1,0:T(8,128)(2,1)S(1)}, bf16[16,4,8,384]{3,2,1,0:T(8,128)(2,1)}) custom-call(s32[6]{0:T(128)S(1)} %stack.35.idx_ref, f32[1,128]{1,0:T(1,128)S(1)} %bitcast.29, f32[1,128]{1,0:T(1,128)S(1)} %bitcast.30, bf16[2,256,3072]{2,1,0:T(8,128)(2,1)S(1)} %norm.1.h_ref, bf16[16,4,56,384]{3,2,1,0:T(8,128)(2,1)S(1)} %bitcast.24), custom_call_target="tpu_custom_call" | custom-call | tf_op jit(solution)/shard_map/attention/pallas_call | solution.py:284
  103.5 25.2 %all_to_all.31 = bf16[64,8,128]{2,1,0:T(8,128)(2,1)S(1)} all-to-all(bf16[64,8,128]{2,1,0:T(8,128)(2,1)S(1)} %copy.14), channel_id=1, replica_groups=mesh['x'=4,'z'=16,'y'=4,'c'=2] {'x','z'}, dimensions={0} | all-to-all | bytes 262144 | tf_op jit(solution)/shard_map/all_to_all | solution.py:298
  128.8 12.2 %all_to_all.32.mine_ref = bf16[4,512,128]{2,1,0:T(8,128)(2,1)S(1)} all-to-all(bf16[4,512,128]{2,1,0:T(8,128)(2,1)S(1)} %broadcast_in_dim.21), channel_id=1, replica_groups=mesh['x'=4,'z'=16,'y'=4,'c'=2] {'y'}, dimensions={0} | all-to-all | bytes 1048576 | tf_op jit(solution)/shard_map/all_to_all | solution.py:31
  141.0 1.9 %collective-permute-start.8 = (bf16[4,512,128]{2,1,0:T(8,128)(2,1)S(1)}, bf16[4,512,128]{2,1,0:T(8,128)(2,1)S(1)}, u32[]{:S(2)}, u32[]{:S(2)}) collective-permute-start(bf16[4,512,128]{2,1,0:T(8,128)(2,1)S(1)} %all_to_all.32.mine_ref), channel_id=1, source_target_pairs={{0,1},{1,0},{2,3},{3,2},{4,5},{5,4},{6,7},{7,6},{8,9},{9,8},{10,11... | collective-permute-start | bytes 1572872 | tf_op jit(solution)/shard_map/ppermute | solution.py:27
  143.8 1.4 copy-done.3
  145.3 2.0 %project.1 = f32[64,2,896]{2,1,0:T(2,128)S(1)} custom-call(s32[6]{0:T(128)S(1)} %stack.35.idx_ref, s32[2]{0:T(128)S(1)} %pad_add_fusion.win_ref, f32[64]{0:T(128)S(1)} %convert_multiply_fusion.dt_ref, f32[64,384]{1,0:T(8,128)S(1)} %get-tuple-element.12.gate_ref, f32[16,4,384]{2,1,0:T(4,128)S(1)} %convert_element_type.30.lat_ref, ...), custom_call_target="tpu_custom_call" | custom-call | tf_op jit(solution)/shard_map/project/pallas_call | solution.py:308
  147.5 26.6 %all_to_all.33 = f16[64,2,896]{2,1,0:T(2,128)(2,1)S(1)} all-to-all(f16[64,2,896]{2,1,0:T(2,128)(2,1)S(1)} %convert_element_type.31), channel_id=1, replica_groups=mesh['x'=4,'z'=16,'y'=4,'c'=2] {'x','z'}, dimensions={0} | all-to-all | bytes 458752 | tf_op jit(solution)/shard_map/all_to_all | solution.py:321
  174.3 1.1 unscale.1
  (55 shorter events, 1.1 us)
Async XLA Ops:
  6.5 91.0 %all-gather.5.cloned.1.call-start = ((), (), s32[]{:S(2)}) async-start(), calls=%async_computation.6 | async-start | bytes 2924544 | tf_op jit(solution)/shard_map/all_gather | solution.py:250
  23.8 1.0 copy-start.4
  24.8 1.1 copy-start.5
  26.7 7.7 %collective-permute-start = (bf16[272,384]{1,0:T(8,128)(2,1)S(1)}, bf16[272,384]{1,0:T(8,128)(2,1)S(1)}, u32[]{:S(2)}, u32[]{:S(2)}) collective-permute-start(bf16[272,384]{1,0:T(8,128)(2,1)S(1)} %get-tuple-element.13), channel_id=1, source_target_pairs={{0,128},{128,0},{256,384},{384,256},{1,129},{129,1},{257,385},{385... | collective-permute-start | bytes 626696 | tf_op jit(solution)/shard_map/ppermute | solution.py:23
  34.4 42.7 %copy-start.1 = (bf16[2,272,384]{2,1,0:T(8,128)(2,1)}, bf16[2,272,384]{2,1,0:T(8,128)(2,1)S(1)}, u32[]{:S(2)}) copy-start(bf16[2,272,384]{2,1,0:T(8,128)(2,1)S(1)} %pad_maximum_fusion.refs_0_) | copy-start | bytes 1253380
  34.5 18.9 %collective-permute-start.2 = (bf16[2,272,384]{2,1,0:T(8,128)(2,1)S(1)}, bf16[2,272,384]{2,1,0:T(8,128)(2,1)S(1)}, u32[]{:S(2)}, u32[]{:S(2)}) collective-permute-start(bf16[2,272,384]{2,1,0:T(8,128)(2,1)S(1)} %pad_maximum_fusion.refs_0_), channel_id=1, source_target_pairs={{0,2},{2,4},{4,6},{6,0},{1,3},{3,5},{5,7},{7,1},{8,10},{10,12},{12... | collective-permute-start | bytes 1253384 | tf_op jit(solution)/shard_map/ppermute | solution.py:19
  36.4 19.7 %collective-permute-start.4 = (bf16[2,272,384]{2,1,0:T(8,128)(2,1)S(1)}, bf16[2,272,384]{2,1,0:T(8,128)(2,1)S(1)}, u32[]{:S(2)}, u32[]{:S(2)}) collective-permute-start(bf16[2,272,384]{2,1,0:T(8,128)(2,1)S(1)} %pad_maximum_fusion.refs_0_), channel_id=1, source_target_pairs={{0,4},{2,6},{4,0},{6,2},{1,5},{3,7},{5,1},{7,3},{8,12},{10,14},{12... | collective-permute-start | bytes 1253384 | tf_op jit(solution)/shard_map/ppermute | solution.py:19
  38.3 20.9 %collective-permute-start.6 = (bf16[2,272,384]{2,1,0:T(8,128)(2,1)S(1)}, bf16[2,272,384]{2,1,0:T(8,128)(2,1)S(1)}, u32[]{:S(2)}, u32[]{:S(2)}) collective-permute-start(bf16[2,272,384]{2,1,0:T(8,128)(2,1)S(1)} %pad_maximum_fusion.refs_0_), channel_id=1, source_target_pairs={{0,6},{2,0},{4,2},{6,4},{1,7},{3,1},{5,3},{7,5},{8,14},{10,8},{12,... | collective-permute-start | bytes 1253384 | tf_op jit(solution)/shard_map/ppermute | solution.py:19
  44.2 17.8 %all-to-all-start.1 = ((f16[4,64,384]{2,1,0:T(8,128)(2,1)}), f16[4,64,384]{2,1,0:T(8,128)(2,1)}, u32[]{:S(2)}, u32[]{:S(2)}) async-start(f16[4,64,384]{2,1,0:T(8,128)(2,1)} %bitcast.7), calls=%async_computation.1 | async-start | bytes 393216 | tf_op jit(solution)/shard_map/all_to_all | solution.py:280
  50.2 25.4 %collective-permute-start.1 = (bf16[2,272,384]{2,1,0:T(8,128)(2,1)S(1)}, bf16[2,272,384]{2,1,0:T(8,128)(2,1)S(1)}, u32[]{:S(2)}, u32[]{:S(2)}) collective-permute-start(bf16[2,272,384]{2,1,0:T(8,128)(2,1)S(1)} %pad_maximum_fusion.refs_0_), channel_id=1, source_target_pairs={{0,1},{1,0},{2,3},{3,2},{4,5},{5,4},{6,7},{7,6},{8,9},{9,8},{10,11... | collective-permute-start | bytes 1253384 | tf_op jit(solution)/shard_map/ppermute | solution.py:27
  53.4 22.9 %collective-permute-start.3 = (bf16[2,272,384]{2,1,0:T(8,128)(2,1)S(1)}, bf16[2,272,384]{2,1,0:T(8,128)(2,1)S(1)}, u32[]{:S(2)}, u32[]{:S(2)}) collective-permute-start(bf16[2,272,384]{2,1,0:T(8,128)(2,1)S(1)} %collective-permute-done.2.refs_2_), channel_id=1, source_target_pairs={{0,1},{1,0},{2,3},{3,2},{4,5},{5,4},{6,7},{7,6},{8,9},{9,8},{10,11... | collective-permute-start | bytes 1253384 | tf_op jit(solution)/shard_map/ppermute | solution.py:27
  55.3 0.8 copy-start.6
  56.1 21.0 %collective-permute-start.5 = (bf16[2,272,384]{2,1,0:T(8,128)(2,1)S(1)}, bf16[2,272,384]{2,1,0:T(8,128)(2,1)S(1)}, u32[]{:S(2)}, u32[]{:S(2)}) collective-permute-start(bf16[2,272,384]{2,1,0:T(8,128)(2,1)S(1)} %collective-permute-done.4.refs_4_), channel_id=1, source_target_pairs={{0,1},{1,0},{2,3},{3,2},{4,5},{5,4},{6,7},{7,6},{8,9},{9,8},{10,11... | collective-permute-start | bytes 1253384 | tf_op jit(solution)/shard_map/ppermute | solution.py:27
  58.5 0.8 copy-start.8
  59.2 18.6 %collective-permute-start.7 = (bf16[2,272,384]{2,1,0:T(8,128)(2,1)S(1)}, bf16[2,272,384]{2,1,0:T(8,128)(2,1)S(1)}, u32[]{:S(2)}, u32[]{:S(2)}) collective-permute-start(bf16[2,272,384]{2,1,0:T(8,128)(2,1)S(1)} %collective-permute-done.6.refs_6_), channel_id=1, source_target_pairs={{0,1},{1,0},{2,3},{3,2},{4,5},{5,4},{6,7},{7,6},{8,9},{9,8},{10,11... | collective-permute-start | bytes 1253384 | tf_op jit(solution)/shard_map/ppermute | solution.py:27
  61.1 0.8 copy-start.10
  63.4 34.2 %copy-start.20 = (f32[128]{0:T(128)S(1)}, f32[128]{0:T(128)}, u32[]{:S(2)}) copy-start(f32[128]{0:T(128)} %param.16) | copy-start | bytes 1540
  63.4 34.2 %copy-start.21 = (f32[128]{0:T(128)S(1)}, f32[128]{0:T(128)}, u32[]{:S(2)}) copy-start(f32[128]{0:T(128)} %param.17) | copy-start | bytes 1540
  63.4 27.2 %all-to-all-start.2 = ((f16[16,4,384]{2,1,0:T(4,128)(2,1)}), f16[16,4,384]{2,1,0:T(4,128)(2,1)S(1)}, u32[]{:S(2)}, u32[]{:S(2)}) async-start(f16[16,4,384]{2,1,0:T(4,128)(2,1)} %reshape.21), calls=%async_computation.2 | async-start | bytes 98304 | tf_op jit(solution)/shard_map/all_to_all | solution.py:282
  75.5 68.2 %all-gather.7.cloned.1.call-start = ((), (), s32[]{:S(2)}) async-start(), calls=%async_computation.7 | async-start | bytes 1966080 | tf_op jit(solution)/shard_map/all_gather | solution.py:296
  75.6 0.8 copy-start.12
  76.3 0.8 copy-start.14
  77.1 0.8 copy-start.16
  77.9 0.8 copy-start.18
  78.6 1.0 copy-start.2
  79.6 1.0 copy-start.7
  80.7 1.0 copy-start.9
  81.7 1.0 copy-start.11
  82.7 1.0 copy-start.13
  83.7 1.0 copy-start.15
  84.7 1.0 copy-start.17
  85.7 1.0 copy-start.19
  97.6 1.8 copy-start
  103.3 40.3 %copy-start.22 = (s32[65]{0:T(128)S(1)}, s32[65]{0:T(128)}, u32[]{:S(2)}) copy-start(s32[65]{0:T(128)} %param.10) | copy-start | bytes 784
  141.0 4.3 %collective-permute-start.8 = (bf16[4,512,128]{2,1,0:T(8,128)(2,1)S(1)}, bf16[4,512,128]{2,1,0:T(8,128)(2,1)S(1)}, u32[]{:S(2)}, u32[]{:S(2)}) collective-permute-start(bf16[4,512,128]{2,1,0:T(8,128)(2,1)S(1)} %all_to_all.32.mine_ref), channel_id=1, source_target_pairs={{0,1},{1,0},{2,3},{3,2},{4,5},{5,4},{6,7},{7,6},{8,9},{9,8},{10,11... | collective-permute-start | bytes 1572872 | tf_op jit(solution)/shard_map/ppermute | solution.py:27
  143.8 1.4 copy-start.3
Sparse Core Ops, SparseCore 0:
  22.3 75.1 all-gather.4
  103.5 30.8 all-gather.6

commit v7 on v6

--- a/solution.py
+++ b/solution.py
@@ -164,7 +164,7 @@
         return run + term_ref[slot]
 
     total = lax.fori_loop(
-        0, count, step, jnp.zeros(run_ref.shape[1:], jnp.float32), unroll=8
+        0, count, step, jnp.zeros(run_ref.shape[1:], jnp.float32), unroll=32
     )
 
     def move(i, _):
@@ -190,14 +190,14 @@
     rows = out_ref.shape[0] // count
     half = rows // 2
     scale = jnp.exp2(in_ref[:, :, half * width :])
-    for token in range(rows):
-        row, at = token // half, token % half * width
-        for g in range(width // 128):
-            part = in_ref[:, row : row + 1, at + g * 128 : at + (g + 1) * 128]
-            values = part * scale[:, row : row + 1, :]
-            for i in range(count):
-                to = i * rows + token
-                out_ref[to : to + 1, g * 128 : (g + 1) * 128] = values[i]
+    for g in range(width // 128):
+        parts = []
+        for token in range(rows):
+            row, at = token // half, token % half * width + g * 128
+            parts.append(in_ref[:, row : row + 1, at : at + 128] * scale[:, row : row + 1, :])
+        values = jnp.concatenate(parts, axis=1)
+        for i in range(count):
+            out_ref[i * rows : (i + 1) * rows, g * 128 : (g + 1) * 128] = values[i]
 
 
 def vmem():

time: 184 us -> 184 us (level)
  no operation moved by 1% of the time
where the time goes in v7:
time: 184 us; the launch traced here: 182 us
  blocking collectives  78.1 us (42%)
  starting transfers between devices  39.5 us (21%)
  local copies, waits for them, and re-layouts  20.3 us (11%)
  between operations  15 us (8%)
  waiting for transfers between devices  13.7 us (7%)
  Pallas kernels  13.4 us (7%)
  other arithmetic  2.14 us (1%)
    all_to_all x1, blocking collectives, per_device(): lax.all_to_all(sums.astype(jnp.float16), STEP, 0, 0, tiled=True)  26.6 us
    all_to_all x1, blocking collectives, per_device(): lax.all_to_all(attn, STEP, 0, 0, tiled=True).reshape(count * 2 * rows, HD)  25.2 us
    unnamed x46, local copies, waits for them, and re-layouts  18.6 us
    all_to_all x1, blocking collectives, per_device(): lax.all_to_all(sorted_rows, 'x', 0, 0, tiled=True)  14 us
    all_to_all x1, blocking collectives, to_all(): lax.all_to_all(jnp.broadcast_to(value[None], (size,) + value.shape), axis...  12.2 us
    all_to_all x1, starting transfers between devices, per_device(): lax.all_to_all(first.reshape(NZ, rows, width), 'z', 0, 0, tiled=True)  12.1 us
    ppermute x5, starting transfers between devices, swap_core(): return lax.ppermute(value, 'c', [(i, i ^ 1) for i in range(NC)])  10 us
    ppermute x3, starting transfers between devices, shift(): lax.ppermute(value, axis, [(i, (i + by) % size) for i in range(size)])  8.97 us
  transfers between devices with their start and end apart: 13, of which 3 were waited for; matrix products, arithmetic and copies ran while one was open for 2% of the time, Pallas kernels for 3%

profile of v7, /device:TPU:6, one launch (start us, length us, event | category | flops | bytes accessed | tf_op | source)
XLA Modules:
  0.0 182.2 jit_solution(2956373149554871713)
XLA Ops:
  6.5 1.6 sort.1
  8.1 14.0 %all_to_all.30 = bf16[4,56,384]{2,1,0:T(8,128)(2,1)} all-to-all(bf16[4,56,384]{2,1,0:T(8,128)(2,1)} %sort.1), channel_id=1, replica_groups=mesh['x'=4,'z'=16,'y'=4,'c'=2] {'x'}, dimensions={0} | all-to-all | bytes 344064 | tf_op jit(solution)/shard_map/all_to_all | solution.py:250
  22.8 0.7 convert_element_type.26
  23.6 0.2 multiply_cosine_fusion
  23.9 1.0 copy-done.4
  24.8 1.1 copy-done.5
  25.9 0.8 pack.1
  26.7 2.4 %collective-permute-start = (bf16[272,384]{1,0:T(8,128)(2,1)S(1)}, bf16[272,384]{1,0:T(8,128)(2,1)S(1)}, u32[]{:S(2)}, u32[]{:S(2)}) collective-permute-start(bf16[272,384]{1,0:T(8,128)(2,1)S(1)} %get-tuple-element.13), channel_id=1, source_target_pairs={{0,128},{128,0},{256,384},{384,256},{1,129},{129,1},{257,385},{385... | collective-permute-start | bytes 626696 | tf_op jit(solution)/shard_map/ppermute | solution.py:23
  29.1 5.3 %collective-permute-done = bf16[272,384]{1,0:T(8,128)(2,1)S(1)} collective-permute-done((bf16[272,384]{1,0:T(8,128)(2,1)S(1)}, bf16[272,384]{1,0:T(8,128)(2,1)S(1)}, u32[]{:S(2)}, u32[]{:S(2)}) %collective-permute-start) | collective-permute-done | bytes 208928 | tf_op jit(solution)/shard_map/ppermute | solution.py:23
  34.5 1.9 %collective-permute-start.2 = (bf16[2,272,384]{2,1,0:T(8,128)(2,1)S(1)}, bf16[2,272,384]{2,1,0:T(8,128)(2,1)S(1)}, u32[]{:S(2)}, u32[]{:S(2)}) collective-permute-start(bf16[2,272,384]{2,1,0:T(8,128)(2,1)S(1)} %pad_maximum_fusion.refs_0_), channel_id=1, source_target_pairs={{0,2},{2,4},{4,6},{6,0},{1,3},{3,5},{5,7},{7,1},{8,10},{10,12},{12... | collective-permute-start | bytes 1253384 | tf_op jit(solution)/shard_map/ppermute | solution.py:19
  36.4 1.9 %collective-permute-start.4 = (bf16[2,272,384]{2,1,0:T(8,128)(2,1)S(1)}, bf16[2,272,384]{2,1,0:T(8,128)(2,1)S(1)}, u32[]{:S(2)}, u32[]{:S(2)}) collective-permute-start(bf16[2,272,384]{2,1,0:T(8,128)(2,1)S(1)} %pad_maximum_fusion.refs_0_), channel_id=1, source_target_pairs={{0,4},{2,6},{4,0},{6,2},{1,5},{3,7},{5,1},{7,3},{8,12},{10,14},{12... | collective-permute-start | bytes 1253384 | tf_op jit(solution)/shard_map/ppermute | solution.py:19
  38.3 5.1 %collective-permute-start.6 = (bf16[2,272,384]{2,1,0:T(8,128)(2,1)S(1)}, bf16[2,272,384]{2,1,0:T(8,128)(2,1)S(1)}, u32[]{:S(2)}, u32[]{:S(2)}) collective-permute-start(bf16[2,272,384]{2,1,0:T(8,128)(2,1)S(1)} %pad_maximum_fusion.refs_0_), channel_id=1, source_target_pairs={{0,6},{2,0},{4,2},{6,4},{1,7},{3,1},{5,3},{7,5},{8,14},{10,8},{12,... | collective-permute-start | bytes 1253384 | tf_op jit(solution)/shard_map/ppermute | solution.py:19
  43.4 0.7 convert_element_type.28
  44.2 6.0 %all-to-all-start.1 = ((f16[4,64,384]{2,1,0:T(8,128)(2,1)}), f16[4,64,384]{2,1,0:T(8,128)(2,1)}, u32[]{:S(2)}, u32[]{:S(2)}) async-start(f16[4,64,384]{2,1,0:T(8,128)(2,1)} %bitcast.7), calls=%async_computation.1 | async-start | bytes 393216 | tf_op jit(solution)/shard_map/all_to_all | solution.py:280
  50.2 1.9 %collective-permute-start.1 = (bf16[2,272,384]{2,1,0:T(8,128)(2,1)S(1)}, bf16[2,272,384]{2,1,0:T(8,128)(2,1)S(1)}, u32[]{:S(2)}, u32[]{:S(2)}) collective-permute-start(bf16[2,272,384]{2,1,0:T(8,128)(2,1)S(1)} %pad_maximum_fusion.refs_0_), channel_id=1, source_target_pairs={{0,1},{1,0},{2,3},{3,2},{4,5},{5,4},{6,7},{7,6},{8,9},{9,8},{10,11... | collective-permute-start | bytes 1253384 | tf_op jit(solution)/shard_map/ppermute | solution.py:27
  52.1 1.3 collective-permute-done.2.refs_2_
  53.4 1.9 %collective-permute-start.3 = (bf16[2,272,384]{2,1,0:T(8,128)(2,1)S(1)}, bf16[2,272,384]{2,1,0:T(8,128)(2,1)S(1)}, u32[]{:S(2)}, u32[]{:S(2)}) collective-permute-start(bf16[2,272,384]{2,1,0:T(8,128)(2,1)S(1)} %collective-permute-done.2.refs_2_), channel_id=1, source_target_pairs={{0,1},{1,0},{2,3},{3,2},{4,5},{5,4},{6,7},{7,6},{8,9},{9,8},{10,11... | collective-permute-start | bytes 1253384 | tf_op jit(solution)/shard_map/ppermute | solution.py:27
  55.3 0.7 copy-done.6
  56.1 2.4 %collective-permute-start.5 = (bf16[2,272,384]{2,1,0:T(8,128)(2,1)S(1)}, bf16[2,272,384]{2,1,0:T(8,128)(2,1)S(1)}, u32[]{:S(2)}, u32[]{:S(2)}) collective-permute-start(bf16[2,272,384]{2,1,0:T(8,128)(2,1)S(1)} %collective-permute-done.4.refs_4_), channel_id=1, source_target_pairs={{0,1},{1,0},{2,3},{3,2},{4,5},{5,4},{6,7},{7,6},{8,9},{9,8},{10,11... | collective-permute-start | bytes 1253384 | tf_op jit(solution)/shard_map/ppermute | solution.py:27
  58.5 0.7 copy-done.8
  59.2 1.9 %collective-permute-start.7 = (bf16[2,272,384]{2,1,0:T(8,128)(2,1)S(1)}, bf16[2,272,384]{2,1,0:T(8,128)(2,1)S(1)}, u32[]{:S(2)}, u32[]{:S(2)}) collective-permute-start(bf16[2,272,384]{2,1,0:T(8,128)(2,1)S(1)} %collective-permute-done.6.refs_6_), channel_id=1, source_target_pairs={{0,1},{1,0},{2,3},{3,2},{4,5},{5,4},{6,7},{7,6},{8,9},{9,8},{10,11... | collective-permute-start | bytes 1253384 | tf_op jit(solution)/shard_map/ppermute | solution.py:27
  61.2 0.8 copy-done.10
  61.9 0.8 constant_dynamic-slice_fusion
  62.7 0.6 reshape.21
  63.4 12.1 %all-to-all-start.2 = ((f16[16,4,384]{2,1,0:T(4,128)(2,1)}), f16[16,4,384]{2,1,0:T(4,128)(2,1)S(1)}, u32[]{:S(2)}, u32[]{:S(2)}) async-start(f16[16,4,384]{2,1,0:T(4,128)(2,1)} %reshape.21), calls=%async_computation.2 | async-start | bytes 98304 | tf_op jit(solution)/shard_map/all_to_all | solution.py:282
  75.6 0.7 copy-done.12
  76.3 0.8 copy-done.14
  77.1 0.8 copy-done.16
  77.9 0.8 copy-done.18
  78.6 1.0 copy-done.2
  79.7 1.0 copy-done.7
  80.7 1.0 copy-done.9
  81.7 1.0 copy-done.11
  82.7 1.0 copy-done.13
  83.7 1.0 copy-done.15
  84.7 1.0 copy-done.17
  85.7 1.0 copy-done.19
  86.7 3.9 %norm.1.h_ref = bf16[2,256,3072]{2,1,0:T(8,128)(2,1)S(1)} custom-call(s32[6]{0:T(128)S(1)} %stack.35.idx_ref, bf16[2,272,384]{2,1,0:T(8,128)(2,1)S(1)} %copy-done.2, bf16[2,272,384]{2,1,0:T(8,128)(2,1)S(1)} %copy-done.13, bf16[2,272,384]{2,1,0:T(8,128)(2,1)S(1)} %copy-done.7, bf16[2,272,384]{2,1,0:T(8,128)(2,1)S(1)} %copy-done.15, ...), custom_call_target="tpu_custom_call" | custom-call | tf_op jit(solution)/shard_map/norm/pallas_call | solution.py:269
  90.6 7.0 %all-gather.5.cloned.1.call-done = bf16[64,56,384]{2,1,0:T(8,128)(2,1)} async-done(((bf16[4,56,384]{2,1,0:T(8,128)(2,1)}), bf16[64,56,384]{2,1,0:T(8,128)(2,1)}) %all-gather.5.cloned.1.call-update) | async-done | bytes 2752528 | tf_op jit(solution)/shard_map/all_gather | solution.py:250
  97.6 1.8 copy-done
  99.3 4.0 %attention.1 = (bf16[2,256,128]{2,1,0:T(8,128)(2,1)S(1)}, bf16[16,4,8,384]{3,2,1,0:T(8,128)(2,1)}) custom-call(s32[6]{0:T(128)S(1)} %stack.35.idx_ref, f32[1,128]{1,0:T(1,128)S(1)} %bitcast.29, f32[1,128]{1,0:T(1,128)S(1)} %bitcast.30, bf16[2,256,3072]{2,1,0:T(8,128)(2,1)S(1)} %norm.1.h_ref, bf16[16,4,56,384]{3,2,1,0:T(8,128)(2,1)S(1)} %bitcast.24), custom_call_target="tpu_custom_call" | custom-call | tf_op jit(solution)/shard_map/attention/pallas_call | solution.py:284
  103.5 25.2 %all_to_all.31 = bf16[64,8,128]{2,1,0:T(8,128)(2,1)S(1)} all-to-all(bf16[64,8,128]{2,1,0:T(8,128)(2,1)S(1)} %copy.14), channel_id=1, replica_groups=mesh['x'=4,'z'=16,'y'=4,'c'=2] {'x','z'}, dimensions={0} | all-to-all | bytes 262144 | tf_op jit(solution)/shard_map/all_to_all | solution.py:298
  128.8 12.2 %all_to_all.32.mine_ref = bf16[4,512,128]{2,1,0:T(8,128)(2,1)S(1)} all-to-all(bf16[4,512,128]{2,1,0:T(8,128)(2,1)S(1)} %broadcast_in_dim.21), channel_id=1, replica_groups=mesh['x'=4,'z'=16,'y'=4,'c'=2] {'y'}, dimensions={0} | all-to-all | bytes 1048576 | tf_op jit(solution)/shard_map/all_to_all | solution.py:31
  141.0 1.9 %collective-permute-start.8 = (bf16[4,512,128]{2,1,0:T(8,128)(2,1)S(1)}, bf16[4,512,128]{2,1,0:T(8,128)(2,1)S(1)}, u32[]{:S(2)}, u32[]{:S(2)}) collective-permute-start(bf16[4,512,128]{2,1,0:T(8,128)(2,1)S(1)} %all_to_all.32.mine_ref), channel_id=1, source_target_pairs={{0,1},{1,0},{2,3},{3,2},{4,5},{5,4},{6,7},{7,6},{8,9},{9,8},{10,11... | collective-permute-start | bytes 1572872 | tf_op jit(solution)/shard_map/ppermute | solution.py:27
  143.8 1.4 copy-done.3
  145.3 2.0 %project.1 = f32[64,2,896]{2,1,0:T(2,128)S(1)} custom-call(s32[6]{0:T(128)S(1)} %stack.35.idx_ref, s32[2]{0:T(128)S(1)} %pad_add_fusion.win_ref, f32[64]{0:T(128)S(1)} %convert_multiply_fusion.dt_ref, f32[64,384]{1,0:T(8,128)S(1)} %get-tuple-element.12.gate_ref, f32[16,4,384]{2,1,0:T(4,128)S(1)} %convert_element_type.30.lat_ref, ...), custom_call_target="tpu_custom_call" | custom-call | tf_op jit(solution)/shard_map/project/pallas_call | solution.py:308
  147.5 26.6 %all_to_all.33 = f16[64,2,896]{2,1,0:T(2,128)(2,1)S(1)} all-to-all(f16[64,2,896]{2,1,0:T(2,128)(2,1)S(1)} %convert_element_type.31), channel_id=1, replica_groups=mesh['x'=4,'z'=16,'y'=4,'c'=2] {'x','z'}, dimensions={0} | all-to-all | bytes 458752 | tf_op jit(solution)/shard_map/all_to_all | solution.py:321
  174.3 1.1 unscale.1
  (55 shorter events, 1.1 us)
Async XLA Ops:
  6.5 91.0 %all-gather.5.cloned.1.call-start = ((), (), s32[]{:S(2)}) async-start(), calls=%async_computation.6 | async-start | bytes 2924544 | tf_op jit(solution)/shard_map/all_gather | solution.py:250
  23.8 1.0 copy-start.4
  24.8 1.1 copy-start.5
  26.7 7.7 %collective-permute-start = (bf16[272,384]{1,0:T(8,128)(2,1)S(1)}, bf16[272,384]{1,0:T(8,128)(2,1)S(1)}, u32[]{:S(2)}, u32[]{:S(2)}) collective-permute-start(bf16[272,384]{1,0:T(8,128)(2,1)S(1)} %get-tuple-element.13), channel_id=1, source_target_pairs={{0,128},{128,0},{256,384},{384,256},{1,129},{129,1},{257,385},{385... | collective-permute-start | bytes 626696 | tf_op jit(solution)/shard_map/ppermute | solution.py:23
  34.4 42.7 %copy-start.1 = (bf16[2,272,384]{2,1,0:T(8,128)(2,1)}, bf16[2,272,384]{2,1,0:T(8,128)(2,1)S(1)}, u32[]{:S(2)}) copy-start(bf16[2,272,384]{2,1,0:T(8,128)(2,1)S(1)} %pad_maximum_fusion.refs_0_) | copy-start | bytes 1253380
  34.5 18.9 %collective-permute-start.2 = (bf16[2,272,384]{2,1,0:T(8,128)(2,1)S(1)}, bf16[2,272,384]{2,1,0:T(8,128)(2,1)S(1)}, u32[]{:S(2)}, u32[]{:S(2)}) collective-permute-start(bf16[2,272,384]{2,1,0:T(8,128)(2,1)S(1)} %pad_maximum_fusion.refs_0_), channel_id=1, source_target_pairs={{0,2},{2,4},{4,6},{6,0},{1,3},{3,5},{5,7},{7,1},{8,10},{10,12},{12... | collective-permute-start | bytes 1253384 | tf_op jit(solution)/shard_map/ppermute | solution.py:19
  36.4 19.7 %collective-permute-start.4 = (bf16[2,272,384]{2,1,0:T(8,128)(2,1)S(1)}, bf16[2,272,384]{2,1,0:T(8,128)(2,1)S(1)}, u32[]{:S(2)}, u32[]{:S(2)}) collective-permute-start(bf16[2,272,384]{2,1,0:T(8,128)(2,1)S(1)} %pad_maximum_fusion.refs_0_), channel_id=1, source_target_pairs={{0,4},{2,6},{4,0},{6,2},{1,5},{3,7},{5,1},{7,3},{8,12},{10,14},{12... | collective-permute-start | bytes 1253384 | tf_op jit(solution)/shard_map/ppermute | solution.py:19
  38.3 20.9 %collective-permute-start.6 = (bf16[2,272,384]{2,1,0:T(8,128)(2,1)S(1)}, bf16[2,272,384]{2,1,0:T(8,128)(2,1)S(1)}, u32[]{:S(2)}, u32[]{:S(2)}) collective-permute-start(bf16[2,272,384]{2,1,0:T(8,128)(2,1)S(1)} %pad_maximum_fusion.refs_0_), channel_id=1, source_target_pairs={{0,6},{2,0},{4,2},{6,4},{1,7},{3,1},{5,3},{7,5},{8,14},{10,8},{12,... | collective-permute-start | bytes 1253384 | tf_op jit(solution)/shard_map/ppermute | solution.py:19
  44.2 17.8 %all-to-all-start.1 = ((f16[4,64,384]{2,1,0:T(8,128)(2,1)}), f16[4,64,384]{2,1,0:T(8,128)(2,1)}, u32[]{:S(2)}, u32[]{:S(2)}) async-start(f16[4,64,384]{2,1,0:T(8,128)(2,1)} %bitcast.7), calls=%async_computation.1 | async-start | bytes 393216 | tf_op jit(solution)/shard_map/all_to_all | solution.py:280
  50.2 25.4 %collective-permute-start.1 = (bf16[2,272,384]{2,1,0:T(8,128)(2,1)S(1)}, bf16[2,272,384]{2,1,0:T(8,128)(2,1)S(1)}, u32[]{:S(2)}, u32[]{:S(2)}) collective-permute-start(bf16[2,272,384]{2,1,0:T(8,128)(2,1)S(1)} %pad_maximum_fusion.refs_0_), channel_id=1, source_target_pairs={{0,1},{1,0},{2,3},{3,2},{4,5},{5,4},{6,7},{7,6},{8,9},{9,8},{10,11... | collective-permute-start | bytes 1253384 | tf_op jit(solution)/shard_map/ppermute | solution.py:27
  53.4 22.9 %collective-permute-start.3 = (bf16[2,272,384]{2,1,0:T(8,128)(2,1)S(1)}, bf16[2,272,384]{2,1,0:T(8,128)(2,1)S(1)}, u32[]{:S(2)}, u32[]{:S(2)}) collective-permute-start(bf16[2,272,384]{2,1,0:T(8,128)(2,1)S(1)} %collective-permute-done.2.refs_2_), channel_id=1, source_target_pairs={{0,1},{1,0},{2,3},{3,2},{4,5},{5,4},{6,7},{7,6},{8,9},{9,8},{10,11... | collective-permute-start | bytes 1253384 | tf_op jit(solution)/shard_map/ppermute | solution.py:27
  55.3 0.8 copy-start.6
  56.1 21.0 %collective-permute-start.5 = (bf16[2,272,384]{2,1,0:T(8,128)(2,1)S(1)}, bf16[2,272,384]{2,1,0:T(8,128)(2,1)S(1)}, u32[]{:S(2)}, u32[]{:S(2)}) collective-permute-start(bf16[2,272,384]{2,1,0:T(8,128)(2,1)S(1)} %collective-permute-done.4.refs_4_), channel_id=1, source_target_pairs={{0,1},{1,0},{2,3},{3,2},{4,5},{5,4},{6,7},{7,6},{8,9},{9,8},{10,11... | collective-permute-start | bytes 1253384 | tf_op jit(solution)/shard_map/ppermute | solution.py:27
  58.5 0.8 copy-start.8
  59.2 18.6 %collective-permute-start.7 = (bf16[2,272,384]{2,1,0:T(8,128)(2,1)S(1)}, bf16[2,272,384]{2,1,0:T(8,128)(2,1)S(1)}, u32[]{:S(2)}, u32[]{:S(2)}) collective-permute-start(bf16[2,272,384]{2,1,0:T(8,128)(2,1)S(1)} %collective-permute-done.6.refs_6_), channel_id=1, source_target_pairs={{0,1},{1,0},{2,3},{3,2},{4,5},{5,4},{6,7},{7,6},{8,9},{9,8},{10,11... | collective-permute-start | bytes 1253384 | tf_op jit(solution)/shard_map/ppermute | solution.py:27
  61.1 0.8 copy-start.10
  63.4 34.2 %copy-start.20 = (f32[128]{0:T(128)S(1)}, f32[128]{0:T(128)}, u32[]{:S(2)}) copy-start(f32[128]{0:T(128)} %param.16) | copy-start | bytes 1540
  63.4 34.2 %copy-start.21 = (f32[128]{0:T(128)S(1)}, f32[128]{0:T(128)}, u32[]{:S(2)}) copy-start(f32[128]{0:T(128)} %param.17) | copy-start | bytes 1540
  63.4 27.2 %all-to-all-start.2 = ((f16[16,4,384]{2,1,0:T(4,128)(2,1)}), f16[16,4,384]{2,1,0:T(4,128)(2,1)S(1)}, u32[]{:S(2)}, u32[]{:S(2)}) async-start(f16[16,4,384]{2,1,0:T(4,128)(2,1)} %reshape.21), calls=%async_computation.2 | async-start | bytes 98304 | tf_op jit(solution)/shard_map/all_to_all | solution.py:282
  75.5 68.2 %all-gather.7.cloned.1.call-start = ((), (), s32[]{:S(2)}) async-start(), calls=%async_computation.7 | async-start | bytes 1966080 | tf_op jit(solution)/shard_map/all_gather | solution.py:296
  75.6 0.8 copy-start.12
  76.3 0.8 copy-start.14
  77.1 0.8 copy-start.16
  77.9 0.8 copy-start.18
  78.6 1.0 copy-start.2
  79.6 1.0 copy-start.7
  80.7 1.0 copy-start.9
  81.7 1.0 copy-start.11
  82.7 1.0 copy-start.13
  83.7 1.0 copy-start.15
  84.7 1.0 copy-start.17
  85.7 1.0 copy-start.19
  97.6 1.8 copy-start
  103.3 40.3 %copy-start.22 = (s32[65]{0:T(128)S(1)}, s32[65]{0:T(128)}, u32[]{:S(2)}) copy-start(s32[65]{0:T(128)} %param.10) | copy-start | bytes 784
  141.0 4.3 %collective-permute-start.8 = (bf16[4,512,128]{2,1,0:T(8,128)(2,1)S(1)}, bf16[4,512,128]{2,1,0:T(8,128)(2,1)S(1)}, u32[]{:S(2)}, u32[]{:S(2)}) collective-permute-start(bf16[4,512,128]{2,1,0:T(8,128)(2,1)S(1)} %all_to_all.32.mine_ref), channel_id=1, source_target_pairs={{0,1},{1,0},{2,3},{3,2},{4,5},{5,4},{6,7},{7,6},{8,9},{9,8},{10,11... | collective-permute-start | bytes 1572872 | tf_op jit(solution)/shard_map/ppermute | solution.py:27
  143.8 1.4 copy-start.3
Sparse Core Ops, SparseCore 0:
  22.3 75.1 all-gather.4
  103.5 30.8 all-gather.6
